TPU v7x, 128 devices: a whole 4x4x4 slice. The times are simulated.
128 devices in a mesh: dp: 64 (over y, z, x), width: 2 (over core).
Axes of the slice: x: 4, y: 4, z: 4, core: 2. Of those that a mesh axis runs over, the one named last changes fastest.
Arguments:
- queries: bfloat16 [4096, 4096], P('dp', 'width'), may hold values from -4 to 4
- passages: bfloat16 [4096, 4096], P('dp', 'width'), may hold values from -4 to 4
- passage_ids: int32 [4096], P('dp'), may hold values from 0 to 4095
- pos_index: int32 [4096], P('dp'), may hold values from 0 to 4095
Outputs:
- loss: float32 [4096], P('dp')
- grad_q: float32 [4096, 4096], P('dp', 'width')
- grad_p: float32 [4096, 4096], P('dp', 'width')
All inputs are finite; a program needn't handle non-finite values.
Results may differ from a plain program's by a relative error of at most 0.001.
Values may be sent and summed in bfloat16 or wider, within the bound.
No kernel may reach another device: no remote copies, remote signals or barrier semaphores. Data moves between devices by JAX's collectives and lax.ppermute only.
A program may use at most 128 MiB of HBM per device.

v0:
```python
import math

import jax
import jax.numpy as jnp
from jax import lax
from jax.sharding import PartitionSpec as P

D = 4096


def inner(left, right):
    return lax.dot_general(
        left, right, (((1,), (1,)), ((), ())), preferred_element_type=jnp.float32
    )


def plain(left, right):
    return jnp.dot(left, right, preferred_element_type=jnp.float32)


def lower(left, right):
    return lax.dot_general(
        left, right, (((0,), (0,)), ((), ())), preferred_element_type=jnp.float32
    )


def body(queries, passages, passage_ids, pos_index):
    rows_dev = queries.shape[0]
    scale = 3.0 / math.sqrt(D)
    minus = jnp.float32(-jnp.inf)
    first_row = lax.axis_index("dp") * rows_dev
    rows = first_row + jnp.arange(rows_dev, dtype=jnp.int32)
    q_all, p_all, id_all = (
        lax.all_gather(queries, "dp", axis=0, tiled=True),
        lax.all_gather(passages, "dp", axis=0, tiled=True),
        lax.all_gather(passage_ids, "dp", axis=0, tiled=True),
    )
    total = q_all.shape[0]
    cols = jnp.arange(total, dtype=jnp.int32)
    part_qp = inner(queries, p_all)
    part_qq = inner(queries, q_all)
    part_pp = inner(passages, p_all)
    part_col = inner(q_all, passages)
    s_qp, s_qq, s_pp, c_qp = lax.psum((part_qp, part_qq, part_pp, part_col), "width")
    s_qp = s_qp * scale
    s_qq = s_qq * scale
    s_pp = s_pp * scale
    is_pos = cols[None, :] == pos_index[:, None]
    target = jnp.sum(jnp.where(is_pos, id_all[None, :], 0), axis=1).astype(jnp.int32)
    keep_qp = is_pos | (id_all[None, :] != target[:, None])
    keep_qq = cols[None, :] != rows[:, None]
    keep_pp = keep_qq & (id_all[None, :] != passage_ids[:, None])
    top = jnp.maximum(
        jnp.max(jnp.where(keep_qp, s_qp, minus), axis=1),
        jnp.maximum(
            jnp.max(jnp.where(keep_qq, s_qq, minus), axis=1),
            jnp.max(jnp.where(keep_pp, s_pp, minus), axis=1),
        ),
    )
    summed = (
        jnp.sum(jnp.where(keep_qp, jnp.exp(s_qp - top[:, None]), 0.0), axis=1)
        + jnp.sum(jnp.where(keep_qq, jnp.exp(s_qq - top[:, None]), 0.0), axis=1)
        + jnp.sum(jnp.where(keep_pp, jnp.exp(s_pp - top[:, None]), 0.0), axis=1)
    )
    lse = top + jnp.log(summed)
    loss = lse - jnp.sum(jnp.where(is_pos, s_qp, 0.0), axis=1)
    g_qp = (
        jnp.where(keep_qp, jnp.exp(s_qp - lse[:, None]), 0.0) - is_pos.astype(jnp.float32)
    ).astype(jnp.bfloat16)
    w_qq = jnp.where(keep_qq, jnp.exp(s_qq - lse[:, None]), 0.0).astype(jnp.bfloat16)
    w_pp = jnp.where(keep_pp, jnp.exp(s_pp - lse[:, None]), 0.0).astype(jnp.bfloat16)
    lse_all, target_all, pos_all = (
        lax.all_gather(lse, "dp", axis=0, tiled=True),
        lax.all_gather(target, "dp", axis=0, tiled=True),
        lax.all_gather(pos_index, "dp", axis=0, tiled=True),
    )
    c_qp = c_qp * scale
    c_qq = s_qq.T
    c_pp = s_pp.T
    pos_col = pos_all[:, None] == rows[None, :]
    keep_cqp = pos_col | (passage_ids[None, :] != target_all[:, None])
    keep_cqq = cols[:, None] != rows[None, :]
    keep_cpp = keep_cqq & (passage_ids[None, :] != id_all[:, None])
    col_gqp = (
        jnp.where(keep_cqp, jnp.exp(c_qp - lse_all[:, None]), 0.0) - pos_col.astype(jnp.float32)
    ).astype(jnp.bfloat16)
    col_wqq = jnp.where(keep_cqq, jnp.exp(c_qq - lse_all[:, None]), 0.0).astype(jnp.bfloat16)
    col_wpp = jnp.where(keep_cpp, jnp.exp(c_pp - lse_all[:, None]), 0.0).astype(jnp.bfloat16)
    grad_q = plain(g_qp, p_all) + plain(w_qq, q_all) + lower(col_wqq, q_all)
    grad_p = lower(col_gqp, q_all) + plain(w_pp, p_all) + lower(col_wpp, p_all)
    return (loss, grad_q, grad_p)


def solution(mesh):
    placed = (P("dp", "width"), P("dp", "width"), P("dp"), P("dp"))
    return jax.shard_map(
        body,
        mesh=mesh,
        in_specs=placed,
        out_specs=(P("dp"), P("dp", "width"), P("dp", "width")),
        check_vma=False,
    )
```

profile of v0, /device:TPU:0, one launch (start us, length us, event | category | flops | bytes accessed | tf_op | source)
XLA Modules:
  0.0 1334.3 jit_solution(16284247093207768823)
XLA Ops:
  7.2 0.7 all-gather.3.cloned.1.call-update
  8.0 0.7 all-gather.5.cloned.1.call-update
  8.7 109.1 %all-gather.3.cloned.1.call-done = bf16[4096,2048]{1,0:T(8,128)(2,1)} async-done(((bf16[64,2048]{1,0:T(8,128)(2,1)}), bf16[4096,2048]{1,0:T(8,128)(2,1)}) %all-gather.3.cloned.1.call-update) | async-done | bytes 16777232 | tf_op jit(solution)/shard_map/all_gather | solution.py:35
  117.8 12.0 fusion.58
  129.8 12.1 fusion.60
  141.9 82.8 %all-gather.5.cloned.1.call-done = bf16[4096,2048]{1,0:T(8,128)(2,1)} async-done(((bf16[64,2048]{1,0:T(8,128)(2,1)}), bf16[4096,2048]{1,0:T(8,128)(2,1)}) %all-gather.5.cloned.1.call-update) | async-done | bytes 16777232 | tf_op jit(solution)/shard_map/all_gather | solution.py:34
  224.7 11.9 fusion.59
  236.6 12.1 fusion.61
  248.8 0.6 dynamic-slice
  250.0 0.3 dynamic-update-slice
  250.6 346.4 %all-reduce = s32[4096]{0:T(1024)S(1)} all-reduce(s32[4096]{0:T(1024)S(1)} %dynamic-update-slice), channel_id=1, replica_groups=mesh['dp'=64,'width'=2] {'dp'}, use_global_device_ids=true, to_apply=%add | all-reduce | flops 4096 | bytes 32768
  597.0 0.3 select_reduce_fusion.7
  597.3 0.3 dynamic-update-slice.3
  597.6 341.5 %all-reduce.4 = (s32[4096]{0:T(1024)S(1)}, s32[4096]{0:T(1024)S(1)}) all-reduce(s32[4096]{0:T(1024)S(1)} %dynamic-update-slice.3, s32[4096]{0:T(1024)S(1)} %dynamic-update-slice.2), channel_id=1, replica_groups=mesh['dp'=64,'width'=2] {'dp'}, use_global_device_ids=true, to_apply=%add.3 | all-reduce | flops 8192 | bytes 65536
  939.1 2.7 select_reduce_fusion.4
  941.8 3.1 select_reduce_fusion
  945.0 341.5 %all-reduce.1 = f32[4096]{0:T(1024)S(1)} all-reduce(f32[4096]{0:T(1024)S(1)} %get-tuple-element.16), channel_id=1, replica_groups=mesh['dp'=64,'width'=2] {'dp'}, use_global_device_ids=true, to_apply=%add.1 | all-reduce | flops 4096 | bytes 32768
  1286.5 0.5 sub.38
  1287.0 9.4 fusion.7
  1296.4 9.0 fusion.10
  1305.5 4.0 convolution_add_fusion.1
  1309.5 5.2 convolution_add_fusion
  1314.7 9.1 convolution_add_fusion.3
  1323.8 3.9 convolution_add_fusion.2
  (47 shorter events, 0.6 us)
Async XLA Ops:
  7.2 122.6 %copy-start.3 = (bf16[64,2048]{1,0:T(8,128)(2,1)S(1)}, bf16[64,2048]{1,0:T(8,128)(2,1)}, u32[]{:S(2)}) copy-start(bf16[64,2048]{1,0:T(8,128)(2,1)} %param.5) | copy-start | bytes 786436
  7.2 110.6 %all-gather.3.cloned.1.call-start = ((), (), s32[]{:S(2)}) async-start(), calls=%async_computation | async-start | bytes 17039360 | tf_op jit(solution)/shard_map/all_gather | solution.py:35
  7.9 216.8 %all-gather.5.cloned.1.call-start = ((), (), s32[]{:S(2)}) async-start(), calls=%async_computation.1 | async-start | bytes 17039360 | tf_op jit(solution)/shard_map/all_gather | solution.py:34
  8.7 216.0 %copy-start.2 = (bf16[64,2048]{1,0:T(8,128)(2,1)S(1)}, bf16[64,2048]{1,0:T(8,128)(2,1)}, u32[]{:S(2)}) copy-start(bf16[64,2048]{1,0:T(8,128)(2,1)} %param.4) | copy-start | bytes 786436
  8.7 930.4 %all-reduce.8.cloned.1.call-start = ((), (), s32[]{:S(2)}) async-start(), calls=%async_computation.2 | async-start | bytes 8388608 | tf_op jit(solution)/shard_map/psum | solution.py:44
  141.9 106.9 %copy-start.7 = (u32[128]{0:T(128)S(1)}, u32[128]{0:T(128)}, u32[]{:S(2)}) copy-start(u32[128]{0:T(128)} %constant.19) | copy-start | bytes 1540
  141.9 108.1 %copy-start.5 = (s32[64]{0:T(128)S(1)}, s32[64]{0:T(128)}, u32[]{:S(2)}) copy-start(s32[64]{0:T(128)} %param.6) | copy-start | bytes 772
  141.9 108.4 %copy-start.6 = (s32[64]{0:T(128)S(1)}, s32[64]{0:T(128)}, u32[]{:S(2)}) copy-start(s32[64]{0:T(128)} %param.7) | copy-start | bytes 772
  939.1 357.3 %copy-start.4 = (f32[4096,64]{0,1:T(8,128)S(1)}, f32[4096,64]{0,1:T(8,128)}, u32[]{:S(2)}) copy-start(f32[4096,64]{0,1:T(8,128)} %get-tuple-element.15) | copy-start | bytes 3145732
  1287.0 18.5 %slice-start = ((s8[16777216]{0:T(1024)(128)(4,1)}), s8[4194304]{0:T(1024)(128)(4,1)S(1)}, s32[]{:S(2)}) async-start(s8[16777216]{0:T(1024)(128)(4,1)} %bitcast.25), calls=%async_computation.3 | async-start | bytes 8388608
  1287.0 18.5 %slice-start.1 = ((s8[16777216]{0:T(1024)(128)(4,1)}), s8[4194304]{0:T(1024)(128)(4,1)S(1)}, s32[]{:S(2)}) async-start(s8[16777216]{0:T(1024)(128)(4,1)} %bitcast.25), calls=%async_computation.4 | async-start | bytes 8388608
  1296.4 9.1 copy-start
  1296.4 9.1 slice-start.2
  1296.4 9.1 slice-start.3
  1309.5 5.2 copy-start.1
  1309.5 14.2 %slice-start.4 = ((s8[16777216]{0:T(1024)(128)(4,1)}), s8[4194304]{0:T(1024)(128)(4,1)S(1)}, s32[]{:S(2)}) async-start(s8[16777216]{0:T(1024)(128)(4,1)} %bitcast.27), calls=%async_computation.7 | async-start | bytes 8388608
  1309.5 14.3 %slice-start.5 = ((s8[16777216]{0:T(1024)(128)(4,1)}), s8[4194304]{0:T(1024)(128)(4,1)S(1)}, s32[]{:S(2)}) async-start(s8[16777216]{0:T(1024)(128)(4,1)} %bitcast.27), calls=%async_computation.8 | async-start | bytes 8388608
  1309.5 14.3 %slice-start.6 = ((s8[16777216]{0:T(1024)(128)(4,1)}), s8[4194304]{0:T(1024)(128)(4,1)S(1)}, s32[]{:S(2)}) async-start(s8[16777216]{0:T(1024)(128)(4,1)} %bitcast.27), calls=%async_computation.9 | async-start | bytes 8388608
  1314.7 9.1 slice-start.7
Sparse Core Ops, SparseCore 0:
  10.9 106.8 all-gather.2
  120.7 103.9 all-gather.4
  248.9 33.8 all-reduce.7
where the time goes:
time: 1330 us
  blocking collectives  1030 us (77%)
  waiting for transfers between devices  193 us (15%)
  matrix products  88.7 us (7%)
  between operations  14.6 us (1%)
    unnamed x3, blocking collectives  1030 us
    all_gather x1, waiting for transfers between devices, body(): lax.all_gather(passages, 'dp', axis=0, tiled=True)  109 us
    all_gather x1, waiting for transfers between devices, body(): lax.all_gather(queries, 'dp', axis=0, tiled=True)  82.8 us
    dot_general x4, matrix products, inner(): lax.dot_general(left, right, (((1,), (1,)), ((), ())), preferred_element_...  48.2 us
  transfers between devices with their start and end apart: 3, of which 2 were waited for; matrix products, arithmetic and copies ran while one was open for 2% of the time, Pallas kernels for 0%

commit v1 on v0

v1 whole, which is shorter than its diff:
```python
import functools
import math

import jax
import jax.numpy as jnp
from jax import lax
from jax.experimental import pallas as pl
from jax.experimental.pallas import tpu as pltpu
from jax.sharding import Mesh, PartitionSpec as P

D = 4096
N = 64
H = N // 2
SCALE = 3.0 / math.sqrt(D)
BIG = 1e30
GRID = ("y", "z", "x", "w")
UP = [(i, (i + 1) % 4) for i in range(4)]
DOWN = [(i, (i - 1) % 4) for i in range(4)]
FAR = [(i, (i + 2) % 4) for i in range(4)]
RING = (0, 1, 3, 2)
PARTS = (256, 256, 256, 256)
J = sum(PARTS)


def steps(first, second, by):
    moves = []
    for y in range(4):
        for z in range(4):
            for x in range(4):
                for w in range(2):
                    axis = second if w else first
                    to_y, to_z = ((y + by) % 4, z) if axis == "y" else (y, (z + by) % 4)
                    flat = lambda y, z: ((y * 4 + z) * 4 + x) * 2 + w
                    moves.append((flat(y, z), flat(to_y, to_z)))
    return moves


FIRST = {by: steps("y", "z", by) for by in (1, 2, 3)}
SECOND = {by: steps("z", "y", by) for by in (1, 2, 3)}


def along(value, moves):
    return lax.ppermute(value, GRID, moves)


def swap(value):
    return lax.ppermute(value, "w", [(0, 1), (1, 0)])


def up(value):
    return lax.ppermute(value, "x", UP)


def down(value):
    return lax.ppermute(value, "x", DOWN)


def far(value):
    return lax.ppermute(value, "x", FAR)


def inner(left, right):
    return lax.dot_general(
        left, right, (((1,), (1,)), ((), ())), preferred_element_type=jnp.float32
    )


def plain(left, right):
    return jnp.dot(left, right, preferred_element_type=jnp.float32)


VMEM = pl.BlockSpec(memory_space=pltpu.VMEM)
SMEM = pl.BlockSpec(memory_space=pltpu.SMEM)


def params(mib):
    return pltpu.CompilerParams(vmem_limit_bytes=mib << 20)


def cost(flops, moved, transcendentals=0):
    return pl.CostEstimate(flops=flops, bytes_accessed=moved, transcendentals=transcendentals)


def pack_kernel(plan, *refs):
    pieces, out = refs[:-1], refs[-1]
    at = 0
    for k, start, count in plan:
        out[:, at:at + count, :] = pieces[k][:, start:start + count, :]
        at += count


def pack(plan, *pieces):
    rows, wide = sum(count for _, _, count in plan), pieces[0].shape[2]
    return pl.pallas_call(
        functools.partial(pack_kernel, plan),
        out_shape=jax.ShapeDtypeStruct((2, rows, wide), jnp.bfloat16),
        in_specs=[VMEM] * len(pieces),
        out_specs=VMEM,
        compiler_params=params(8),
        cost_estimate=cost(0, 8 * rows * wide),
    )(*pieces)


def rows_kernel(*refs):
    mine, theirs, outs = refs[:5], refs[5:10], refs[10:]
    for k, pieces in enumerate((mine, theirs)):
        at = 4 * k * N
        for piece in pieces:
            count = piece.shape[1]
            for h in (0, 1):
                outs[h][at:at + count, :] = piece[h ^ k]
            at += count


def rows_from(mine, theirs):
    wide = mine[0].shape[2]
    return pl.pallas_call(
        rows_kernel,
        out_shape=[jax.ShapeDtypeStruct((8 * N, wide), jnp.bfloat16)] * 2,
        in_specs=[VMEM] * 10,
        out_specs=[VMEM] * 2,
        compiler_params=params(12),
        cost_estimate=cost(0, 8 << 20),
    )(*mine, *theirs)


def masks(rows, cols, at, count):
    same_u, cross_u, cross_e = (rows[pl.ds(at, count), k:k + 1] for k in range(3))
    same_v, cross_v, cross_p = (cols[k:k + 1, :] for k in range(3))
    hit = cross_e == cross_p
    return same_u != same_v, (cross_u != cross_v) | hit, hit


def scores_at(parts, at, count):
    return jnp.concatenate([part[pl.ds(at, count), :] for part in parts], axis=1) * SCALE


STATS = 16


def stats_kernel(core, amax, *refs):
    parts, (rows, cols, out, keep) = refs[:-4], refs[-4:]
    step = 32
    inc = core[0] == 1
    keep[...] = jnp.zeros_like(keep)

    @pl.loop(0, 4 * N // step)
    def _(k):
        at = pl.multiple_of(k * step, step)
        keep_s, keep_c, hit = masks(rows, cols, at, step)
        keep_c = keep_c & inc
        same = scores_at(parts, at, step)
        cross = scores_at(parts, pl.multiple_of(at + 4 * N, step), step)
        same = jnp.where(keep_s, same, -BIG)
        hits = jnp.sum(jnp.where(hit & inc, cross, 0.0), axis=1, keepdims=True)
        cross = jnp.where(keep_c, cross, -BIG)
        top = jnp.max(jnp.maximum(same, cross), axis=1, keepdims=True)
        total = jnp.sum(
            jnp.where(keep_s, jnp.exp(same - top), 0.0) + jnp.where(keep_c, jnp.exp(cross - top), 0.0),
            axis=1,
            keepdims=True,
        )
        group, low = k // (N // step), pl.multiple_of((k % (N // step)) * step, step)
        for n, value in enumerate((top, total, hits)):
            keep[n * 4 + group, pl.ds(low, step), :] = jnp.broadcast_to(value, (step, 128))

    for n in range(12):
        out[n:n + 1, :] = keep[n].T[0:1, :]
    out[12:16, :] = jnp.full((4, 128), amax[0], jnp.float32)


def stats_of(core, amax, parts, rows, cols):
    return pl.pallas_call(
        stats_kernel,
        out_shape=jax.ShapeDtypeStruct((STATS, 128), jnp.float32),
        in_specs=[SMEM] * 2 + [VMEM] * (len(parts) + 2),
        out_specs=VMEM,
        scratch_shapes=[pltpu.VMEM((12, 128, 128), jnp.float32)],
        compiler_params=params(8),
        cost_estimate=cost(10 << 20, 2 << 20, 1 << 19),
    )(core, amax, *parts, rows, cols)


TURNED = ((0, 1, 2, 3), (2, 0, 3, 1), (1, 3, 0, 2), (3, 2, 1, 0))


def merge_kernel(core, *refs):
    (mine, theirs), (out, ends) = (refs[:4], refs[4:8]), refs[8:]
    first = core[0] == 0
    a = [ref[...] for ref in mine]
    b = [ref[...] for ref in theirs]
    line = [jnp.where(first, u, v) for u, v in zip(a, b)] + [jnp.where(first, v, u) for u, v in zip(a, b)]
    loose = jnp.zeros((1, 128), jnp.float32)
    valid = lax.broadcasted_iota(jnp.int32, (1, 128), 1) < N
    for g in range(4):
        of = lambda k: [v[4 * k + t[g]:4 * k + t[g] + 1] for v, t in zip(line, TURNED * 2)]
        tops, sums, hits = of(0), of(1), of(2)
        top = functools.reduce(jnp.maximum, tops)
        total = sum(u * jnp.exp(t - top) for u, t in zip(sums, tops))
        lse = top + jnp.log(total)
        gap = lse - sum(hits)
        out[g:g + 1, :] = lse
        out[4 + g:5 + g, :] = gap
        loose = jnp.maximum(loose, jnp.where(valid, 1.0 - jnp.exp(-gap), 0.0))
        if g == 0:
            ends[0:1, :] = lse
    ends[1:2, :] = loose
    most = functools.reduce(jnp.maximum, [v[12:13] for v in line])
    ends[2:8, :] = jnp.broadcast_to(most, (6, 128))


def merged(core, mine, theirs):
    return pl.pallas_call(
        merge_kernel,
        out_shape=[jax.ShapeDtypeStruct((8, 128), jnp.float32)] * 2,
        in_specs=[SMEM] + [VMEM] * 8,
        out_specs=[VMEM] * 2,
        compiler_params=params(4),
        cost_estimate=cost(1 << 16, 1 << 16, 1 << 14),
    )(core, *mine, *theirs)


def lanes_of(rows):
    lane = lax.broadcasted_iota(jnp.int32, (8, 128), 1)
    wide = lambda v: jnp.broadcast_to(v, (8, 128))
    turn = lambda v, by: pltpu.roll(wide(v), by, axis=1) if by % 128 else wide(v)
    out = []
    for b in range(3):
        for a in (0, 2):
            out.append(jnp.where(lane < 64, wide(rows[4 * b + a]), turn(rows[4 * b + a + 1], 64)))
    for h in (0, 1):
        q = [turn(rows[12 + a], (32 * a - 32 * h) % 128) for a in range(4)]
        out.append(jnp.where(lane < 64, jnp.where(lane < 32, q[0], q[1]), jnp.where(lane < 96, q[2], q[3])))
    return jnp.concatenate(out, axis=1)[0:1]


def weights_kernel(first, count, core, *refs):
    parts, (rows, cols, lse_i, *plane, out, bound, col) = refs[:len(PARTS)], refs[len(PARTS):]
    step = 32
    w = core[0]
    for g in range(4):
        line = jnp.broadcast_to(lse_i[g:g + 1, :], (128, 128)).T[:N]
        col[0, g * N:(g + 1) * N, :] = line
        col[1, g * N:(g + 1) * N, :] = jnp.where(w == 1, line, 0.0)
    ends = [ref[8 * a:8 * a + 8, :] for ref in plane for a in range(4)]
    lj = lanes_of([v[0:1] for v in ends])
    cross_j = jnp.where(w == 1, 0.0, lj)
    loose = jnp.max(functools.reduce(jnp.maximum, [v[1:2] for v in ends]), axis=1, keepdims=True)
    most = jnp.max(functools.reduce(jnp.maximum, [v[2:3] for v in ends]), axis=1, keepdims=True)
    bound[...] = jnp.broadcast_to(jnp.maximum(loose, 1e-3) * jnp.maximum(most, 1e-20), (8, 128))

    @pl.loop(0, count * N // step)
    def _(k):
        at = pl.multiple_of(first * N + k * step, step)
        keep_s, keep_c, hit = masks(rows, cols, at, step)
        li = col[0, pl.ds(at, step), 0:1]
        lc = col[1, pl.ds(at, step), 0:1]
        same = scores_at(parts, at, step)
        cross = scores_at(parts, pl.multiple_of(at + 4 * N, step), step)
        m_s = jnp.where(keep_s, jnp.exp(same - li) + jnp.exp(same - lj), 0.0)
        m_c = jnp.where(keep_c, jnp.exp((cross - lc) - cross_j), 0.0) - jnp.where(hit, 1.0, 0.0)
        group = k // (N // step)
        base = group * 2 * N + (k % (N // step)) * step
        out[pl.ds(pl.multiple_of(base + w * N, step), step), :] = m_s.astype(jnp.bfloat16)
        out[pl.ds(pl.multiple_of(base + (1 - w) * N, step), step), :] = m_c.astype(jnp.bfloat16)


def weights_of(first, count, core, parts, rows, cols, lse_i, plane):
    return pl.pallas_call(
        functools.partial(weights_kernel, first, count),
        out_shape=[
            jax.ShapeDtypeStruct((count * 2 * N, J), jnp.bfloat16),
            jax.ShapeDtypeStruct((8, 128), jnp.float32),
        ],
        in_specs=[SMEM] + [VMEM] * (len(parts) + 7),
        out_specs=[VMEM] * 2,
        scratch_shapes=[pltpu.VMEM((2, 4 * N, 128), jnp.float32)],
        compiler_params=params(8),
        cost_estimate=cost(count * (3 << 20), count << 19, count * 3 * N * J),
    )(core, *parts, rows, cols, lse_i, *plane)


def product_kernel(bound, rest, rest_o, far, far_o, *refs):
    blocks, (here, down_o, up_o, far_out) = refs[:-4], refs[-4:]
    shrink = 1.0 / bound[0:1, 0:1]

    def total(mine, theirs):
        out = None
        for k, weights in enumerate((mine, theirs)):
            for n, size in enumerate(PARTS):
                at = sum(PARTS[:n])
                term = plain(weights[:, at:at + size], blocks[k * len(PARTS) + n][0])
                out = term if out is None else out + term
        return out

    far_out[...] = total(far, far_o) * shrink
    near = total(rest, rest_o)
    here[...] = near[:2 * N]
    down_o[...] = near[2 * N:4 * N] * shrink
    up_o[...] = near[4 * N:] * shrink


def product_of(bound, rest, rest_o, far, far_o, blocks, others):
    wide, step = blocks[0].shape[2], 256
    whole = lambda a: pl.BlockSpec(a.shape, lambda i: (0, 0))
    own = [pl.BlockSpec((1, a.shape[1], step), lambda i: (0, 0, i)) for a in blocks]
    other = [pl.BlockSpec((1, a.shape[1], step), lambda i: (1, 0, i)) for a in others]
    heads = (bound, rest, rest_o, far, far_o)
    return pl.pallas_call(
        product_kernel,
        grid=(wide // step,),
        out_shape=[jax.ShapeDtypeStruct((2 * N, wide), jnp.float32)] * 4,
        in_specs=[whole(a) for a in heads] + own + other,
        out_specs=[pl.BlockSpec((2 * N, step), lambda i: (0, i))] * 4,
        compiler_params=params(16),
        cost_estimate=cost(32 * N * J * wide, 4 * J * wide + 32 * N * wide),
    )(*heads, *blocks, *others)


def after(value, *others):
    return lax.optimization_barrier((value, *others))[0]


def settle(*values):
    return lax.optimization_barrier(values)


def body(queries, passages, passage_ids, pos_index):
    y, z, x, w = (lax.axis_index(name) for name in GRID)
    first = w == 0
    core = w.astype(jnp.int32).reshape(1)
    pick = lambda a, b: jnp.where(first, a, b)
    rows_of = functools.partial(lax.slice_in_dim, axis=1)
    low = lambda a: [rows_of(a, k * N, k * N + H) for k in range(a.shape[1] // N)]
    high = lambda a: [rows_of(a, k * N + H, (k + 1) * N) for k in range(a.shape[1] // N)]
    join = lambda parts: jnp.concatenate(parts, axis=1)
    line = lambda v, k: (up, far, down)[k - 1](v)
    by_first = lambda v, k: along(v, FIRST[k])
    by_second = lambda v, k: along(v, SECOND[k])
    ring = lambda v, send: [v] + [send(v, k) for k in RING[1:]]

    got = swap(pick(passages, queries))
    own = jnp.stack([pick(queries, passages), got])
    ints = jnp.stack([passage_ids, pos_index])

    fl, fr, own, *ints = settle(along(own, FIRST[1]), along(own, FIRST[3]), own, *ring(ints, line))
    f_low, f_high, own, fl, fr, *ints = settle(
        along(low(fl)[0], FIRST[1]), along(high(fr)[0], FIRST[3]), own, fl, fr, *ring(jnp.stack(ints), by_first)
    )
    group = pack(((0, 0, N), (1, 0, N), (2, 0, N), (3, 0, H), (4, 0, H)), own, fl, fr, f_low, f_high)
    group, own, *ints = settle(group, own, *ring(jnp.stack(ints), by_second))
    ints = jnp.stack(ints)
    ids = ints[..., 0, :]
    dev, off = ints[..., 1, :] // N, ints[..., 1, :] % N
    near = lambda at, other: (lambda d: d ^ (d >> 1))((at - other) % 4)
    dy, dz, dx = near(y, dev // 16), near(z, dev // 4 % 4), near(x, dev % 4)
    pos = ((pick(dz, dy) * 4 + pick(dy, dz)) * 4 + dx) * N + off
    pair = jnp.arange(64 * N, dtype=jnp.int32).reshape(4, 4, 4, N)
    i_of = lambda t: t[0, 0].reshape(-1)
    j_of = lambda t: jnp.concatenate(
        [t[:3, :, 0].reshape(-1), t[3, :, 0].reshape(4, 2, H).transpose(1, 0, 2).reshape(-1)]
    )
    i_pair, i_id, i_pos = i_of(pair), i_of(ids), i_of(pos)
    j_pair, j_id, j_pos = j_of(pair), j_of(ids), j_of(pos)
    table, every = ids.reshape(1, -1), pair.reshape(1, -1)
    look = lambda at: jnp.sum(jnp.where(at[:, None] == every, table, 0), axis=1)
    i_tgt, j_tgt = look(i_pos), look(j_pos)
    rows = jnp.stack([pick(i_pair, i_id), pick(i_id, i_tgt), pick(i_pair, i_pos)] + [i_pair] * 5, axis=1)
    cols = jnp.stack([pick(j_pair, j_id), pick(j_tgt, j_id), pick(j_pos, j_pair)] + [j_pair] * 5)
    xl, xr = up(own), down(own)
    mine = [own, xl, xr, up(low(xl)[0]), down(high(xr)[0])]
    dl, dr, group, rows, cols, *held = settle(
        along(group, SECOND[1]), along(group, SECOND[3]), group, rows, cols, *mine, *[swap(a) for a in mine]
    )
    to_l = pack(tuple((0, k * N, H) for k in range(4)), dl)
    to_r = pack(tuple((0, k * N + H, H) for k in range(4)), dr)
    i0, i1 = rows_from(held[:5], held[5:])
    score = lambda a: inner(i0, a[0]) + inner(i1, a[1])
    blocks = [group, dl, dr]
    parts = [score(a) for a in blocks]
    others = [swap(after(a, part)) for a, part in zip(blocks, parts)]
    gl, gr, i0, i1, *held = settle(along(to_l, SECOND[1]), along(to_r, SECOND[3]), i0, i1, *parts, *blocks)
    parts, blocks = held[:3], held[3:]
    last = pack(((0, 0, 2 * N), (1, 0, 2 * N)), gl, gr)
    blocks.append(last)

    amax = jnp.maximum(
        jnp.max(jnp.abs(queries.astype(jnp.float32))), jnp.max(jnp.abs(passages.astype(jnp.float32)))
    )

    parts.append(score(last))
    found, *held = settle(stats_of(core, amax.reshape(1), parts, rows, cols), *others, swap(last), *blocks)
    others, blocks = held[:4], held[4:]
    found = ring(found, line)
    lse_i, ends = merged(core, found, [swap(a) for a in found])
    loss = lse_i[4, :N]
    plane = ring(jnp.concatenate(ring(ends, by_first)), by_second)

    args = (core, parts, rows, cols, lse_i, plane)
    m_far, bound = weights_of(3, 1, *args)
    m_rest, _ = weights_of(0, 3, *args)
    f16, f32 = jnp.float16, jnp.float32
    here, to_down, to_up, opposite = product_of(bound, m_rest, swap(m_rest), m_far, swap(m_far), blocks, others)
    opposite, near_q, near_p = opposite.astype(f16), to_down[:N].astype(f16), to_up[N:].astype(f16)
    got_q, got_p, down_q, up_p = settle(up(opposite[:N]), down(opposite[N:]), down(near_q), up(near_p))
    up_q = up((to_up[:N] + got_q.astype(f32)).astype(f16))
    down_p = down((to_down[N:] + got_p.astype(f32)).astype(f16))
    grow = bound[0, 0]
    grad_q = here[:N] + (up_q.astype(f32) + down_q.astype(f32)) * grow
    grad_p = here[N:] + (up_p.astype(f32) + down_p.astype(f32)) * grow
    return loss, grad_q, grad_p


def solution(mesh):
    grid = Mesh(mesh.devices.reshape(4, 4, 4, 2), GRID)
    pair = ("y", "z", "x")
    placed = (P(pair, "w"), P(pair, "w"), P(pair), P(pair))
    return jax.shard_map(
        body,
        mesh=grid,
        in_specs=placed,
        out_specs=(P(pair), P(pair, "w"), P(pair, "w")),
        check_vma=False,
    )
```

time: 1330 us -> 165 us (0.12)
  blocking collectives: 1030 us -> 0 us
  waiting for transfers between devices: 193 us -> 51 us
  matrix products: 88.7 us -> 14.9 us
  starting transfers between devices: 0.11 us -> 59.2 us
  Pallas kernels: 0 us -> 21.1 us
    unnamed x3 -> x0, blocking collectives: 1030 us -> none
    all_gather x2 -> x0, waiting for transfers between devices: 192 us -> none  [the longest x1 109 us: body(): lax.all_gather(passages, 'dp', axis=0, tiled=True)]
    ppermute x0 -> x52, starting transfers between devices: none -> 59.2 us  [the longest x20 31 us: along(): return lax.ppermute(value, GRID, moves)]
    ppermute x0 -> x52, waiting for transfers between devices: none -> 51 us  [the longest x20 15.4 us: along(): return lax.ppermute(value, GRID, moves)]
    dot_general x6 -> x0, matrix products: 40.6 us -> none  [the longest x3 22.4 us: plain(): return jnp.dot(left, right, preferred_element_type=jnp.float32)]
    dot_general x4 -> x8, matrix products: 48.2 us -> 14.9 us  [inner(): lax.dot_general(left, right, (((1,), (1,)), ((), ())), preferred_element_...]
    pallas_call x0 -> x10, Pallas kernels: none -> 21.1 us  [the longest x1 9.19 us: product_of(): pl.pallas_call(product_kernel, grid=(wide // step,), out_shape=[jax.Shape...]
  transfers between devices with their start and end apart: 3 -> 52, of which waited for: 2 -> 22; matrix products, arithmetic and copies ran while one was open for 2% -> 15% of each run, Pallas kernels for 0% -> 5%
where the time goes in v1:
time: 165 us
  starting transfers between devices  59.2 us (36%)
  waiting for transfers between devices  51 us (31%)
  Pallas kernels  21.1 us (13%)
  matrix products  14.9 us (9%)
  local copies, waits for them, and re-layouts  8.95 us (5%)
  other arithmetic  7.23 us (4%)
  between operations  2.4 us (1%)
    ppermute x20, starting transfers between devices, along(): return lax.ppermute(value, GRID, moves)  31 us
    ppermute x7, starting transfers between devices, down(): return lax.ppermute(value, 'x', DOWN)  16 us
    ppermute x20, waiting for transfers between devices, along(): return lax.ppermute(value, GRID, moves)  15.4 us
    ppermute x7, waiting for transfers between devices, up(): return lax.ppermute(value, 'x', UP)  15.4 us
    dot_general x8, matrix products, inner(): lax.dot_general(left, right, (((1,), (1,)), ((), ())), preferred_element_...  14.9 us
    pallas_call x1, Pallas kernels, product_of(): pl.pallas_call(product_kernel, grid=(wide // step,), out_shape=[jax.Shape...  9.19 us
    ppermute x7, waiting for transfers between devices, down(): return lax.ppermute(value, 'x', DOWN)  7.57 us
    ppermute x16, waiting for transfers between devices, swap(): return lax.ppermute(value, 'w', [(0, 1), (1, 0)])  6.38 us
  transfers between devices with their start and end apart: 52, of which 22 were waited for; matrix products, arithmetic and copies ran while one was open for 15% of the time, Pallas kernels for 5%

profile of v1, /device:TPU:0, one launch (start us, length us, event | category | flops | bytes accessed | tf_op | source)
XLA Modules:
  0.0 164.8 jit_solution(16154784169974890723)
XLA Ops:
  11.9 3.2 %collective-permute-done.5 = s32[2,64]{1,0:T(2,128)S(1)} collective-permute-done((s32[2,64]{1,0:T(2,128)S(1)}, s32[2,64]{1,0:T(2,128)S(1)}, u32[]{:S(2)}, u32[]{:S(2)}) %collective-permute-start.5) | collective-permute-done | bytes 544 | tf_op jit(solution)/shard_map/ppermute | solution.py:59
  16.0 2.5 %collective-permute-start.7 = (bf16[2,32,2048]{2,1,0:T(8,128)(2,1)S(1)}, bf16[2,32,2048]{2,1,0:T(8,128)(2,1)S(1)}, u32[]{:S(2)}, u32[]{:S(2)}) collective-permute-start(bf16[2,32,2048]{2,1,0:T(8,128)(2,1)S(1)} %slice.117), channel_id=1, source_target_pairs={{0,96},{1,25},{2,98},{3,27},{4,100},{5,29},{6,102},{7,31},{8,104},... | collective-permute-start | bytes 786440 | tf_op jit(solution)/shard_map/ppermute | solution.py:43
  18.6 3.2 %collective-permute-start.9 = (s32[4,2,64]{2,1,0:T(2,128)S(1)}, s32[4,2,64]{2,1,0:T(2,128)S(1)}, u32[]{:S(2)}, u32[]{:S(2)}) collective-permute-start(s32[4,2,64]{2,1,0:T(2,128)S(1)} %pad_add_fusion.2), channel_id=1, source_target_pairs={{0,96},{1,25},{2,98},{3,27},{4,100},{5,29},{6,102},{7,31},{8,104},... | collective-permute-start | bytes 6152 | tf_op jit(solution)/shard_map/ppermute | solution.py:43
  23.4 3.5 %collective-permute-done.10 = s32[4,2,64]{2,1,0:T(2,128)S(1)} collective-permute-done((s32[4,2,64]{2,1,0:T(2,128)S(1)}, s32[4,2,64]{2,1,0:T(2,128)S(1)}, u32[]{:S(2)}, u32[]{:S(2)}) %collective-permute-start.10) | collective-permute-done | bytes 2080 | tf_op jit(solution)/shard_map/ppermute | solution.py:43
  37.3 3.1 %collective-permute-start.15 = (bf16[2,256,2048]{2,1,0:T(8,128)(2,1)S(1)}, bf16[2,256,2048]{2,1,0:T(8,128)(2,1)}, u32[]{:S(2)}, u32[]{:S(2)}) collective-permute-start(bf16[2,256,2048]{2,1,0:T(8,128)(2,1)S(1)} %shard_map.67.refs_0_), channel_id=1, source_target_pairs={{0,24},{1,97},{2,26},{3,99},{4,28},{5,101},{6,30},{7,103},{8,0},{9... | collective-permute-start | bytes 6291464 | tf_op jit(solution)/shard_map/ppermute | solution.py:43
  47.7 3.1 %collective-permute-done.16.refs_1_ = bf16[2,64,2048]{2,1,0:T(8,128)(2,1)S(1)} collective-permute-done((bf16[2,64,2048]{2,1,0:T(8,128)(2,1)S(1)}, bf16[2,64,2048]{2,1,0:T(8,128)(2,1)S(1)}, u32[]{:S(2)}, u32[]{:S(2)}) %collective-permute-start.16) | collective-permute-done | bytes 524320 | tf_op jit(solution)/shard_map/ppermute | solution.py:51
  53.3 3.2 %collective-permute-start.19 = (bf16[2,32,2048]{2,1,0:T(8,128)(2,1)}, bf16[2,32,2048]{2,1,0:T(8,128)(2,1)}, u32[]{:S(2)}, u32[]{:S(2)}) collective-permute-start(bf16[2,32,2048]{2,1,0:T(8,128)(2,1)} %slice.161), channel_id=1, source_target_pairs={{0,6},{2,0},{4,2},{6,4},{1,7},{3,1},{5,3},{7,5},{8,14},{10,8},{12,... | collective-permute-start | bytes 786440 | tf_op jit(solution)/shard_map/ppermute | solution.py:55
  56.6 2.7 %collective-permute-done.18.refs_3_ = bf16[2,32,2048]{2,1,0:T(8,128)(2,1)S(1)} collective-permute-done((bf16[2,32,2048]{2,1,0:T(8,128)(2,1)}, bf16[2,32,2048]{2,1,0:T(8,128)(2,1)S(1)}, u32[]{:S(2)}, u32[]{:S(2)}) %collective-permute-start.18) | collective-permute-done | bytes 262176 | tf_op jit(solution)/shard_map/ppermute | solution.py:51
  68.4 2.8 %collective-permute-start.26 = (bf16[2,128,2048]{2,1,0:T(8,128)(2,1)S(1)}, bf16[2,128,2048]{2,1,0:T(8,128)(2,1)S(1)}, u32[]{:S(2)}, u32[]{:S(2)}) collective-permute-start(bf16[2,128,2048]{2,1,0:T(8,128)(2,1)S(1)} %shard_map.69), channel_id=1, source_target_pairs={{0,24},{1,97},{2,26},{3,99},{4,28},{5,101},{6,30},{7,103},{8,0},{9... | collective-permute-start | bytes 3145736 | tf_op jit(solution)/shard_map/ppermute | solution.py:43
  81.4 2.8 %convolution_add_fusion.1.refs_2_ = f32[512,256]{1,0:T(8,128)} fusion(f32[512,256]{1,0:T(8,128)S(1)} %fusion.2, bf16[512,2048]{1,0:T(8,128)(2,1)S(1)} %get-tuple-element.120, bf16[2,256,2048]{2,1,0:T(8,128)(2,1)} %collective-permute-done.15.refs_0_.refs_2_), kind=kOutput, calls=%fused_computation.5 | convolution fusion | flops 537001984 | bytes 4194304 | tf_op jit(solution)/shard_map/dot_general | solution.py:63
  88.4 2.7 %fusion = f32[512,256]{1,0:T(8,128)S(1)} fusion(bf16[512,2048]{1,0:T(8,128)(2,1)} %copy-done.9, bf16[2,256,2048]{2,1,0:T(8,128)(2,1)} %shard_map.71.refs_3_), kind=kOutput, calls=%fused_computation.9 | convolution fusion | flops 536870912 | bytes 3670016 | tf_op jit(solution)/shard_map/dot_general | solution.py:63
  93.2 2.7 %shard_map.72.refs_0_ = f32[16,128]{1,0:T(8,128)S(1)} custom-call(s32[1]{0:T(128)} %bitcast.core, f32[1]{0:T(128)} %bitcast.1.amax, f32[512,256]{1,0:T(8,128)S(1)} %convolution_add_fusion.3.refs_0_, f32[512,256]{1,0:T(8,128)S(1)} %convolution_add_fusion.2.refs_1_, f32[512,256]{1,0:T(8,128)S(1)} %copy-done, f32[512,256]{1,0:T(8,128)S(1)} %convolution_add_fusion.refs_3_, ...), custom_call_target="tpu_custom_call" | custom-call | flops 10485760 | bytes 2097152 | tf_op jit(solution)/shard_map/pallas_call | solution.py:173
  101.4 3.0 %collective-permute-done.33.refs_3_ = f32[16,128]{1,0:T(8,128)S(1)} collective-permute-done((f32[16,128]{1,0:T(8,128)S(1)}, f32[16,128]{1,0:T(8,128)S(1)}, u32[]{:S(2)}, u32[]{:S(2)}) %collective-permute-start.33) | collective-permute-done | bytes 8224 | tf_op jit(solution)/shard_map/ppermute | solution.py:59
  106.0 3.2 %collective-permute-start.39 = (f32[8,128]{1,0:T(8,128)S(1)}, f32[8,128]{1,0:T(8,128)S(1)}, u32[]{:S(2)}, u32[]{:S(2)}) collective-permute-start(f32[8,128]{1,0:T(8,128)S(1)} %get-tuple-element.131), channel_id=1, source_target_pairs={{0,96},{1,25},{2,98},{3,27},{4,100},{5,29},{6,102},{7,31},{8,104},... | collective-permute-start | bytes 12296 | tf_op jit(solution)/shard_map/ppermute | solution.py:43
  110.8 3.5 %collective-permute-done.40 = f32[8,128]{1,0:T(8,128)S(1)} collective-permute-done((f32[8,128]{1,0:T(8,128)S(1)}, f32[8,128]{1,0:T(8,128)S(1)}, u32[]{:S(2)}, u32[]{:S(2)}) %collective-permute-start.40) | collective-permute-done | bytes 4128 | tf_op jit(solution)/shard_map/ppermute | solution.py:43
  115.1 2.5 %collective-permute-start.42 = (f32[32,128]{1,0:T(8,128)S(1)}, f32[32,128]{1,0:T(8,128)S(1)}, u32[]{:S(2)}, u32[]{:S(2)}) collective-permute-start(f32[32,128]{1,0:T(8,128)S(1)} %constant_dynamic-update-slice_fusion.4.refs_7_), channel_id=1, source_target_pairs={{0,24},{1,97},{2,26},{3,99},{4,28},{5,101},{6,30},{7,103},{8,0},{9... | collective-permute-start | bytes 49160 | tf_op jit(solution)/shard_map/ppermute | solution.py:43
  119.3 3.5 %collective-permute-done.43.refs_10_ = f32[32,128]{1,0:T(8,128)S(1)} collective-permute-done((f32[32,128]{1,0:T(8,128)S(1)}, f32[32,128]{1,0:T(8,128)S(1)}, u32[]{:S(2)}, u32[]{:S(2)}) %collective-permute-start.43) | collective-permute-done | bytes 16416 | tf_op jit(solution)/shard_map/ppermute | solution.py:43
  127.1 9.2 %shard_map.76 = (f32[128,2048]{1,0:T(8,128)S(1)}, f32[128,2048]{1,0:T(8,128)S(1)}, f32[128,2048]{1,0:T(8,128)S(1)}, f32[128,2048]{1,0:T(8,128)S(1)}) custom-call(f32[8,128]{1,0:T(8,128)S(1)} %get-tuple-element.132.bound, bf16[384,1024]{1,0:T(8,128)(2,1)S(1)} %get-tuple-element.133.rest, bf16[384,1024]{1,0:T(8,128)(2,1)S(1)} %collective-permute-done.44.rest_o, ...), custom_call_target="tpu_custom_call" | custom-call | flops 4294967296 | bytes 12582912 | tf_op jit(solution)/shard_map/pallas_call | solution.py:309
  136.5 3.2 %collective-permute-start.47 = (f16[64,2048]{1,0:T(8,128)(2,1)S(1)}, f16[64,2048]{1,0:T(8,128)(2,1)S(1)}, u32[]{:S(2)}, u32[]{:S(2)}) collective-permute-start(f16[64,2048]{1,0:T(8,128)(2,1)S(1)} %get-tuple-element.153), channel_id=1, source_target_pairs={{0,6},{2,0},{4,2},{6,4},{1,7},{3,1},{5,3},{7,5},{8,14},{10,8},{12,... | collective-permute-start | bytes 786440 | tf_op jit(solution)/shard_map/ppermute | solution.py:55
  142.0 4.9 %collective-permute-done.46 = f16[64,2048]{1,0:T(8,128)(2,1)S(1)} collective-permute-done((f16[64,2048]{1,0:T(8,128)(2,1)S(1)}, f16[64,2048]{1,0:T(8,128)(2,1)S(1)}, u32[]{:S(2)}, u32[]{:S(2)}) %collective-permute-start.46) | collective-permute-done | bytes 262176 | tf_op jit(solution)/shard_map/ppermute | solution.py:51
  146.9 4.0 %collective-permute-done.48 = f16[64,2048]{1,0:T(8,128)(2,1)S(1)} collective-permute-done((f16[64,2048]{1,0:T(8,128)(2,1)S(1)}, f16[64,2048]{1,0:T(8,128)(2,1)S(1)}, u32[]{:S(2)}, u32[]{:S(2)}) %collective-permute-start.48) | collective-permute-done | bytes 262176 | tf_op jit(solution)/shard_map/ppermute | solution.py:55
  151.7 3.0 %collective-permute-start.51 = (f16[64,2048]{1,0:T(8,128)(2,1)S(1)}, f16[64,2048]{1,0:T(8,128)(2,1)S(1)}, u32[]{:S(2)}, u32[]{:S(2)}) collective-permute-start(f16[64,2048]{1,0:T(8,128)(2,1)S(1)} %add_convert_fusion), channel_id=1, source_target_pairs={{0,6},{2,0},{4,2},{6,4},{1,7},{3,1},{5,3},{7,5},{8,14},{10,8},{12,... | collective-permute-start | bytes 786440 | tf_op jit(solution)/shard_map/ppermute | solution.py:55
  155.9 3.5 %collective-permute-done.51 = f16[64,2048]{1,0:T(8,128)(2,1)S(1)} collective-permute-done((f16[64,2048]{1,0:T(8,128)(2,1)S(1)}, f16[64,2048]{1,0:T(8,128)(2,1)S(1)}, u32[]{:S(2)}, u32[]{:S(2)}) %collective-permute-start.51) | collective-permute-done | bytes 262176 | tf_op jit(solution)/shard_map/ppermute | solution.py:55
  159.4 3.6 %collective-permute-done.50 = f16[64,2048]{1,0:T(8,128)(2,1)S(1)} collective-permute-done((f16[64,2048]{1,0:T(8,128)(2,1)S(1)}, f16[64,2048]{1,0:T(8,128)(2,1)S(1)}, u32[]{:S(2)}, u32[]{:S(2)}) %collective-permute-start.50) | collective-permute-done | bytes 262176 | tf_op jit(solution)/shard_map/ppermute | solution.py:51
  (194 shorter events, 79.5 us)
Async XLA Ops:
  3.4 11.7 %collective-permute-start.1 = (bf16[2,64,2048]{2,1,0:T(8,128)(2,1)S(1)}, bf16[2,64,2048]{2,1,0:T(8,128)(2,1)S(1)}, u32[]{:S(2)}, u32[]{:S(2)}) collective-permute-start(bf16[2,64,2048]{2,1,0:T(8,128)(2,1)S(1)} %pad_maximum_fusion.refs_0_), channel_id=1, source_target_pairs={{0,32},{1,9},{2,34},{3,11},{4,36},{5,13},{6,38},{7,15},{8,40},{9,1... | collective-permute-start | bytes 1572872 | tf_op jit(solution)/shard_map/ppermute | solution.py:43
  5.1 10.0 %collective-permute-start.2 = (bf16[2,64,2048]{2,1,0:T(8,128)(2,1)S(1)}, bf16[2,64,2048]{2,1,0:T(8,128)(2,1)S(1)}, u32[]{:S(2)}, u32[]{:S(2)}) collective-permute-start(bf16[2,64,2048]{2,1,0:T(8,128)(2,1)S(1)} %pad_maximum_fusion.refs_0_), channel_id=1, source_target_pairs={{0,96},{1,25},{2,98},{3,27},{4,100},{5,29},{6,102},{7,31},{8,104},... | collective-permute-start | bytes 1572872 | tf_op jit(solution)/shard_map/ppermute | solution.py:43
  15.1 11.8 %collective-permute-start.6 = (bf16[2,32,2048]{2,1,0:T(8,128)(2,1)S(1)}, bf16[2,32,2048]{2,1,0:T(8,128)(2,1)S(1)}, u32[]{:S(2)}, u32[]{:S(2)}) collective-permute-start(bf16[2,32,2048]{2,1,0:T(8,128)(2,1)S(1)} %slice.116), channel_id=1, source_target_pairs={{0,32},{1,9},{2,34},{3,11},{4,36},{5,13},{6,38},{7,15},{8,40},{9,1... | collective-permute-start | bytes 786440 | tf_op jit(solution)/shard_map/ppermute | solution.py:43
  16.0 10.9 %collective-permute-start.7 = (bf16[2,32,2048]{2,1,0:T(8,128)(2,1)S(1)}, bf16[2,32,2048]{2,1,0:T(8,128)(2,1)S(1)}, u32[]{:S(2)}, u32[]{:S(2)}) collective-permute-start(bf16[2,32,2048]{2,1,0:T(8,128)(2,1)S(1)} %slice.117), channel_id=1, source_target_pairs={{0,96},{1,25},{2,98},{3,27},{4,100},{5,29},{6,102},{7,31},{8,104},... | collective-permute-start | bytes 786440 | tf_op jit(solution)/shard_map/ppermute | solution.py:43
  27.6 8.6 %collective-permute-start.11 = (s32[4,4,2,64]{3,2,1,0:T(2,128)S(1)}, s32[4,4,2,64]{3,2,1,0:T(2,128)S(1)}, u32[]{:S(2)}, u32[]{:S(2)}) collective-permute-start(s32[4,4,2,64]{3,2,1,0:T(2,128)S(1)} %pad_add_fusion.1), channel_id=1, source_target_pairs={{0,8},{1,33},{2,10},{3,35},{4,12},{5,37},{6,14},{7,39},{8,16},{9,4... | collective-permute-start | bytes 24584 | tf_op jit(solution)/shard_map/ppermute | solution.py:43
  37.2 27.4 %collective-permute-start.14 = (bf16[2,256,2048]{2,1,0:T(8,128)(2,1)S(1)}, bf16[2,256,2048]{2,1,0:T(8,128)(2,1)}, u32[]{:S(2)}, u32[]{:S(2)}) collective-permute-start(bf16[2,256,2048]{2,1,0:T(8,128)(2,1)S(1)} %shard_map.67.refs_0_), channel_id=1, source_target_pairs={{0,8},{1,33},{2,10},{3,35},{4,12},{5,37},{6,14},{7,39},{8,16},{9,4... | collective-permute-start | bytes 6291464 | tf_op jit(solution)/shard_map/ppermute | solution.py:43
  37.3 27.2 %collective-permute-start.15 = (bf16[2,256,2048]{2,1,0:T(8,128)(2,1)S(1)}, bf16[2,256,2048]{2,1,0:T(8,128)(2,1)}, u32[]{:S(2)}, u32[]{:S(2)}) collective-permute-start(bf16[2,256,2048]{2,1,0:T(8,128)(2,1)S(1)} %shard_map.67.refs_0_), channel_id=1, source_target_pairs={{0,24},{1,97},{2,26},{3,99},{4,28},{5,101},{6,30},{7,103},{8,0},{9... | collective-permute-start | bytes 6291464 | tf_op jit(solution)/shard_map/ppermute | solution.py:43
  40.4 10.4 %collective-permute-start.16 = (bf16[2,64,2048]{2,1,0:T(8,128)(2,1)S(1)}, bf16[2,64,2048]{2,1,0:T(8,128)(2,1)S(1)}, u32[]{:S(2)}, u32[]{:S(2)}) collective-permute-start(bf16[2,64,2048]{2,1,0:T(8,128)(2,1)S(1)} %pad_maximum_fusion.refs_0_), channel_id=1, source_target_pairs={{0,2},{2,4},{4,6},{6,0},{1,3},{3,5},{5,7},{7,1},{8,10},{10,12},{12... | collective-permute-start | bytes 1572872 | tf_op jit(solution)/shard_map/ppermute | solution.py:51
  41.3 10.3 %collective-permute-start.17 = (bf16[2,64,2048]{2,1,0:T(8,128)(2,1)S(1)}, bf16[2,64,2048]{2,1,0:T(8,128)(2,1)}, u32[]{:S(2)}, u32[]{:S(2)}) collective-permute-start(bf16[2,64,2048]{2,1,0:T(8,128)(2,1)S(1)} %pad_maximum_fusion.refs_0_), channel_id=1, source_target_pairs={{0,6},{2,0},{4,2},{6,4},{1,7},{3,1},{5,3},{7,5},{8,14},{10,8},{12,... | collective-permute-start | bytes 1572872 | tf_op jit(solution)/shard_map/ppermute | solution.py:55
  43.6 16.7 %collective-permute-start.20 = (bf16[2,64,2048]{2,1,0:T(8,128)(2,1)S(1)}, bf16[2,64,2048]{2,1,0:T(8,128)(2,1)}, u32[]{:S(2)}, u32[]{:S(2)}) collective-permute-start(bf16[2,64,2048]{2,1,0:T(8,128)(2,1)S(1)} %pad_maximum_fusion.refs_0_), channel_id=1, source_target_pairs={{0,1},{1,0},{2,3},{3,2},{4,5},{5,4},{6,7},{7,6},{8,9},{9,8},{10,11... | collective-permute-start | bytes 1572872 | tf_op jit(solution)/shard_map/ppermute | solution.py:47
  51.5 7.8 %collective-permute-start.18 = (bf16[2,32,2048]{2,1,0:T(8,128)(2,1)}, bf16[2,32,2048]{2,1,0:T(8,128)(2,1)S(1)}, u32[]{:S(2)}, u32[]{:S(2)}) collective-permute-start(bf16[2,32,2048]{2,1,0:T(8,128)(2,1)} %slice.160), channel_id=1, source_target_pairs={{0,2},{2,4},{4,6},{6,0},{1,3},{3,5},{5,7},{7,1},{8,10},{10,12},{12... | collective-permute-start | bytes 786440 | tf_op jit(solution)/shard_map/ppermute | solution.py:51
  53.3 7.6 %collective-permute-start.19 = (bf16[2,32,2048]{2,1,0:T(8,128)(2,1)}, bf16[2,32,2048]{2,1,0:T(8,128)(2,1)}, u32[]{:S(2)}, u32[]{:S(2)}) collective-permute-start(bf16[2,32,2048]{2,1,0:T(8,128)(2,1)} %slice.161), channel_id=1, source_target_pairs={{0,6},{2,0},{4,2},{6,4},{1,7},{3,1},{5,3},{7,5},{8,14},{10,8},{12,... | collective-permute-start | bytes 786440 | tf_op jit(solution)/shard_map/ppermute | solution.py:55
  66.2 18.0 %collective-permute-start.25 = (bf16[2,128,2048]{2,1,0:T(8,128)(2,1)S(1)}, bf16[2,128,2048]{2,1,0:T(8,128)(2,1)S(1)}, u32[]{:S(2)}, u32[]{:S(2)}) collective-permute-start(bf16[2,128,2048]{2,1,0:T(8,128)(2,1)S(1)} %shard_map.68), channel_id=1, source_target_pairs={{0,8},{1,33},{2,10},{3,35},{4,12},{5,37},{6,14},{7,39},{8,16},{9,4... | collective-permute-start | bytes 3145736 | tf_op jit(solution)/shard_map/ppermute | solution.py:43
  68.4 15.8 %collective-permute-start.26 = (bf16[2,128,2048]{2,1,0:T(8,128)(2,1)S(1)}, bf16[2,128,2048]{2,1,0:T(8,128)(2,1)S(1)}, u32[]{:S(2)}, u32[]{:S(2)}) collective-permute-start(bf16[2,128,2048]{2,1,0:T(8,128)(2,1)S(1)} %shard_map.69), channel_id=1, source_target_pairs={{0,24},{1,97},{2,26},{3,99},{4,28},{5,101},{6,30},{7,103},{8,0},{9... | collective-permute-start | bytes 3145736 | tf_op jit(solution)/shard_map/ppermute | solution.py:43
  76.8 19.1 %collective-permute-start.27 = (bf16[2,256,2048]{2,1,0:T(8,128)(2,1)S(1)}, bf16[2,256,2048]{2,1,0:T(8,128)(2,1)}, u32[]{:S(2)}, u32[]{:S(2)}) collective-permute-start(bf16[2,256,2048]{2,1,0:T(8,128)(2,1)S(1)} %shard_map.67.refs_0_), channel_id=1, source_target_pairs={{0,1},{1,0},{2,3},{3,2},{4,5},{5,4},{6,7},{7,6},{8,9},{9,8},{10,11... | collective-permute-start | bytes 6291464 | tf_op jit(solution)/shard_map/ppermute | solution.py:47
  78.8 17.1 %collective-permute-start.28 = (bf16[2,256,2048]{2,1,0:T(8,128)(2,1)}, bf16[2,256,2048]{2,1,0:T(8,128)(2,1)}, u32[]{:S(2)}, u32[]{:S(2)}) collective-permute-start(bf16[2,256,2048]{2,1,0:T(8,128)(2,1)} %collective-permute-done.14.refs_0_.refs_1_), channel_id=1, source_target_pairs={{0,1},{1,0},{2,3},{3,2},{4,5},{5,4},{6,7},{7,6},{8,9},{9,8},{10,11... | collective-permute-start | bytes 6291464 | tf_op jit(solution)/shard_map/ppermute | solution.py:47
  84.2 11.8 %collective-permute-start.29 = (bf16[2,256,2048]{2,1,0:T(8,128)(2,1)}, bf16[2,256,2048]{2,1,0:T(8,128)(2,1)}, u32[]{:S(2)}, u32[]{:S(2)}) collective-permute-start(bf16[2,256,2048]{2,1,0:T(8,128)(2,1)} %collective-permute-done.15.refs_0_.refs_2_), channel_id=1, source_target_pairs={{0,1},{1,0},{2,3},{3,2},{4,5},{5,4},{6,7},{7,6},{8,9},{9,8},{10,11... | collective-permute-start | bytes 6291464 | tf_op jit(solution)/shard_map/ppermute | solution.py:47
  85.7 10.2 %collective-permute-start.30 = (bf16[2,256,2048]{2,1,0:T(8,128)(2,1)}, bf16[2,256,2048]{2,1,0:T(8,128)(2,1)}, u32[]{:S(2)}, u32[]{:S(2)}) collective-permute-start(bf16[2,256,2048]{2,1,0:T(8,128)(2,1)} %shard_map.71.refs_3_), channel_id=1, source_target_pairs={{0,1},{1,0},{2,3},{3,2},{4,5},{5,4},{6,7},{7,6},{8,9},{9,8},{10,11... | collective-permute-start | bytes 6291464 | tf_op jit(solution)/shard_map/ppermute | solution.py:47
  136.4 10.4 %collective-permute-start.46 = (f16[64,2048]{1,0:T(8,128)(2,1)S(1)}, f16[64,2048]{1,0:T(8,128)(2,1)S(1)}, u32[]{:S(2)}, u32[]{:S(2)}) collective-permute-start(f16[64,2048]{1,0:T(8,128)(2,1)S(1)} %get-tuple-element.154), channel_id=1, source_target_pairs={{0,2},{2,4},{4,6},{6,0},{1,3},{3,5},{5,7},{7,1},{8,10},{10,12},{12... | collective-permute-start | bytes 786440 | tf_op jit(solution)/shard_map/ppermute | solution.py:51
  136.5 10.4 %collective-permute-start.47 = (f16[64,2048]{1,0:T(8,128)(2,1)S(1)}, f16[64,2048]{1,0:T(8,128)(2,1)S(1)}, u32[]{:S(2)}, u32[]{:S(2)}) collective-permute-start(f16[64,2048]{1,0:T(8,128)(2,1)S(1)} %get-tuple-element.153), channel_id=1, source_target_pairs={{0,6},{2,0},{4,2},{6,4},{1,7},{3,1},{5,3},{7,5},{8,14},{10,8},{12,... | collective-permute-start | bytes 786440 | tf_op jit(solution)/shard_map/ppermute | solution.py:55
  139.8 11.1 %collective-permute-start.48 = (f16[64,2048]{1,0:T(8,128)(2,1)S(1)}, f16[64,2048]{1,0:T(8,128)(2,1)S(1)}, u32[]{:S(2)}, u32[]{:S(2)}) collective-permute-start(f16[64,2048]{1,0:T(8,128)(2,1)S(1)} %slice_convert_fusion.1), channel_id=1, source_target_pairs={{0,6},{2,0},{4,2},{6,4},{1,7},{3,1},{5,3},{7,5},{8,14},{10,8},{12,... | collective-permute-start | bytes 786440 | tf_op jit(solution)/shard_map/ppermute | solution.py:55
  140.0 11.7 %collective-permute-start.49 = (f16[64,2048]{1,0:T(8,128)(2,1)S(1)}, f16[64,2048]{1,0:T(8,128)(2,1)S(1)}, u32[]{:S(2)}, u32[]{:S(2)}) collective-permute-start(f16[64,2048]{1,0:T(8,128)(2,1)S(1)} %slice_convert_fusion), channel_id=1, source_target_pairs={{0,2},{2,4},{4,6},{6,0},{1,3},{3,5},{5,7},{7,1},{8,10},{10,12},{12... | collective-permute-start | bytes 786440 | tf_op jit(solution)/shard_map/ppermute | solution.py:51
  151.7 7.7 %collective-permute-start.51 = (f16[64,2048]{1,0:T(8,128)(2,1)S(1)}, f16[64,2048]{1,0:T(8,128)(2,1)S(1)}, u32[]{:S(2)}, u32[]{:S(2)}) collective-permute-start(f16[64,2048]{1,0:T(8,128)(2,1)S(1)} %add_convert_fusion), channel_id=1, source_target_pairs={{0,6},{2,0},{4,2},{6,4},{1,7},{3,1},{5,3},{7,5},{8,14},{10,8},{12,... | collective-permute-start | bytes 786440 | tf_op jit(solution)/shard_map/ppermute | solution.py:55
  154.8 8.2 %collective-permute-start.50 = (f16[64,2048]{1,0:T(8,128)(2,1)S(1)}, f16[64,2048]{1,0:T(8,128)(2,1)S(1)}, u32[]{:S(2)}, u32[]{:S(2)}) collective-permute-start(f16[64,2048]{1,0:T(8,128)(2,1)S(1)} %add_convert_fusion.1), channel_id=1, source_target_pairs={{0,2},{2,4},{4,6},{6,0},{1,3},{3,5},{5,7},{7,1},{8,10},{10,12},{12... | collective-permute-start | bytes 786440 | tf_op jit(solution)/shard_map/ppermute | solution.py:51
  (42 other events, 158.1 us)

commit v2 on v1

--- a/solution.py
+++ b/solution.py
@@ -18,7 +18,7 @@
 DOWN = [(i, (i - 1) % 4) for i in range(4)]
 FAR = [(i, (i + 2) % 4) for i in range(4)]
 RING = (0, 1, 3, 2)
-PARTS = (256, 256, 256, 256)
+PARTS = (256, 256, 256, 128, 128)
 J = sum(PARTS)
 
 
@@ -122,6 +122,26 @@
         compiler_params=params(12),
         cost_estimate=cost(0, 8 << 20),
     )(*mine, *theirs)
+
+
+def last_kernel(i0, i1, gl, gr, out_l, out_r):
+    total = None
+    for h, rows in enumerate((i0, i1)):
+        term = inner(rows[...], jnp.concatenate([gl[h], gr[h]]))
+        total = term if total is None else total + term
+    out_l[...] = total[:, :2 * N]
+    out_r[...] = total[:, 2 * N:]
+
+
+def last_scores(i0, i1, gl, gr):
+    return pl.pallas_call(
+        last_kernel,
+        out_shape=[jax.ShapeDtypeStruct((8 * N, 2 * N), jnp.float32)] * 2,
+        in_specs=[VMEM] * 4,
+        out_specs=[VMEM] * 2,
+        compiler_params=params(12),
+        cost_estimate=cost(8 * 8 * N * 2 * N * i0.shape[1], 7 << 20),
+    )(i0, i1, gl, gr)
 
 
 def masks(rows, cols, at, count):
@@ -280,41 +300,48 @@
     )(core, *parts, rows, cols, lse_i, *plane)
 
 
-def product_kernel(bound, rest, rest_o, far, far_o, *refs):
-    blocks, (here, down_o, up_o, far_out) = refs[:-4], refs[-4:]
+def product_kernel(scaled, bound, mine, theirs, *refs):
+    count = mine.shape[0] // (2 * N)
+    blocks, outs, (held, sems) = refs[:2 * len(PARTS)], refs[2 * len(PARTS):-2], refs[-2:]
+    copies = ([], [])
+    for k in (0, 1):
+        at = 0
+        for n, size in enumerate(PARTS):
+            i = k * len(PARTS) + n
+            copies[k].append(pltpu.make_async_copy(blocks[i].at[k], held.at[k, pl.ds(at, size)], sems.at[i]))
+            copies[k][-1].start()
+            at += size
     shrink = 1.0 / bound[0:1, 0:1]
-
-    def total(mine, theirs):
-        out = None
-        for k, weights in enumerate((mine, theirs)):
-            for n, size in enumerate(PARTS):
-                at = sum(PARTS[:n])
-                term = plain(weights[:, at:at + size], blocks[k * len(PARTS) + n][0])
-                out = term if out is None else out + term
-        return out
-
-    far_out[...] = total(far, far_o) * shrink
-    near = total(rest, rest_o)
-    here[...] = near[:2 * N]
-    down_o[...] = near[2 * N:4 * N] * shrink
-    up_o[...] = near[4 * N:] * shrink
-
-
-def product_of(bound, rest, rest_o, far, far_o, blocks, others):
-    wide, step = blocks[0].shape[2], 256
-    whole = lambda a: pl.BlockSpec(a.shape, lambda i: (0, 0))
-    own = [pl.BlockSpec((1, a.shape[1], step), lambda i: (0, 0, i)) for a in blocks]
-    other = [pl.BlockSpec((1, a.shape[1], step), lambda i: (1, 0, i)) for a in others]
-    heads = (bound, rest, rest_o, far, far_o)
-    return pl.pallas_call(
-        product_kernel,
-        grid=(wide // step,),
-        out_shape=[jax.ShapeDtypeStruct((2 * N, wide), jnp.float32)] * 4,
-        in_specs=[whole(a) for a in heads] + own + other,
-        out_specs=[pl.BlockSpec((2 * N, step), lambda i: (0, i))] * 4,
-        compiler_params=params(16),
-        cost_estimate=cost(32 * N * J * wide, 4 * J * wide + 32 * N * wide),
-    )(*heads, *blocks, *others)
+    step = 512
+    for k, weights in enumerate((mine, theirs)):
+        for copy in copies[k]:
+            copy.wait()
+
+        @pl.loop(0, held.shape[2] // step)
+        def _(j):
+            here = pl.ds(pl.multiple_of(j * step, step), step)
+            term = plain(weights[...], held[k, :, here])
+            for g in range(count):
+                part = term[2 * N * g:2 * N * (g + 1)]
+                if k == 0:
+                    outs[g][:, here] = part
+                else:
+                    part = outs[g][:, here] + part
+                    outs[g][:, here] = part * shrink if g >= scaled else part
+
+
+def product_of(scaled, bound, mine, theirs, blocks, others):
+    rows, wide = mine.shape[0], blocks[0].shape[2]
+    outs = rows // (2 * N)
+    return pl.pallas_call(
+        functools.partial(product_kernel, scaled),
+        out_shape=[jax.ShapeDtypeStruct((2 * N, wide), jnp.float32)] * outs,
+        in_specs=[VMEM] * 3 + [pl.BlockSpec(memory_space=pl.ANY)] * (2 * len(PARTS)),
+        out_specs=[VMEM] * outs,
+        scratch_shapes=[pltpu.VMEM((2, J, wide), jnp.bfloat16), pltpu.SemaphoreType.DMA((2 * len(PARTS),))],
+        compiler_params=params(20),
+        cost_estimate=cost(4 * rows * J * wide, 4 * J * wide + 4 * rows * wide),
+    )(bound, mine, theirs, *blocks, *others)
 
 
 def after(value, *others):
@@ -367,10 +394,13 @@
     i_tgt, j_tgt = look(i_pos), look(j_pos)
     rows = jnp.stack([pick(i_pair, i_id), pick(i_id, i_tgt), pick(i_pair, i_pos)] + [i_pair] * 5, axis=1)
     cols = jnp.stack([pick(j_pair, j_id), pick(j_tgt, j_id), pick(j_pos, j_pair)] + [j_pair] * 5)
+    amax = jnp.maximum(
+        jnp.max(jnp.abs(queries.astype(jnp.float32))), jnp.max(jnp.abs(passages.astype(jnp.float32)))
+    )
     xl, xr = up(own), down(own)
     mine = [own, xl, xr, up(low(xl)[0]), down(high(xr)[0])]
-    dl, dr, group, rows, cols, *held = settle(
-        along(group, SECOND[1]), along(group, SECOND[3]), group, rows, cols, *mine, *[swap(a) for a in mine]
+    dl, dr, group, rows, cols, amax, *held = settle(
+        along(group, SECOND[1]), along(group, SECOND[3]), group, rows, cols, amax, *mine, *[swap(a) for a in mine]
     )
     to_l = pack(tuple((0, k * N, H) for k in range(4)), dl)
     to_r = pack(tuple((0, k * N + H, H) for k in range(4)), dr)
@@ -381,33 +411,30 @@
     others = [swap(after(a, part)) for a, part in zip(blocks, parts)]
     gl, gr, i0, i1, *held = settle(along(to_l, SECOND[1]), along(to_r, SECOND[3]), i0, i1, *parts, *blocks)
     parts, blocks = held[:3], held[3:]
-    last = pack(((0, 0, 2 * N), (1, 0, 2 * N)), gl, gr)
-    blocks.append(last)
-
-    amax = jnp.maximum(
-        jnp.max(jnp.abs(queries.astype(jnp.float32))), jnp.max(jnp.abs(passages.astype(jnp.float32)))
-    )
-
-    parts.append(score(last))
-    found, *held = settle(stats_of(core, amax.reshape(1), parts, rows, cols), *others, swap(last), *blocks)
-    others, blocks = held[:4], held[4:]
+    blocks += [gl, gr]
+
+    parts += last_scores(i0, i1, gl, gr)
+    found, *held = settle(stats_of(core, amax.reshape(1), parts, rows, cols), *others, swap(gl), swap(gr), *blocks)
+    others, blocks = held[:5], held[5:]
     found = ring(found, line)
     lse_i, ends = merged(core, found, [swap(a) for a in found])
     loss = lse_i[4, :N]
     plane = ring(jnp.concatenate(ring(ends, by_first)), by_second)
 
-    args = (core, parts, rows, cols, lse_i, plane)
-    m_far, bound = weights_of(3, 1, *args)
-    m_rest, _ = weights_of(0, 3, *args)
     f16, f32 = jnp.float16, jnp.float32
-    here, to_down, to_up, opposite = product_of(bound, m_rest, swap(m_rest), m_far, swap(m_far), blocks, others)
-    opposite, near_q, near_p = opposite.astype(f16), to_down[:N].astype(f16), to_up[N:].astype(f16)
-    got_q, got_p, down_q, up_p = settle(up(opposite[:N]), down(opposite[N:]), down(near_q), up(near_p))
-    up_q = up((to_up[:N] + got_q.astype(f32)).astype(f16))
-    down_p = down((to_down[N:] + got_p.astype(f32)).astype(f16))
-    grow = bound[0, 0]
-    grad_q = here[:N] + (up_q.astype(f32) + down_q.astype(f32)) * grow
-    grad_p = here[N:] + (up_p.astype(f32) + down_p.astype(f32)) * grow
+    args = (parts, rows, cols, lse_i, plane)
+    m_far, bound = weights_of(3, 1, core, *args)
+    m_far_o = swap(m_far)
+    m_rest, _ = weights_of(0, 3, after(core, m_far), *args)
+    (opposite,) = product_of(0, bound, m_far, m_far_o, blocks, others)
+    opposite = opposite.astype(f16)
+    got_q, got_p, here, to_down, to_up = settle(
+        up(opposite[:N]), down(opposite[N:]), *product_of(1, bound, m_rest, swap(m_rest), blocks, others)
+    )
+    below = up(jnp.concatenate([to_up[:N] + got_q.astype(f32), to_up[N:]]).astype(f16))
+    above = down(jnp.concatenate([to_down[:N], to_down[N:] + got_p.astype(f32)]).astype(f16))
+    grad = here + (below.astype(f32) + above.astype(f32)) * bound[0, 0]
+    grad_q, grad_p = grad[:N], grad[N:]
     return loss, grad_q, grad_p
 
 

time: 165 us -> 165 us (level)
  local copies, waits for them, and re-layouts: 8.95 us -> 13.2 us
  waiting for transfers between devices: 51 us -> 48 us
  Pallas kernels: 21.1 us -> 24 us
  matrix products: 14.9 us -> 12.6 us
  starting transfers between devices: 59.2 us -> 57.2 us
    ppermute x7 -> x6, waiting for transfers between devices: 15.4 us -> 9.44 us  [up(): return lax.ppermute(value, 'x', UP)]
    pallas_call x1 -> x3, Pallas kernels: 9.19 us -> 13.6 us  [the longest x2 10.9 us: product_of(): pl.pallas_call(functools.partial(product_kernel, scaled), out_shape=[jax....]
    unnamed x33 -> x39, local copies, waits for them, and re-layouts: 3.45 us -> 6.63 us
    ppermute x20, waiting for transfers between devices: 15.4 us -> 18.2 us  [along(): return lax.ppermute(value, GRID, moves)]
    dot_general x8 -> x6, matrix products: 14.9 us -> 12.6 us  [inner(): lax.dot_general(left, right, (((1,), (1,)), ((), ())), preferred_element_...]
    ppermute x7 -> x6, waiting for transfers between devices: 7.57 us -> 9.33 us  [down(): return lax.ppermute(value, 'x', DOWN)]
    ppermute x7 -> x6, starting transfers between devices: 5.65 us -> 3.9 us  [up(): return lax.ppermute(value, 'x', UP)]
    ppermute x16 -> x17, waiting for transfers between devices: 6.38 us -> 4.83 us  [swap(): return lax.ppermute(value, 'w', [(0, 1), (1, 0)])]
  transfers between devices with their start and end apart: 52 -> 51, of which waited for: 22 -> 17; matrix products, arithmetic and copies ran while one was open for 15% -> 11% of each run, Pallas kernels for 5% -> 11%
where the time goes in v2:
time: 165 us; the launch traced here: 164 us
  starting transfers between devices  57.2 us (35%)
  waiting for transfers between devices  48 us (29%)
  Pallas kernels  24 us (15%)
  local copies, waits for them, and re-layouts  13.2 us (8%)
  matrix products  12.6 us (8%)
  other arithmetic  6.61 us (4%)
  between operations  2.38 us (1%)
    ppermute x20, starting transfers between devices, along(): return lax.ppermute(value, GRID, moves)  31.6 us
    ppermute x20, waiting for transfers between devices, along(): return lax.ppermute(value, GRID, moves)  18.2 us
    ppermute x6, starting transfers between devices, down(): return lax.ppermute(value, 'x', DOWN)  15.3 us
    dot_general x6, matrix products, inner(): lax.dot_general(left, right, (((1,), (1,)), ((), ())), preferred_element_...  12.6 us
    pallas_call x2, Pallas kernels, product_of(): pl.pallas_call(functools.partial(product_kernel, scaled), out_shape=[jax....  10.9 us
    ppermute x6, waiting for transfers between devices, up(): return lax.ppermute(value, 'x', UP)  9.44 us
    ppermute x6, waiting for transfers between devices, down(): return lax.ppermute(value, 'x', DOWN)  9.33 us
    unnamed x39, local copies, waits for them, and re-layouts  6.63 us
  transfers between devices with their start and end apart: 51, of which 17 were waited for; matrix products, arithmetic and copies ran while one was open for 11% of the time, Pallas kernels for 11%

profile of v2, /device:TPU:0, one launch (start us, length us, event | category | flops | bytes accessed | tf_op | source)
XLA Modules:
  0.0 164.0 jit_solution(2143794308211521615)
XLA Ops:
  12.0 3.2 %collective-permute-done.5 = s32[2,64]{1,0:T(2,128)S(1)} collective-permute-done((s32[2,64]{1,0:T(2,128)S(1)}, s32[2,64]{1,0:T(2,128)S(1)}, u32[]{:S(2)}, u32[]{:S(2)}) %collective-permute-start.5) | collective-permute-done | bytes 544 | tf_op jit(solution)/shard_map/ppermute | solution.py:59
  16.1 2.5 %collective-permute-start.7 = (bf16[2,32,2048]{2,1,0:T(8,128)(2,1)S(1)}, bf16[2,32,2048]{2,1,0:T(8,128)(2,1)S(1)}, u32[]{:S(2)}, u32[]{:S(2)}) collective-permute-start(bf16[2,32,2048]{2,1,0:T(8,128)(2,1)S(1)} %slice.111), channel_id=1, source_target_pairs={{0,96},{1,25},{2,98},{3,27},{4,100},{5,29},{6,102},{7,31},{8,104},... | collective-permute-start | bytes 786440 | tf_op jit(solution)/shard_map/ppermute | solution.py:43
  19.3 3.2 %collective-permute-start.9 = (s32[4,2,64]{2,1,0:T(2,128)S(1)}, s32[4,2,64]{2,1,0:T(2,128)S(1)}, u32[]{:S(2)}, u32[]{:S(2)}) collective-permute-start(s32[4,2,64]{2,1,0:T(2,128)S(1)} %pad_add_fusion.2), channel_id=1, source_target_pairs={{0,96},{1,25},{2,98},{3,27},{4,100},{5,29},{6,102},{7,31},{8,104},... | collective-permute-start | bytes 6152 | tf_op jit(solution)/shard_map/ppermute | solution.py:43
  24.2 3.5 %collective-permute-done.10 = s32[4,2,64]{2,1,0:T(2,128)S(1)} collective-permute-done((s32[4,2,64]{2,1,0:T(2,128)S(1)}, s32[4,2,64]{2,1,0:T(2,128)S(1)}, u32[]{:S(2)}, u32[]{:S(2)}) %collective-permute-start.10) | collective-permute-done | bytes 2080 | tf_op jit(solution)/shard_map/ppermute | solution.py:43
  48.8 3.1 %collective-permute-done.16.refs_1_ = bf16[2,64,2048]{2,1,0:T(8,128)(2,1)S(1)} collective-permute-done((bf16[2,64,2048]{2,1,0:T(8,128)(2,1)S(1)}, bf16[2,64,2048]{2,1,0:T(8,128)(2,1)S(1)}, u32[]{:S(2)}, u32[]{:S(2)}) %collective-permute-start.16) | collective-permute-done | bytes 524320 | tf_op jit(solution)/shard_map/ppermute | solution.py:51
  54.6 3.1 %collective-permute-start.19 = (bf16[2,32,2048]{2,1,0:T(8,128)(2,1)}, bf16[2,32,2048]{2,1,0:T(8,128)(2,1)}, u32[]{:S(2)}, u32[]{:S(2)}) collective-permute-start(bf16[2,32,2048]{2,1,0:T(8,128)(2,1)} %slice.153), channel_id=1, source_target_pairs={{0,6},{2,0},{4,2},{6,4},{1,7},{3,1},{5,3},{7,5},{8,14},{10,8},{12,... | collective-permute-start | bytes 786440 | tf_op jit(solution)/shard_map/ppermute | solution.py:55
  57.7 2.7 %collective-permute-done.18.refs_3_ = bf16[2,32,2048]{2,1,0:T(8,128)(2,1)S(1)} collective-permute-done((bf16[2,32,2048]{2,1,0:T(8,128)(2,1)}, bf16[2,32,2048]{2,1,0:T(8,128)(2,1)S(1)}, u32[]{:S(2)}, u32[]{:S(2)}) %collective-permute-start.18) | collective-permute-done | bytes 262176 | tf_op jit(solution)/shard_map/ppermute | solution.py:51
  71.1 2.8 %fusion.4 = f32[512,256]{1,0:T(8,128)S(1)} fusion(bf16[512,2048]{1,0:T(8,128)(2,1)S(1)} %get-tuple-element.124.i0, bf16[2,256,2048]{2,1,0:T(8,128)(2,1)} %collective-permute-done.14.refs_0_.refs_1_), kind=kOutput, calls=%fused_computation.11 | convolution fusion | flops 536870912 | bytes 3670016 | tf_op jit(solution)/shard_map/dot_general | solution.py:63
  76.4 2.8 %collective-permute-start.26 = (bf16[2,128,2048]{2,1,0:T(8,128)(2,1)S(1)}, bf16[2,128,2048]{2,1,0:T(8,128)(2,1)}, u32[]{:S(2)}, u32[]{:S(2)}) collective-permute-start(bf16[2,128,2048]{2,1,0:T(8,128)(2,1)S(1)} %shard_map.69), channel_id=1, source_target_pairs={{0,24},{1,97},{2,26},{3,99},{4,28},{5,101},{6,30},{7,103},{8,0},{9... | collective-permute-start | bytes 3145736 | tf_op jit(solution)/shard_map/ppermute | solution.py:43
  81.5 2.8 %convolution_add_fusion.1.refs_1_ = f32[512,256]{1,0:T(8,128)} fusion(f32[512,256]{1,0:T(8,128)S(1)} %fusion.4, bf16[512,2048]{1,0:T(8,128)(2,1)S(1)} %get-tuple-element.125.i1, bf16[2,256,2048]{2,1,0:T(8,128)(2,1)} %collective-permute-done.14.refs_0_.refs_1_), kind=kOutput, calls=%fused_computation.5 | convolution fusion | flops 537001984 | bytes 4194304 | tf_op jit(solution)/shard_map/dot_general | solution.py:63
  84.3 2.8 %convolution_add_fusion.refs_2_ = f32[512,256]{1,0:T(8,128)} fusion(f32[512,256]{1,0:T(8,128)S(1)} %fusion.1, bf16[512,2048]{1,0:T(8,128)(2,1)S(1)} %get-tuple-element.125.i1, bf16[2,256,2048]{2,1,0:T(8,128)(2,1)} %collective-permute-done.15.refs_0_.refs_2_), kind=kOutput, calls=%fused_computation.4 | convolution fusion | flops 537001984 | bytes 4194304 | tf_op jit(solution)/shard_map/dot_general | solution.py:63
  87.6 4.3 %collective-permute-done.25.gl.refs_3_ = bf16[2,128,2048]{2,1,0:T(8,128)(2,1)S(1)} collective-permute-done((bf16[2,128,2048]{2,1,0:T(8,128)(2,1)S(1)}, bf16[2,128,2048]{2,1,0:T(8,128)(2,1)S(1)}, u32[]{:S(2)}, u32[]{:S(2)}) %collective-permute-start.25) | collective-permute-done | bytes 1048608 | tf_op jit(solution)/shard_map/ppermute | solution.py:43
  95.8 2.6 %shard_map.71 = (f32[512,128]{1,0:T(8,128)S(1)}, f32[512,128]{1,0:T(8,128)S(1)}) custom-call(bf16[512,2048]{1,0:T(8,128)(2,1)S(1)} %copy-done.4, bf16[512,2048]{1,0:T(8,128)(2,1)S(1)} %copy-done.6, bf16[2,128,2048]{2,1,0:T(8,128)(2,1)S(1)} %collective-permute-done.25.gl.refs_3_, bf16[2,128,2048]{2,1,0:T(8,128)(2,1)} %collective-permute-done.26.gr.refs_4_), custom_call_target="tpu_custom_call" | custom-call | flops 1073741824 | bytes 7340032 | tf_op jit(solution)/shard_map/pallas_call | solution.py:137
  98.4 2.7 %shard_map.72.refs_0_ = f32[16,128]{1,0:T(8,128)S(1)} custom-call(s32[1]{0:T(128)} %bitcast.core, f32[1]{0:T(128)} %bitcast.25.amax, f32[512,256]{1,0:T(8,128)S(1)} %copy-done, f32[512,256]{1,0:T(8,128)S(1)} %copy-done.1, f32[512,256]{1,0:T(8,128)S(1)} %copy-done.2, f32[512,128]{1,0:T(8,128)S(1)} %get-tuple-element.128.refs_3_, ...), custom_call_target="tpu_custom_call" | custom-call | flops 10485760 | bytes 2097152 | tf_op jit(solution)/shard_map/pallas_call | solution.py:193
  106.6 3.0 %collective-permute-done.34.refs_3_ = f32[16,128]{1,0:T(8,128)S(1)} collective-permute-done((f32[16,128]{1,0:T(8,128)S(1)}, f32[16,128]{1,0:T(8,128)S(1)}, u32[]{:S(2)}, u32[]{:S(2)}) %collective-permute-start.34) | collective-permute-done | bytes 8224 | tf_op jit(solution)/shard_map/ppermute | solution.py:59
  111.0 3.2 %collective-permute-start.40 = (f32[8,128]{1,0:T(8,128)S(1)}, f32[8,128]{1,0:T(8,128)S(1)}, u32[]{:S(2)}, u32[]{:S(2)}) collective-permute-start(f32[8,128]{1,0:T(8,128)S(1)} %get-tuple-element.140), channel_id=1, source_target_pairs={{0,96},{1,25},{2,98},{3,27},{4,100},{5,29},{6,102},{7,31},{8,104},... | collective-permute-start | bytes 12296 | tf_op jit(solution)/shard_map/ppermute | solution.py:43
  115.8 3.5 %collective-permute-done.41 = f32[8,128]{1,0:T(8,128)S(1)} collective-permute-done((f32[8,128]{1,0:T(8,128)S(1)}, f32[8,128]{1,0:T(8,128)S(1)}, u32[]{:S(2)}, u32[]{:S(2)}) %collective-permute-start.41) | collective-permute-done | bytes 4128 | tf_op jit(solution)/shard_map/ppermute | solution.py:43
  124.9 3.0 %collective-permute-done.44.refs_11_ = f32[32,128]{1,0:T(8,128)S(1)} collective-permute-done((f32[32,128]{1,0:T(8,128)S(1)}, f32[32,128]{1,0:T(8,128)S(1)}, u32[]{:S(2)}, u32[]{:S(2)}) %collective-permute-start.44) | collective-permute-done | bytes 16416 | tf_op jit(solution)/shard_map/ppermute | solution.py:43
  130.7 4.4 %shard_map.75 = f32[128,2048]{1,0:T(8,128)S(1)} custom-call(f32[8,128]{1,0:T(8,128)S(1)} %get-tuple-element.141.bound, bf16[128,1024]{1,0:T(8,128)(2,1)S(1)} %get-tuple-element.142.mine, bf16[128,1024]{1,0:T(8,128)(2,1)S(1)} %collective-permute-done.45.theirs, bf16[2,256,2048]{2,1,0:T(8,128)(2,1)S(1)} %shard_map.67.refs_0_, ...), custom_call_target="tpu_custom_call" | custom-call | flops 1073741824 | bytes 9437184 | tf_op jit(solution)/shard_map/pallas_call | solution.py:336
  135.4 3.2 %collective-permute-start.47 = (f16[64,2048]{1,0:T(8,128)(2,1)S(1)}, f16[64,2048]{1,0:T(8,128)(2,1)S(1)}, u32[]{:S(2)}, u32[]{:S(2)}) collective-permute-start(f16[64,2048]{1,0:T(8,128)(2,1)S(1)} %get-tuple-element.169), channel_id=1, source_target_pairs={{0,6},{2,0},{4,2},{6,4},{1,7},{3,1},{5,3},{7,5},{8,14},{10,8},{12,... | collective-permute-start | bytes 786440 | tf_op jit(solution)/shard_map/ppermute | solution.py:55
  138.6 6.5 %shard_map.77 = (f32[128,2048]{1,0:T(8,128)S(1)}, f32[128,2048]{1,0:T(8,128)S(1)}, f32[128,2048]{1,0:T(8,128)S(1)}) custom-call(f32[8,128]{1,0:T(8,128)S(1)} %get-tuple-element.141.bound, bf16[384,1024]{1,0:T(8,128)(2,1)S(1)} %get-tuple-element.154.mine, bf16[384,1024]{1,0:T(8,128)(2,1)S(1)} %collective-permute-done.48.theirs, ...), custom_call_target="tpu_custom_call" | custom-call | flops 3221225472 | bytes 11534336 | tf_op jit(solution)/shard_map/pallas_call | solution.py:336
  145.4 2.7 %collective-permute-start.50 = (f16[128,2048]{1,0:T(8,128)(2,1)S(1)}, f16[128,2048]{1,0:T(8,128)(2,1)S(1)}, u32[]{:S(2)}, u32[]{:S(2)}) collective-permute-start(f16[128,2048]{1,0:T(8,128)(2,1)S(1)} %pad_maximum_fusion.2), channel_id=1, source_target_pairs={{0,6},{2,0},{4,2},{6,4},{1,7},{3,1},{5,3},{7,5},{8,14},{10,8},{12,... | collective-permute-start | bytes 1572872 | tf_op jit(solution)/shard_map/ppermute | solution.py:55
  149.5 9.3 %collective-permute-done.50 = f16[128,2048]{1,0:T(8,128)(2,1)S(1)} collective-permute-done((f16[128,2048]{1,0:T(8,128)(2,1)S(1)}, f16[128,2048]{1,0:T(8,128)(2,1)S(1)}, u32[]{:S(2)}, u32[]{:S(2)}) %collective-permute-start.50) | collective-permute-done | bytes 524320 | tf_op jit(solution)/shard_map/ppermute | solution.py:55
  158.8 3.3 %collective-permute-done.49 = f16[128,2048]{1,0:T(8,128)(2,1)S(1)} collective-permute-done((f16[128,2048]{1,0:T(8,128)(2,1)S(1)}, f16[128,2048]{1,0:T(8,128)(2,1)S(1)}, u32[]{:S(2)}, u32[]{:S(2)}) %collective-permute-start.49) | collective-permute-done | bytes 524320 | tf_op jit(solution)/shard_map/ppermute | solution.py:51
  (198 shorter events, 77.2 us)
Async XLA Ops:
  3.5 11.7 %collective-permute-start.1 = (bf16[2,64,2048]{2,1,0:T(8,128)(2,1)S(1)}, bf16[2,64,2048]{2,1,0:T(8,128)(2,1)S(1)}, u32[]{:S(2)}, u32[]{:S(2)}) collective-permute-start(bf16[2,64,2048]{2,1,0:T(8,128)(2,1)S(1)} %pad_maximum_fusion.refs_0_), channel_id=1, source_target_pairs={{0,32},{1,9},{2,34},{3,11},{4,36},{5,13},{6,38},{7,15},{8,40},{9,1... | collective-permute-start | bytes 1572872 | tf_op jit(solution)/shard_map/ppermute | solution.py:43
  5.2 10.0 %collective-permute-start.2 = (bf16[2,64,2048]{2,1,0:T(8,128)(2,1)S(1)}, bf16[2,64,2048]{2,1,0:T(8,128)(2,1)S(1)}, u32[]{:S(2)}, u32[]{:S(2)}) collective-permute-start(bf16[2,64,2048]{2,1,0:T(8,128)(2,1)S(1)} %pad_maximum_fusion.refs_0_), channel_id=1, source_target_pairs={{0,96},{1,25},{2,98},{3,27},{4,100},{5,29},{6,102},{7,31},{8,104},... | collective-permute-start | bytes 1572872 | tf_op jit(solution)/shard_map/ppermute | solution.py:43
  15.2 12.5 %collective-permute-start.6 = (bf16[2,32,2048]{2,1,0:T(8,128)(2,1)S(1)}, bf16[2,32,2048]{2,1,0:T(8,128)(2,1)S(1)}, u32[]{:S(2)}, u32[]{:S(2)}) collective-permute-start(bf16[2,32,2048]{2,1,0:T(8,128)(2,1)S(1)} %slice.110), channel_id=1, source_target_pairs={{0,32},{1,9},{2,34},{3,11},{4,36},{5,13},{6,38},{7,15},{8,40},{9,1... | collective-permute-start | bytes 786440 | tf_op jit(solution)/shard_map/ppermute | solution.py:43
  16.1 11.6 %collective-permute-start.7 = (bf16[2,32,2048]{2,1,0:T(8,128)(2,1)S(1)}, bf16[2,32,2048]{2,1,0:T(8,128)(2,1)S(1)}, u32[]{:S(2)}, u32[]{:S(2)}) collective-permute-start(bf16[2,32,2048]{2,1,0:T(8,128)(2,1)S(1)} %slice.111), channel_id=1, source_target_pairs={{0,96},{1,25},{2,98},{3,27},{4,100},{5,29},{6,102},{7,31},{8,104},... | collective-permute-start | bytes 786440 | tf_op jit(solution)/shard_map/ppermute | solution.py:43
  28.4 9.8 %collective-permute-start.11 = (s32[4,4,2,64]{3,2,1,0:T(2,128)S(1)}, s32[4,4,2,64]{3,2,1,0:T(2,128)S(1)}, u32[]{:S(2)}, u32[]{:S(2)}) collective-permute-start(s32[4,4,2,64]{3,2,1,0:T(2,128)S(1)} %pad_add_fusion.1), channel_id=1, source_target_pairs={{0,8},{1,33},{2,10},{3,35},{4,12},{5,37},{6,14},{7,39},{8,16},{9,4... | collective-permute-start | bytes 24584 | tf_op jit(solution)/shard_map/ppermute | solution.py:43
  30.5 7.7 %collective-permute-start.12 = (s32[4,4,2,64]{3,2,1,0:T(2,128)S(1)}, s32[4,4,2,64]{3,2,1,0:T(2,128)S(1)}, u32[]{:S(2)}, u32[]{:S(2)}) collective-permute-start(s32[4,4,2,64]{3,2,1,0:T(2,128)S(1)} %pad_add_fusion.1), channel_id=1, source_target_pairs={{0,24},{1,97},{2,26},{3,99},{4,28},{5,101},{6,30},{7,103},{8,0},{9... | collective-permute-start | bytes 24584 | tf_op jit(solution)/shard_map/ppermute | solution.py:43
  38.2 27.4 %collective-permute-start.14 = (bf16[2,256,2048]{2,1,0:T(8,128)(2,1)S(1)}, bf16[2,256,2048]{2,1,0:T(8,128)(2,1)}, u32[]{:S(2)}, u32[]{:S(2)}) collective-permute-start(bf16[2,256,2048]{2,1,0:T(8,128)(2,1)S(1)} %shard_map.67.refs_0_), channel_id=1, source_target_pairs={{0,8},{1,33},{2,10},{3,35},{4,12},{5,37},{6,14},{7,39},{8,16},{9,4... | collective-permute-start | bytes 6291464 | tf_op jit(solution)/shard_map/ppermute | solution.py:43
  39.3 26.3 %collective-permute-start.15 = (bf16[2,256,2048]{2,1,0:T(8,128)(2,1)S(1)}, bf16[2,256,2048]{2,1,0:T(8,128)(2,1)}, u32[]{:S(2)}, u32[]{:S(2)}) collective-permute-start(bf16[2,256,2048]{2,1,0:T(8,128)(2,1)S(1)} %shard_map.67.refs_0_), channel_id=1, source_target_pairs={{0,24},{1,97},{2,26},{3,99},{4,28},{5,101},{6,30},{7,103},{8,0},{9... | collective-permute-start | bytes 6291464 | tf_op jit(solution)/shard_map/ppermute | solution.py:43
  41.5 10.4 %collective-permute-start.16 = (bf16[2,64,2048]{2,1,0:T(8,128)(2,1)S(1)}, bf16[2,64,2048]{2,1,0:T(8,128)(2,1)S(1)}, u32[]{:S(2)}, u32[]{:S(2)}) collective-permute-start(bf16[2,64,2048]{2,1,0:T(8,128)(2,1)S(1)} %pad_maximum_fusion.refs_0_), channel_id=1, source_target_pairs={{0,2},{2,4},{4,6},{6,0},{1,3},{3,5},{5,7},{7,1},{8,10},{10,12},{12... | collective-permute-start | bytes 1572872 | tf_op jit(solution)/shard_map/ppermute | solution.py:51
  42.5 10.4 %collective-permute-start.17 = (bf16[2,64,2048]{2,1,0:T(8,128)(2,1)S(1)}, bf16[2,64,2048]{2,1,0:T(8,128)(2,1)}, u32[]{:S(2)}, u32[]{:S(2)}) collective-permute-start(bf16[2,64,2048]{2,1,0:T(8,128)(2,1)S(1)} %pad_maximum_fusion.refs_0_), channel_id=1, source_target_pairs={{0,6},{2,0},{4,2},{6,4},{1,7},{3,1},{5,3},{7,5},{8,14},{10,8},{12,... | collective-permute-start | bytes 1572872 | tf_op jit(solution)/shard_map/ppermute | solution.py:55
  44.8 16.7 %collective-permute-start.20 = (bf16[2,64,2048]{2,1,0:T(8,128)(2,1)S(1)}, bf16[2,64,2048]{2,1,0:T(8,128)(2,1)}, u32[]{:S(2)}, u32[]{:S(2)}) collective-permute-start(bf16[2,64,2048]{2,1,0:T(8,128)(2,1)S(1)} %pad_maximum_fusion.refs_0_), channel_id=1, source_target_pairs={{0,1},{1,0},{2,3},{3,2},{4,5},{5,4},{6,7},{7,6},{8,9},{9,8},{10,11... | collective-permute-start | bytes 1572872 | tf_op jit(solution)/shard_map/ppermute | solution.py:47
  52.7 7.8 %collective-permute-start.18 = (bf16[2,32,2048]{2,1,0:T(8,128)(2,1)}, bf16[2,32,2048]{2,1,0:T(8,128)(2,1)S(1)}, u32[]{:S(2)}, u32[]{:S(2)}) collective-permute-start(bf16[2,32,2048]{2,1,0:T(8,128)(2,1)} %slice.152), channel_id=1, source_target_pairs={{0,2},{2,4},{4,6},{6,0},{1,3},{3,5},{5,7},{7,1},{8,10},{10,12},{12... | collective-permute-start | bytes 786440 | tf_op jit(solution)/shard_map/ppermute | solution.py:51
  75.8 16.1 %collective-permute-start.25 = (bf16[2,128,2048]{2,1,0:T(8,128)(2,1)S(1)}, bf16[2,128,2048]{2,1,0:T(8,128)(2,1)S(1)}, u32[]{:S(2)}, u32[]{:S(2)}) collective-permute-start(bf16[2,128,2048]{2,1,0:T(8,128)(2,1)S(1)} %shard_map.68), channel_id=1, source_target_pairs={{0,8},{1,33},{2,10},{3,35},{4,12},{5,37},{6,14},{7,39},{8,16},{9,4... | collective-permute-start | bytes 3145736 | tf_op jit(solution)/shard_map/ppermute | solution.py:43
  76.4 15.5 %collective-permute-start.26 = (bf16[2,128,2048]{2,1,0:T(8,128)(2,1)S(1)}, bf16[2,128,2048]{2,1,0:T(8,128)(2,1)}, u32[]{:S(2)}, u32[]{:S(2)}) collective-permute-start(bf16[2,128,2048]{2,1,0:T(8,128)(2,1)S(1)} %shard_map.69), channel_id=1, source_target_pairs={{0,24},{1,97},{2,26},{3,99},{4,28},{5,101},{6,30},{7,103},{8,0},{9... | collective-permute-start | bytes 3145736 | tf_op jit(solution)/shard_map/ppermute | solution.py:43
  87.1 14.1 %collective-permute-start.27 = (bf16[2,256,2048]{2,1,0:T(8,128)(2,1)S(1)}, bf16[2,256,2048]{2,1,0:T(8,128)(2,1)}, u32[]{:S(2)}, u32[]{:S(2)}) collective-permute-start(bf16[2,256,2048]{2,1,0:T(8,128)(2,1)S(1)} %shard_map.67.refs_0_), channel_id=1, source_target_pairs={{0,1},{1,0},{2,3},{3,2},{4,5},{5,4},{6,7},{7,6},{8,9},{9,8},{10,11... | collective-permute-start | bytes 6291464 | tf_op jit(solution)/shard_map/ppermute | solution.py:47
  87.1 14.1 %collective-permute-start.28 = (bf16[2,256,2048]{2,1,0:T(8,128)(2,1)}, bf16[2,256,2048]{2,1,0:T(8,128)(2,1)}, u32[]{:S(2)}, u32[]{:S(2)}) collective-permute-start(bf16[2,256,2048]{2,1,0:T(8,128)(2,1)} %collective-permute-done.14.refs_0_.refs_1_), channel_id=1, source_target_pairs={{0,1},{1,0},{2,3},{3,2},{4,5},{5,4},{6,7},{7,6},{8,9},{9,8},{10,11... | collective-permute-start | bytes 6291464 | tf_op jit(solution)/shard_map/ppermute | solution.py:47
  87.6 13.6 %collective-permute-start.29 = (bf16[2,256,2048]{2,1,0:T(8,128)(2,1)}, bf16[2,256,2048]{2,1,0:T(8,128)(2,1)}, u32[]{:S(2)}, u32[]{:S(2)}) collective-permute-start(bf16[2,256,2048]{2,1,0:T(8,128)(2,1)} %collective-permute-done.15.refs_0_.refs_2_), channel_id=1, source_target_pairs={{0,1},{1,0},{2,3},{3,2},{4,5},{5,4},{6,7},{7,6},{8,9},{9,8},{10,11... | collective-permute-start | bytes 6291464 | tf_op jit(solution)/shard_map/ppermute | solution.py:47
  91.9 9.2 %collective-permute-start.30 = (bf16[2,128,2048]{2,1,0:T(8,128)(2,1)S(1)}, bf16[2,128,2048]{2,1,0:T(8,128)(2,1)}, u32[]{:S(2)}, u32[]{:S(2)}) collective-permute-start(bf16[2,128,2048]{2,1,0:T(8,128)(2,1)S(1)} %collective-permute-done.25.gl.refs_3_), channel_id=1, source_target_pairs={{0,1},{1,0},{2,3},{3,2},{4,5},{5,4},{6,7},{7,6},{8,9},{9,8},{10,11... | collective-permute-start | bytes 3145736 | tf_op jit(solution)/shard_map/ppermute | solution.py:47
  91.9 9.3 %collective-permute-start.31 = (bf16[2,128,2048]{2,1,0:T(8,128)(2,1)}, bf16[2,128,2048]{2,1,0:T(8,128)(2,1)}, u32[]{:S(2)}, u32[]{:S(2)}) collective-permute-start(bf16[2,128,2048]{2,1,0:T(8,128)(2,1)} %collective-permute-done.26.gr.refs_4_), channel_id=1, source_target_pairs={{0,1},{1,0},{2,3},{3,2},{4,5},{5,4},{6,7},{7,6},{8,9},{9,8},{10,11... | collective-permute-start | bytes 3145736 | tf_op jit(solution)/shard_map/ppermute | solution.py:47
  130.2 8.4 %collective-permute-start.48 = (bf16[384,1024]{1,0:T(8,128)(2,1)S(1)}, bf16[384,1024]{1,0:T(8,128)(2,1)S(1)}, u32[]{:S(2)}, u32[]{:S(2)}) collective-permute-start(bf16[384,1024]{1,0:T(8,128)(2,1)S(1)} %get-tuple-element.154.mine), channel_id=1, source_target_pairs={{0,1},{1,0},{2,3},{3,2},{4,5},{5,4},{6,7},{7,6},{8,9},{9,8},{10,11... | collective-permute-start | bytes 2359304 | tf_op jit(solution)/shard_map/ppermute | solution.py:47
  135.3 9.8 %collective-permute-start.46 = (f16[64,2048]{1,0:T(8,128)(2,1)S(1)}, f16[64,2048]{1,0:T(8,128)(2,1)S(1)}, u32[]{:S(2)}, u32[]{:S(2)}) collective-permute-start(f16[64,2048]{1,0:T(8,128)(2,1)S(1)} %get-tuple-element.170), channel_id=1, source_target_pairs={{0,2},{2,4},{4,6},{6,0},{1,3},{3,5},{5,7},{7,1},{8,10},{10,12},{12... | collective-permute-start | bytes 786440 | tf_op jit(solution)/shard_map/ppermute | solution.py:51
  135.4 9.8 %collective-permute-start.47 = (f16[64,2048]{1,0:T(8,128)(2,1)S(1)}, f16[64,2048]{1,0:T(8,128)(2,1)S(1)}, u32[]{:S(2)}, u32[]{:S(2)}) collective-permute-start(f16[64,2048]{1,0:T(8,128)(2,1)S(1)} %get-tuple-element.169), channel_id=1, source_target_pairs={{0,6},{2,0},{4,2},{6,4},{1,7},{3,1},{5,3},{7,5},{8,14},{10,8},{12,... | collective-permute-start | bytes 786440 | tf_op jit(solution)/shard_map/ppermute | solution.py:55
  145.4 13.4 %collective-permute-start.50 = (f16[128,2048]{1,0:T(8,128)(2,1)S(1)}, f16[128,2048]{1,0:T(8,128)(2,1)S(1)}, u32[]{:S(2)}, u32[]{:S(2)}) collective-permute-start(f16[128,2048]{1,0:T(8,128)(2,1)S(1)} %pad_maximum_fusion.2), channel_id=1, source_target_pairs={{0,6},{2,0},{4,2},{6,4},{1,7},{3,1},{5,3},{7,5},{8,14},{10,8},{12,... | collective-permute-start | bytes 1572872 | tf_op jit(solution)/shard_map/ppermute | solution.py:55
  148.4 13.7 %collective-permute-start.49 = (f16[128,2048]{1,0:T(8,128)(2,1)S(1)}, f16[128,2048]{1,0:T(8,128)(2,1)S(1)}, u32[]{:S(2)}, u32[]{:S(2)}) collective-permute-start(f16[128,2048]{1,0:T(8,128)(2,1)S(1)} %pad_maximum_fusion.1), channel_id=1, source_target_pairs={{0,2},{2,4},{4,6},{6,0},{1,3},{3,5},{5,7},{7,1},{8,10},{10,12},{12... | collective-permute-start | bytes 1572872 | tf_op jit(solution)/shard_map/ppermute | solution.py:51
  (44 other events, 199.1 us)

commit v3 on v2

--- a/solution.py
+++ b/solution.py
@@ -71,22 +71,30 @@
 
 VMEM = pl.BlockSpec(memory_space=pltpu.VMEM)
 SMEM = pl.BlockSpec(memory_space=pltpu.SMEM)
+HBM = pl.BlockSpec(memory_space=pltpu.HBM)
+GRANT = 52
 
 
 def params(mib):
     return pltpu.CompilerParams(vmem_limit_bytes=mib << 20)
 
 
-def cost(flops, moved, transcendentals=0):
-    return pl.CostEstimate(flops=flops, bytes_accessed=moved, transcendentals=transcendentals)
+FREE = pl.CostEstimate(flops=0, bytes_accessed=0, transcendentals=0)
 
 
 def pack_kernel(plan, *refs):
-    pieces, out = refs[:-1], refs[-1]
-    at = 0
-    for k, start, count in plan:
-        out[:, at:at + count, :] = pieces[k][:, start:start + count, :]
+    pieces, out, sems = refs[:-2], refs[-2], refs[-1]
+    copies, at = [], 0
+    for n, (k, start, count) in enumerate(plan):
+        copies.append(
+            pltpu.make_async_copy(
+                pieces[k].at[:, pl.ds(start, count)], out.at[:, pl.ds(at, count)], sems.at[n]
+            )
+        )
+        copies[n].start()
         at += count
+    for copy in copies:
+        copy.wait()
 
 
 def pack(plan, *pieces):
@@ -94,54 +102,90 @@
     return pl.pallas_call(
         functools.partial(pack_kernel, plan),
         out_shape=jax.ShapeDtypeStruct((2, rows, wide), jnp.bfloat16),
-        in_specs=[VMEM] * len(pieces),
+        in_specs=[pl.BlockSpec(memory_space=pl.ANY)] * len(pieces),
         out_specs=VMEM,
+        scratch_shapes=[pltpu.SemaphoreType.DMA((len(plan),))],
         compiler_params=params(8),
-        cost_estimate=cost(0, 8 * rows * wide),
+        cost_estimate=FREE,
     )(*pieces)
 
 
 def rows_kernel(*refs):
-    mine, theirs, outs = refs[:5], refs[5:10], refs[10:]
-    for k, pieces in enumerate((mine, theirs)):
-        at = 4 * k * N
-        for piece in pieces:
-            count = piece.shape[1]
-            for h in (0, 1):
-                outs[h][at:at + count, :] = piece[h ^ k]
+    pieces, out = refs[:10], refs[10]
+    at = 0
+    for k, piece in enumerate(pieces):
+        count = piece.shape[1]
+        for h in (0, 1):
+            out[h ^ (k // 5), at:at + count, :] = piece[h]
+        at += count
+
+
+def rows_from(pieces):
+    wide = pieces[0].shape[2]
+    return pl.pallas_call(
+        rows_kernel,
+        out_shape=jax.ShapeDtypeStruct((2, 8 * N, wide), jnp.bfloat16),
+        in_specs=[VMEM] * 10,
+        out_specs=VMEM,
+        compiler_params=params(12),
+        cost_estimate=FREE,
+    )(*pieces)
+
+
+def scores_kernel(plan, *refs):
+    blocks = sum(len(group) for group in plan)
+    rows, parts, outs = refs[0], refs[1:1 + blocks], refs[1 + blocks:1 + 2 * blocks]
+    left, held, made, row_sems, sems, out_sems = refs[1 + 2 * blocks:]
+    row_copies = [pltpu.make_async_copy(rows.at[h], left.at[h], row_sems.at[h]) for h in (0, 1)]
+    copies = []
+    for n, group in enumerate(plan):
+        at = 0
+        copies.append([])
+        for k in group:
+            count = parts[k].shape[1]
+            copies[n].append(pltpu.make_async_copy(parts[k], held.at[n, :, pl.ds(at, count)], sems.at[k]))
             at += count
-
-
-def rows_from(mine, theirs):
-    wide = mine[0].shape[2]
-    return pl.pallas_call(
-        rows_kernel,
-        out_shape=[jax.ShapeDtypeStruct((8 * N, wide), jnp.bfloat16)] * 2,
-        in_specs=[VMEM] * 10,
-        out_specs=[VMEM] * 2,
-        compiler_params=params(12),
-        cost_estimate=cost(0, 8 << 20),
-    )(*mine, *theirs)
-
-
-def last_kernel(i0, i1, gl, gr, out_l, out_r):
-    total = None
-    for h, rows in enumerate((i0, i1)):
-        term = inner(rows[...], jnp.concatenate([gl[h], gr[h]]))
-        total = term if total is None else total + term
-    out_l[...] = total[:, :2 * N]
-    out_r[...] = total[:, 2 * N:]
-
-
-def last_scores(i0, i1, gl, gr):
-    return pl.pallas_call(
-        last_kernel,
-        out_shape=[jax.ShapeDtypeStruct((8 * N, 2 * N), jnp.float32)] * 2,
-        in_specs=[VMEM] * 4,
-        out_specs=[VMEM] * 2,
-        compiler_params=params(12),
-        cost_estimate=cost(8 * 8 * N * 2 * N * i0.shape[1], 7 << 20),
-    )(i0, i1, gl, gr)
+    order = [row_copies[0]] + copies[0] + [row_copies[1]] + [copy for group in copies[1:] for copy in group]
+    for copy in order:
+        copy.start()
+    results = []
+    for n, group in enumerate(plan):
+        for copy in copies[n]:
+            copy.wait()
+        if n == 0:
+            row_copies[0].wait()
+        total = inner(left[0], held[n, 0])
+        if n == 0:
+            row_copies[1].wait()
+        made[n] = total + inner(left[1], held[n, 1])
+        at = 0
+        for k in group:
+            count = parts[k].shape[1]
+            results.append(pltpu.make_async_copy(made.at[n, :, pl.ds(at, count)], outs[k], out_sems.at[k]))
+            results[-1].start()
+            at += count
+    for copy in results:
+        copy.wait()
+
+
+def scores_of(grant, rows, plan, *blocks):
+    wide = rows.shape[2]
+    return pl.pallas_call(
+        functools.partial(scores_kernel, plan),
+        out_shape=[jax.ShapeDtypeStruct((8 * N, a.shape[1]), jnp.float32) for a in blocks],
+        in_specs=[pl.BlockSpec(memory_space=pl.ANY)] * (1 + len(blocks)),
+        out_specs=[HBM] * len(blocks),
+        scratch_shapes=[
+            pltpu.VMEM((2, 8 * N, wide), jnp.bfloat16),
+            pltpu.VMEM((len(plan), 2, 4 * N, wide), jnp.bfloat16),
+            pltpu.VMEM((len(plan), 8 * N, 4 * N), jnp.float32),
+            pltpu.SemaphoreType.DMA((2,)),
+            pltpu.SemaphoreType.DMA((len(blocks),)),
+            pltpu.SemaphoreType.DMA((len(blocks),)),
+        ],
+        compiler_params=params(grant),
+        cost_estimate=FREE,
+    )(rows, *blocks)
 
 
 def masks(rows, cols, at, count):
@@ -151,26 +195,37 @@
     return same_u != same_v, (cross_u != cross_v) | hit, hit
 
 
-def scores_at(parts, at, count):
-    return jnp.concatenate([part[pl.ds(at, count), :] for part in parts], axis=1) * SCALE
+def gather_parts(parts, held, sems):
+    copies, at = [], 0
+    for n, (part, size) in enumerate(zip(parts, PARTS)):
+        copies.append(pltpu.make_async_copy(part, held.at[:, pl.ds(at, size)], sems.at[n]))
+        copies[n].start()
+        at += size
+    return copies
+
+
+HELD = [pltpu.VMEM((8 * N, J), jnp.float32), pltpu.SemaphoreType.DMA((len(PARTS),))]
 
 
 STATS = 16
 
 
 def stats_kernel(core, amax, *refs):
-    parts, (rows, cols, out, keep) = refs[:-4], refs[-4:]
+    parts, (rows, cols, out, keep, held, sems) = refs[:-6], refs[-6:]
+    copies = gather_parts(parts, held, sems)
     step = 32
     inc = core[0] == 1
     keep[...] = jnp.zeros_like(keep)
+    for copy in copies:
+        copy.wait()
 
     @pl.loop(0, 4 * N // step)
     def _(k):
         at = pl.multiple_of(k * step, step)
         keep_s, keep_c, hit = masks(rows, cols, at, step)
         keep_c = keep_c & inc
-        same = scores_at(parts, at, step)
-        cross = scores_at(parts, pl.multiple_of(at + 4 * N, step), step)
+        same = held[pl.ds(at, step), :] * SCALE
+        cross = held[pl.ds(pl.multiple_of(at + 4 * N, step), step), :] * SCALE
         same = jnp.where(keep_s, same, -BIG)
         hits = jnp.sum(jnp.where(hit & inc, cross, 0.0), axis=1, keepdims=True)
         cross = jnp.where(keep_c, cross, -BIG)
@@ -193,11 +248,11 @@
     return pl.pallas_call(
         stats_kernel,
         out_shape=jax.ShapeDtypeStruct((STATS, 128), jnp.float32),
-        in_specs=[SMEM] * 2 + [VMEM] * (len(parts) + 2),
+        in_specs=[SMEM] * 2 + [HBM] * len(parts) + [VMEM] * 2,
         out_specs=VMEM,
-        scratch_shapes=[pltpu.VMEM((12, 128, 128), jnp.float32)],
-        compiler_params=params(8),
-        cost_estimate=cost(10 << 20, 2 << 20, 1 << 19),
+        scratch_shapes=[pltpu.VMEM((12, 128, 128), jnp.float32)] + HELD,
+        compiler_params=params(GRANT),
+        cost_estimate=FREE,
     )(core, amax, *parts, rows, cols)
 
 
@@ -236,7 +291,7 @@
         in_specs=[SMEM] + [VMEM] * 8,
         out_specs=[VMEM] * 2,
         compiler_params=params(4),
-        cost_estimate=cost(1 << 16, 1 << 16, 1 << 14),
+        cost_estimate=FREE,
     )(core, *mine, *theirs)
 
 
@@ -255,7 +310,8 @@
 
 
 def weights_kernel(first, count, core, *refs):
-    parts, (rows, cols, lse_i, *plane, out, bound, col) = refs[:len(PARTS)], refs[len(PARTS):]
+    parts, (rows, cols, lse_i, *plane, out, bound, col, held, sems) = refs[:len(PARTS)], refs[len(PARTS):]
+    copies = gather_parts(parts, held, sems)
     step = 32
     w = core[0]
     for g in range(4):
@@ -268,6 +324,8 @@
     loose = jnp.max(functools.reduce(jnp.maximum, [v[1:2] for v in ends]), axis=1, keepdims=True)
     most = jnp.max(functools.reduce(jnp.maximum, [v[2:3] for v in ends]), axis=1, keepdims=True)
     bound[...] = jnp.broadcast_to(jnp.maximum(loose, 1e-3) * jnp.maximum(most, 1e-20), (8, 128))
+    for copy in copies:
+        copy.wait()
 
     @pl.loop(0, count * N // step)
     def _(k):
@@ -275,8 +333,8 @@
         keep_s, keep_c, hit = masks(rows, cols, at, step)
         li = col[0, pl.ds(at, step), 0:1]
         lc = col[1, pl.ds(at, step), 0:1]
-        same = scores_at(parts, at, step)
-        cross = scores_at(parts, pl.multiple_of(at + 4 * N, step), step)
+        same = held[pl.ds(at, step), :] * SCALE
+        cross = held[pl.ds(pl.multiple_of(at + 4 * N, step), step), :] * SCALE
         m_s = jnp.where(keep_s, jnp.exp(same - li) + jnp.exp(same - lj), 0.0)
         m_c = jnp.where(keep_c, jnp.exp((cross - lc) - cross_j), 0.0) - jnp.where(hit, 1.0, 0.0)
         group = k // (N // step)
@@ -292,11 +350,11 @@
             jax.ShapeDtypeStruct((count * 2 * N, J), jnp.bfloat16),
             jax.ShapeDtypeStruct((8, 128), jnp.float32),
         ],
-        in_specs=[SMEM] + [VMEM] * (len(parts) + 7),
+        in_specs=[SMEM] + [HBM] * len(parts) + [VMEM] * 7,
         out_specs=[VMEM] * 2,
-        scratch_shapes=[pltpu.VMEM((2, 4 * N, 128), jnp.float32)],
-        compiler_params=params(8),
-        cost_estimate=cost(count * (3 << 20), count << 19, count * 3 * N * J),
+        scratch_shapes=[pltpu.VMEM((2, 4 * N, 128), jnp.float32)] + HELD,
+        compiler_params=params(GRANT),
+        cost_estimate=FREE,
     )(core, *parts, rows, cols, lse_i, *plane)
 
 
@@ -336,11 +394,11 @@
     return pl.pallas_call(
         functools.partial(product_kernel, scaled),
         out_shape=[jax.ShapeDtypeStruct((2 * N, wide), jnp.float32)] * outs,
-        in_specs=[VMEM] * 3 + [pl.BlockSpec(memory_space=pl.ANY)] * (2 * len(PARTS)),
+        in_specs=[VMEM] * 3 + [HBM] * (2 * len(PARTS)),
         out_specs=[VMEM] * outs,
         scratch_shapes=[pltpu.VMEM((2, J, wide), jnp.bfloat16), pltpu.SemaphoreType.DMA((2 * len(PARTS),))],
-        compiler_params=params(20),
-        cost_estimate=cost(4 * rows * J * wide, 4 * J * wide + 4 * rows * wide),
+        compiler_params=params(GRANT),
+        cost_estimate=FREE,
     )(bound, mine, theirs, *blocks, *others)
 
 
@@ -404,16 +462,15 @@
     )
     to_l = pack(tuple((0, k * N, H) for k in range(4)), dl)
     to_r = pack(tuple((0, k * N + H, H) for k in range(4)), dr)
-    i0, i1 = rows_from(held[:5], held[5:])
-    score = lambda a: inner(i0, a[0]) + inner(i1, a[1])
+    rows_i = rows_from([after(held[0], to_l, to_r)] + held[1:])
     blocks = [group, dl, dr]
-    parts = [score(a) for a in blocks]
-    others = [swap(after(a, part)) for a, part in zip(blocks, parts)]
-    gl, gr, i0, i1, *held = settle(along(to_l, SECOND[1]), along(to_r, SECOND[3]), i0, i1, *parts, *blocks)
+    parts = scores_of(24, rows_i, ((0,), (1,), (2,)), *blocks)
+    others = [swap(after(a, rows_i)) for a in blocks]
+    gl, gr, *held = settle(along(to_l, SECOND[1]), along(to_r, SECOND[3]), *parts, *blocks)
     parts, blocks = held[:3], held[3:]
     blocks += [gl, gr]
 
-    parts += last_scores(i0, i1, gl, gr)
+    parts += scores_of(56, rows_i, ((0, 1),), gl, gr)
     found, *held = settle(stats_of(core, amax.reshape(1), parts, rows, cols), *others, swap(gl), swap(gr), *blocks)
     others, blocks = held[:5], held[5:]
     found = ring(found, line)

time: 165 us -> 168 us (1.018)
  Pallas kernels: 24 us -> 38.8 us
  matrix products: 12.6 us -> 0 us
  other arithmetic: 6.61 us -> 10.7 us
  waiting for transfers between devices: 48 us -> 44.6 us
    dot_general x6 -> x0, matrix products: 12.6 us -> none  [inner(): lax.dot_general(left, right, (((1,), (1,)), ((), ())), preferred_element_...]
    pallas_call x2 -> x3, Pallas kernels: 4.64 us -> 14.1 us  [the longest x2 12.1 us: scores_of(): pl.pallas_call(functools.partial(scores_kernel, plan), out_shape=[jax.Sha...]
    ppermute x20, waiting for transfers between devices: 18.2 us -> 15.5 us  [along(): return lax.ppermute(value, GRID, moves)]
    pallas_call x2, Pallas kernels: 2.12 us -> 4.65 us  [weights_of(): pl.pallas_call(functools.partial(weights_kernel, first, count), out_shape...]
    another operation x2, other arithmetic: 0.22 us -> 2.68 us
    pallas_call x2, Pallas kernels: 10.9 us -> 13.4 us  [product_of(): pl.pallas_call(functools.partial(product_kernel, scaled), out_shape=[jax....]
  transfers between devices with their start and end apart: 51 -> 51, of which waited for: 17 -> 18; matrix products, arithmetic and copies ran while one was open for 11% -> 8% of each run, Pallas kernels for 11% -> 21%
where the time goes in v3:
time: 168 us; the launch traced here: 167 us
  starting transfers between devices  56.4 us (34%)
  waiting for transfers between devices  44.6 us (27%)
  Pallas kernels  38.8 us (23%)
  local copies, waits for them, and re-layouts  14 us (8%)
  other arithmetic  10.7 us (6%)
  between operations  2.39 us (1%)
    ppermute x20, starting transfers between devices, along(): return lax.ppermute(value, GRID, moves)  31.8 us
    ppermute x20, waiting for transfers between devices, along(): return lax.ppermute(value, GRID, moves)  15.5 us
    ppermute x6, starting transfers between devices, down(): return lax.ppermute(value, 'x', DOWN)  14.6 us
    pallas_call x2, Pallas kernels, product_of(): pl.pallas_call(functools.partial(product_kernel, scaled), out_shape=[jax....  13.4 us
    pallas_call x2, Pallas kernels, scores_of(): pl.pallas_call(functools.partial(scores_kernel, plan), out_shape=[jax.Sha...  12.1 us
    ppermute x6, waiting for transfers between devices, up(): return lax.ppermute(value, 'x', UP)  9.41 us
    ppermute x6, waiting for transfers between devices, down(): return lax.ppermute(value, 'x', DOWN)  8.74 us
    unnamed x39, local copies, waits for them, and re-layouts  7.4 us
  transfers between devices with their start and end apart: 51, of which 18 were waited for; matrix products, arithmetic and copies ran while one was open for 8% of the time, Pallas kernels for 21%

profile of v3, /device:TPU:0, one launch (start us, length us, event | category | flops | bytes accessed | tf_op | source)
XLA Modules:
  0.0 166.9 jit_solution(10159143389084727877)
XLA Ops:
  12.5 3.2 %collective-permute-done.5 = s32[2,64]{1,0:T(2,128)S(1)} collective-permute-done((s32[2,64]{1,0:T(2,128)S(1)}, s32[2,64]{1,0:T(2,128)S(1)}, u32[]{:S(2)}, u32[]{:S(2)}) %collective-permute-start.5) | collective-permute-done | bytes 544 | tf_op jit(solution)/shard_map/ppermute | solution.py:59
  16.5 2.6 %collective-permute-start.7 = (bf16[2,32,2048]{2,1,0:T(8,128)(2,1)S(1)}, bf16[2,32,2048]{2,1,0:T(8,128)(2,1)S(1)}, u32[]{:S(2)}, u32[]{:S(2)}) collective-permute-start(bf16[2,32,2048]{2,1,0:T(8,128)(2,1)S(1)} %slice.93), channel_id=1, source_target_pairs={{0,96},{1,25},{2,98},{3,27},{4,100},{5,29},{6,102},{7,31},{8,104},... | collective-permute-start | bytes 786440 | tf_op jit(solution)/shard_map/ppermute | solution.py:43
  20.9 3.2 %collective-permute-start.9 = (s32[4,2,64]{2,1,0:T(2,128)S(1)}, s32[4,2,64]{2,1,0:T(2,128)S(1)}, u32[]{:S(2)}, u32[]{:S(2)}) collective-permute-start(s32[4,2,64]{2,1,0:T(2,128)S(1)} %pad_add_fusion.2), channel_id=1, source_target_pairs={{0,96},{1,25},{2,98},{3,27},{4,100},{5,29},{6,102},{7,31},{8,104},... | collective-permute-start | bytes 6152 | tf_op jit(solution)/shard_map/ppermute | solution.py:43
  25.7 3.5 %collective-permute-done.10 = s32[4,2,64]{2,1,0:T(2,128)S(1)} collective-permute-done((s32[4,2,64]{2,1,0:T(2,128)S(1)}, s32[4,2,64]{2,1,0:T(2,128)S(1)}, u32[]{:S(2)}, u32[]{:S(2)}) %collective-permute-start.10) | collective-permute-done | bytes 2080 | tf_op jit(solution)/shard_map/ppermute | solution.py:43
  43.5 2.9 %collective-permute-start.17 = (bf16[2,64,2048]{2,1,0:T(8,128)(2,1)S(1)}, bf16[2,64,2048]{2,1,0:T(8,128)(2,1)}, u32[]{:S(2)}, u32[]{:S(2)}) collective-permute-start(bf16[2,64,2048]{2,1,0:T(8,128)(2,1)S(1)} %pad_maximum_fusion.refs_0_), channel_id=1, source_target_pairs={{0,6},{2,0},{4,2},{6,4},{1,7},{3,1},{5,3},{7,5},{8,14},{10,8},{12,... | collective-permute-start | bytes 1572872 | tf_op jit(solution)/shard_map/ppermute | solution.py:55
  47.2 2.3 %select_reduce_fusion = s32[1024]{0:T(1024)S(1)} fusion(s32[4096]{0:T(1024)S(1)} %broadcast_in_dim.27, s32[1024]{0:T(1024)S(1)} %pad_add_fusion.3), kind=kLoop, calls=%fused_computation | loop fusion | flops 12581888 | bytes 24576 | tf_op jit(solution)/shard_map/reduce_sum | solution.py:451
  50.4 3.1 %collective-permute-done.16.refs_1_ = bf16[2,64,2048]{2,1,0:T(8,128)(2,1)S(1)} collective-permute-done((bf16[2,64,2048]{2,1,0:T(8,128)(2,1)S(1)}, bf16[2,64,2048]{2,1,0:T(8,128)(2,1)S(1)}, u32[]{:S(2)}, u32[]{:S(2)}) %collective-permute-start.16) | collective-permute-done | bytes 524320 | tf_op jit(solution)/shard_map/ppermute | solution.py:51
  56.0 3.2 %collective-permute-start.19 = (bf16[2,32,2048]{2,1,0:T(8,128)(2,1)}, bf16[2,32,2048]{2,1,0:T(8,128)(2,1)}, u32[]{:S(2)}, u32[]{:S(2)}) collective-permute-start(bf16[2,32,2048]{2,1,0:T(8,128)(2,1)} %slice.129), channel_id=1, source_target_pairs={{0,6},{2,0},{4,2},{6,4},{1,7},{3,1},{5,3},{7,5},{8,14},{10,8},{12,... | collective-permute-start | bytes 786440 | tf_op jit(solution)/shard_map/ppermute | solution.py:55
  59.4 2.7 %collective-permute-done.18.refs_3_ = bf16[2,32,2048]{2,1,0:T(8,128)(2,1)S(1)} collective-permute-done((bf16[2,32,2048]{2,1,0:T(8,128)(2,1)}, bf16[2,32,2048]{2,1,0:T(8,128)(2,1)S(1)}, u32[]{:S(2)}, u32[]{:S(2)}) %collective-permute-start.18) | collective-permute-done | bytes 262176 | tf_op jit(solution)/shard_map/ppermute | solution.py:51
  70.3 2.8 %collective-permute-start.26 = (bf16[2,128,2048]{2,1,0:T(8,128)(2,1)S(1)}, bf16[2,128,2048]{2,1,0:T(8,128)(2,1)}, u32[]{:S(2)}, u32[]{:S(2)}) collective-permute-start(bf16[2,128,2048]{2,1,0:T(8,128)(2,1)S(1)} %shard_map.69), channel_id=1, source_target_pairs={{0,24},{1,97},{2,26},{3,99},{4,28},{5,101},{6,30},{7,103},{8,0},{9... | collective-permute-start | bytes 3145736 | tf_op jit(solution)/shard_map/ppermute | solution.py:43
  75.8 7.2 %shard_map.71 = (f32[512,256]{1,0:T(8,128)S(1)}, f32[512,256]{1,0:T(8,128)S(1)}, f32[512,256]{1,0:T(8,128)S(1)}) custom-call(bf16[2,512,2048]{2,1,0:T(8,128)(2,1)S(1)} %shard_map.70.refs_0_, bf16[2,256,2048]{2,1,0:T(8,128)(2,1)S(1)} %shard_map.67.refs_1_.refs_0_, bf16[2,256,2048]{2,1,0:T(8,128)(2,1)} %collective-permute-done.14.refs_0_.refs_2_.refs_1_, ...), custom_call_target="tpu_custom_call" | custom-call | tf_op jit(solution)/shard_map/pallas_call | solution.py:173
  86.1 5.0 %shard_map.72 = (f32[512,128]{1,0:T(8,128)}, f32[512,128]{1,0:T(8,128)}) custom-call(bf16[2,512,2048]{2,1,0:T(8,128)(2,1)} %copy-done, bf16[2,128,2048]{2,1,0:T(8,128)(2,1)} %collective-permute-done.25.refs_1_.refs_3_, bf16[2,128,2048]{2,1,0:T(8,128)(2,1)} %collective-permute-done.26.refs_2_.refs_4_), custom_call_target="tpu_custom_call" | custom-call | tf_op jit(solution)/shard_map/pallas_call | solution.py:173
  93.0 3.9 %shard_map.73.refs_0_ = f32[16,128]{1,0:T(8,128)S(1)} custom-call(s32[1]{0:T(128)} %bitcast.core, f32[1]{0:T(128)} %bitcast.25.amax, f32[512,256]{1,0:T(8,128)S(1)} %get-tuple-element.123.refs_0_, f32[512,256]{1,0:T(8,128)S(1)} %get-tuple-element.124.refs_1_, f32[512,256]{1,0:T(8,128)} %copy-done.4, f32[512,128]{1,0:T(8,128)S(1)} %copy-done.5, ...), custom_call_target="tpu_custom_call" | custom-call | tf_op jit(solution)/shard_map/pallas_call | solution.py:248
  97.3 2.9 %collective-permute-start.33 = (f32[16,128]{1,0:T(8,128)S(1)}, f32[16,128]{1,0:T(8,128)S(1)}, u32[]{:S(2)}, u32[]{:S(2)}) collective-permute-start(f32[16,128]{1,0:T(8,128)S(1)} %shard_map.73.refs_0_), channel_id=1, source_target_pairs={{0,6},{2,0},{4,2},{6,4},{1,7},{3,1},{5,3},{7,5},{8,14},{10,8},{12,... | collective-permute-start | bytes 24584 | tf_op jit(solution)/shard_map/ppermute | solution.py:55
  102.4 3.0 %collective-permute-done.34.refs_3_ = f32[16,128]{1,0:T(8,128)S(1)} collective-permute-done((f32[16,128]{1,0:T(8,128)S(1)}, f32[16,128]{1,0:T(8,128)S(1)}, u32[]{:S(2)}, u32[]{:S(2)}) %collective-permute-start.34) | collective-permute-done | bytes 8224 | tf_op jit(solution)/shard_map/ppermute | solution.py:59
  106.7 3.2 %collective-permute-start.40 = (f32[8,128]{1,0:T(8,128)S(1)}, f32[8,128]{1,0:T(8,128)S(1)}, u32[]{:S(2)}, u32[]{:S(2)}) collective-permute-start(f32[8,128]{1,0:T(8,128)S(1)} %get-tuple-element.140), channel_id=1, source_target_pairs={{0,96},{1,25},{2,98},{3,27},{4,100},{5,29},{6,102},{7,31},{8,104},... | collective-permute-start | bytes 12296 | tf_op jit(solution)/shard_map/ppermute | solution.py:43
  111.5 3.5 %collective-permute-done.41 = f32[8,128]{1,0:T(8,128)S(1)} collective-permute-done((f32[8,128]{1,0:T(8,128)S(1)}, f32[8,128]{1,0:T(8,128)S(1)}, u32[]{:S(2)}, u32[]{:S(2)}) %collective-permute-start.41) | collective-permute-done | bytes 4128 | tf_op jit(solution)/shard_map/ppermute | solution.py:43
  121.1 3.0 %collective-permute-done.44.refs_11_ = f32[32,128]{1,0:T(8,128)S(1)} collective-permute-done((f32[32,128]{1,0:T(8,128)S(1)}, f32[32,128]{1,0:T(8,128)S(1)}, u32[]{:S(2)}, u32[]{:S(2)}) %collective-permute-start.44) | collective-permute-done | bytes 16416 | tf_op jit(solution)/shard_map/ppermute | solution.py:43
  126.9 3.0 %shard_map.77 = (bf16[384,1024]{1,0:T(8,128)(2,1)}, f32[8,128]{1,0:T(8,128)}) custom-call(s32[1]{0:T(128)} %bitcast.core, f32[512,256]{1,0:T(8,128)S(1)} %get-tuple-element.123.refs_0_, f32[512,256]{1,0:T(8,128)S(1)} %copy-done.3, f32[512,256]{1,0:T(8,128)} %copy-done.4, f32[512,128]{1,0:T(8,128)S(1)} %copy-done.6, f32[512,128]{1,0:T(8,128)S(1)} %copy-done.8, ...), custom_call_target="tpu_custom_call" | custom-call | tf_op jit(solution)/shard_map/pallas_call | solution.py:347
  130.5 4.9 %shard_map.76 = f32[128,2048]{1,0:T(8,128)S(1)} custom-call(f32[8,128]{1,0:T(8,128)S(1)} %get-tuple-element.141.bound, bf16[128,1024]{1,0:T(8,128)(2,1)S(1)} %get-tuple-element.142.mine, bf16[128,1024]{1,0:T(8,128)(2,1)S(1)} %collective-permute-done.45.theirs, bf16[2,256,2048]{2,1,0:T(8,128)(2,1)} %copy-done.1, ...), custom_call_target="tpu_custom_call" | custom-call | tf_op jit(solution)/shard_map/pallas_call | solution.py:394
  135.7 3.2 %collective-permute-start.47 = (f16[64,2048]{1,0:T(8,128)(2,1)S(1)}, f16[64,2048]{1,0:T(8,128)(2,1)S(1)}, u32[]{:S(2)}, u32[]{:S(2)}) collective-permute-start(f16[64,2048]{1,0:T(8,128)(2,1)S(1)} %get-tuple-element.169), channel_id=1, source_target_pairs={{0,6},{2,0},{4,2},{6,4},{1,7},{3,1},{5,3},{7,5},{8,14},{10,8},{12,... | collective-permute-start | bytes 786440 | tf_op jit(solution)/shard_map/ppermute | solution.py:55
  138.9 8.5 %shard_map.78 = (f32[128,2048]{1,0:T(8,128)}, f32[128,2048]{1,0:T(8,128)}, f32[128,2048]{1,0:T(8,128)}) custom-call(f32[8,128]{1,0:T(8,128)S(1)} %get-tuple-element.141.bound, bf16[384,1024]{1,0:T(8,128)(2,1)S(1)} %copy-done.11, bf16[384,1024]{1,0:T(8,128)(2,1)S(1)} %collective-permute-done.48.theirs, bf16[2,256,2048]{2,1,0:T(8,128)(2,1)} %copy-done.1, ...), custom_call_target="tpu_custom_call" | custom-call | tf_op jit(solution)/shard_map/pallas_call | solution.py:394
  153.6 8.7 %collective-permute-done.50 = f16[128,2048]{1,0:T(8,128)(2,1)S(1)} collective-permute-done((f16[128,2048]{1,0:T(8,128)(2,1)S(1)}, f16[128,2048]{1,0:T(8,128)(2,1)S(1)}, u32[]{:S(2)}, u32[]{:S(2)}) %collective-permute-start.50) | collective-permute-done | bytes 524320 | tf_op jit(solution)/shard_map/ppermute | solution.py:55
  162.3 2.7 %collective-permute-done.49 = f16[128,2048]{1,0:T(8,128)(2,1)S(1)} collective-permute-done((f16[128,2048]{1,0:T(8,128)(2,1)S(1)}, f16[128,2048]{1,0:T(8,128)(2,1)S(1)}, u32[]{:S(2)}, u32[]{:S(2)}) %collective-permute-start.49) | collective-permute-done | bytes 524320 | tf_op jit(solution)/shard_map/ppermute | solution.py:51
  (193 shorter events, 72.2 us)
Async XLA Ops:
  3.4 12.3 %collective-permute-start.1 = (bf16[2,64,2048]{2,1,0:T(8,128)(2,1)S(1)}, bf16[2,64,2048]{2,1,0:T(8,128)(2,1)S(1)}, u32[]{:S(2)}, u32[]{:S(2)}) collective-permute-start(bf16[2,64,2048]{2,1,0:T(8,128)(2,1)S(1)} %pad_maximum_fusion.refs_0_), channel_id=1, source_target_pairs={{0,32},{1,9},{2,34},{3,11},{4,36},{5,13},{6,38},{7,15},{8,40},{9,1... | collective-permute-start | bytes 1572872 | tf_op jit(solution)/shard_map/ppermute | solution.py:43
  5.1 10.6 %collective-permute-start.2 = (bf16[2,64,2048]{2,1,0:T(8,128)(2,1)S(1)}, bf16[2,64,2048]{2,1,0:T(8,128)(2,1)S(1)}, u32[]{:S(2)}, u32[]{:S(2)}) collective-permute-start(bf16[2,64,2048]{2,1,0:T(8,128)(2,1)S(1)} %pad_maximum_fusion.refs_0_), channel_id=1, source_target_pairs={{0,96},{1,25},{2,98},{3,27},{4,100},{5,29},{6,102},{7,31},{8,104},... | collective-permute-start | bytes 1572872 | tf_op jit(solution)/shard_map/ppermute | solution.py:43
  15.7 13.5 %collective-permute-start.6 = (bf16[2,32,2048]{2,1,0:T(8,128)(2,1)S(1)}, bf16[2,32,2048]{2,1,0:T(8,128)(2,1)S(1)}, u32[]{:S(2)}, u32[]{:S(2)}) collective-permute-start(bf16[2,32,2048]{2,1,0:T(8,128)(2,1)S(1)} %slice.92), channel_id=1, source_target_pairs={{0,32},{1,9},{2,34},{3,11},{4,36},{5,13},{6,38},{7,15},{8,40},{9,1... | collective-permute-start | bytes 786440 | tf_op jit(solution)/shard_map/ppermute | solution.py:43
  16.5 12.7 %collective-permute-start.7 = (bf16[2,32,2048]{2,1,0:T(8,128)(2,1)S(1)}, bf16[2,32,2048]{2,1,0:T(8,128)(2,1)S(1)}, u32[]{:S(2)}, u32[]{:S(2)}) collective-permute-start(bf16[2,32,2048]{2,1,0:T(8,128)(2,1)S(1)} %slice.93), channel_id=1, source_target_pairs={{0,96},{1,25},{2,98},{3,27},{4,100},{5,29},{6,102},{7,31},{8,104},... | collective-permute-start | bytes 786440 | tf_op jit(solution)/shard_map/ppermute | solution.py:43
  29.9 9.9 %collective-permute-start.11 = (s32[4,4,2,64]{3,2,1,0:T(2,128)S(1)}, s32[4,4,2,64]{3,2,1,0:T(2,128)S(1)}, u32[]{:S(2)}, u32[]{:S(2)}) collective-permute-start(s32[4,4,2,64]{3,2,1,0:T(2,128)S(1)} %pad_add_fusion.1), channel_id=1, source_target_pairs={{0,8},{1,33},{2,10},{3,35},{4,12},{5,37},{6,14},{7,39},{8,16},{9,4... | collective-permute-start | bytes 24584 | tf_op jit(solution)/shard_map/ppermute | solution.py:43
  32.0 7.8 %collective-permute-start.12 = (s32[4,4,2,64]{3,2,1,0:T(2,128)S(1)}, s32[4,4,2,64]{3,2,1,0:T(2,128)S(1)}, u32[]{:S(2)}, u32[]{:S(2)}) collective-permute-start(s32[4,4,2,64]{3,2,1,0:T(2,128)S(1)} %pad_add_fusion.1), channel_id=1, source_target_pairs={{0,24},{1,97},{2,26},{3,99},{4,28},{5,101},{6,30},{7,103},{8,0},{9... | collective-permute-start | bytes 24584 | tf_op jit(solution)/shard_map/ppermute | solution.py:43
  39.8 27.4 %collective-permute-start.14 = (bf16[2,256,2048]{2,1,0:T(8,128)(2,1)S(1)}, bf16[2,256,2048]{2,1,0:T(8,128)(2,1)}, u32[]{:S(2)}, u32[]{:S(2)}) collective-permute-start(bf16[2,256,2048]{2,1,0:T(8,128)(2,1)S(1)} %shard_map.67.refs_1_.refs_0_), channel_id=1, source_target_pairs={{0,8},{1,33},{2,10},{3,35},{4,12},{5,37},{6,14},{7,39},{8,16},{9,4... | collective-permute-start | bytes 6291464 | tf_op jit(solution)/shard_map/ppermute | solution.py:43
  40.9 26.3 %collective-permute-start.15 = (bf16[2,256,2048]{2,1,0:T(8,128)(2,1)S(1)}, bf16[2,256,2048]{2,1,0:T(8,128)(2,1)}, u32[]{:S(2)}, u32[]{:S(2)}) collective-permute-start(bf16[2,256,2048]{2,1,0:T(8,128)(2,1)S(1)} %shard_map.67.refs_1_.refs_0_), channel_id=1, source_target_pairs={{0,24},{1,97},{2,26},{3,99},{4,28},{5,101},{6,30},{7,103},{8,0},{9... | collective-permute-start | bytes 6291464 | tf_op jit(solution)/shard_map/ppermute | solution.py:43
  43.2 10.4 %collective-permute-start.16 = (bf16[2,64,2048]{2,1,0:T(8,128)(2,1)S(1)}, bf16[2,64,2048]{2,1,0:T(8,128)(2,1)S(1)}, u32[]{:S(2)}, u32[]{:S(2)}) collective-permute-start(bf16[2,64,2048]{2,1,0:T(8,128)(2,1)S(1)} %pad_maximum_fusion.refs_0_), channel_id=1, source_target_pairs={{0,2},{2,4},{4,6},{6,0},{1,3},{3,5},{5,7},{7,1},{8,10},{10,12},{12... | collective-permute-start | bytes 1572872 | tf_op jit(solution)/shard_map/ppermute | solution.py:51
  43.5 10.9 %collective-permute-start.17 = (bf16[2,64,2048]{2,1,0:T(8,128)(2,1)S(1)}, bf16[2,64,2048]{2,1,0:T(8,128)(2,1)}, u32[]{:S(2)}, u32[]{:S(2)}) collective-permute-start(bf16[2,64,2048]{2,1,0:T(8,128)(2,1)S(1)} %pad_maximum_fusion.refs_0_), channel_id=1, source_target_pairs={{0,6},{2,0},{4,2},{6,4},{1,7},{3,1},{5,3},{7,5},{8,14},{10,8},{12,... | collective-permute-start | bytes 1572872 | tf_op jit(solution)/shard_map/ppermute | solution.py:55
  46.4 16.7 %collective-permute-start.20 = (bf16[2,64,2048]{2,1,0:T(8,128)(2,1)S(1)}, bf16[2,64,2048]{2,1,0:T(8,128)(2,1)}, u32[]{:S(2)}, u32[]{:S(2)}) collective-permute-start(bf16[2,64,2048]{2,1,0:T(8,128)(2,1)S(1)} %pad_maximum_fusion.refs_0_), channel_id=1, source_target_pairs={{0,1},{1,0},{2,3},{3,2},{4,5},{5,4},{6,7},{7,6},{8,9},{9,8},{10,11... | collective-permute-start | bytes 1572872 | tf_op jit(solution)/shard_map/ppermute | solution.py:47
  54.3 7.8 %collective-permute-start.18 = (bf16[2,32,2048]{2,1,0:T(8,128)(2,1)}, bf16[2,32,2048]{2,1,0:T(8,128)(2,1)S(1)}, u32[]{:S(2)}, u32[]{:S(2)}) collective-permute-start(bf16[2,32,2048]{2,1,0:T(8,128)(2,1)} %slice.128), channel_id=1, source_target_pairs={{0,2},{2,4},{4,6},{6,0},{1,3},{3,5},{5,7},{7,1},{8,10},{10,12},{12... | collective-permute-start | bytes 786440 | tf_op jit(solution)/shard_map/ppermute | solution.py:51
  68.5 16.2 %collective-permute-start.25 = (bf16[2,128,2048]{2,1,0:T(8,128)(2,1)S(1)}, bf16[2,128,2048]{2,1,0:T(8,128)(2,1)}, u32[]{:S(2)}, u32[]{:S(2)}) collective-permute-start(bf16[2,128,2048]{2,1,0:T(8,128)(2,1)S(1)} %shard_map.68), channel_id=1, source_target_pairs={{0,8},{1,33},{2,10},{3,35},{4,12},{5,37},{6,14},{7,39},{8,16},{9,4... | collective-permute-start | bytes 3145736 | tf_op jit(solution)/shard_map/ppermute | solution.py:43
  70.3 15.1 %collective-permute-start.26 = (bf16[2,128,2048]{2,1,0:T(8,128)(2,1)S(1)}, bf16[2,128,2048]{2,1,0:T(8,128)(2,1)}, u32[]{:S(2)}, u32[]{:S(2)}) collective-permute-start(bf16[2,128,2048]{2,1,0:T(8,128)(2,1)S(1)} %shard_map.69), channel_id=1, source_target_pairs={{0,24},{1,97},{2,26},{3,99},{4,28},{5,101},{6,30},{7,103},{8,0},{9... | collective-permute-start | bytes 3145736 | tf_op jit(solution)/shard_map/ppermute | solution.py:43
  75.1 21.8 %collective-permute-start.27 = (bf16[2,256,2048]{2,1,0:T(8,128)(2,1)S(1)}, bf16[2,256,2048]{2,1,0:T(8,128)(2,1)}, u32[]{:S(2)}, u32[]{:S(2)}) collective-permute-start(bf16[2,256,2048]{2,1,0:T(8,128)(2,1)S(1)} %shard_map.67.refs_1_.refs_0_), channel_id=1, source_target_pairs={{0,1},{1,0},{2,3},{3,2},{4,5},{5,4},{6,7},{7,6},{8,9},{9,8},{10,11... | collective-permute-start | bytes 6291464 | tf_op jit(solution)/shard_map/ppermute | solution.py:47
  75.2 21.7 %collective-permute-start.28 = (bf16[2,256,2048]{2,1,0:T(8,128)(2,1)}, bf16[2,256,2048]{2,1,0:T(8,128)(2,1)}, u32[]{:S(2)}, u32[]{:S(2)}) collective-permute-start(bf16[2,256,2048]{2,1,0:T(8,128)(2,1)} %collective-permute-done.14.refs_0_.refs_2_.refs_1_), channel_id=1, source_target_pairs={{0,1},{1,0},{2,3},{3,2},{4,5},{5,4},{6,7},{7,6},{8,9},{9,8},{10,11... | collective-permute-start | bytes 6291464 | tf_op jit(solution)/shard_map/ppermute | solution.py:47
  75.7 21.2 %collective-permute-start.29 = (bf16[2,256,2048]{2,1,0:T(8,128)(2,1)}, bf16[2,256,2048]{2,1,0:T(8,128)(2,1)}, u32[]{:S(2)}, u32[]{:S(2)}) collective-permute-start(bf16[2,256,2048]{2,1,0:T(8,128)(2,1)} %collective-permute-done.15.refs_0_.refs_3_.refs_2_), channel_id=1, source_target_pairs={{0,1},{1,0},{2,3},{3,2},{4,5},{5,4},{6,7},{7,6},{8,9},{9,8},{10,11... | collective-permute-start | bytes 6291464 | tf_op jit(solution)/shard_map/ppermute | solution.py:47
  85.4 11.5 %collective-permute-start.30 = (bf16[2,128,2048]{2,1,0:T(8,128)(2,1)}, bf16[2,128,2048]{2,1,0:T(8,128)(2,1)}, u32[]{:S(2)}, u32[]{:S(2)}) collective-permute-start(bf16[2,128,2048]{2,1,0:T(8,128)(2,1)} %collective-permute-done.25.refs_1_.refs_3_), channel_id=1, source_target_pairs={{0,1},{1,0},{2,3},{3,2},{4,5},{5,4},{6,7},{7,6},{8,9},{9,8},{10,11... | collective-permute-start | bytes 3145736 | tf_op jit(solution)/shard_map/ppermute | solution.py:47
  85.4 11.5 %collective-permute-start.31 = (bf16[2,128,2048]{2,1,0:T(8,128)(2,1)}, bf16[2,128,2048]{2,1,0:T(8,128)(2,1)}, u32[]{:S(2)}, u32[]{:S(2)}) collective-permute-start(bf16[2,128,2048]{2,1,0:T(8,128)(2,1)} %collective-permute-done.26.refs_2_.refs_4_), channel_id=1, source_target_pairs={{0,1},{1,0},{2,3},{3,2},{4,5},{5,4},{6,7},{7,6},{8,9},{9,8},{10,11... | collective-permute-start | bytes 3145736 | tf_op jit(solution)/shard_map/ppermute | solution.py:47
  129.9 9.0 %collective-permute-start.48 = (bf16[384,1024]{1,0:T(8,128)(2,1)}, bf16[384,1024]{1,0:T(8,128)(2,1)S(1)}, u32[]{:S(2)}, u32[]{:S(2)}) collective-permute-start(bf16[384,1024]{1,0:T(8,128)(2,1)} %get-tuple-element.154.mine), channel_id=1, source_target_pairs={{0,1},{1,0},{2,3},{3,2},{4,5},{5,4},{6,7},{7,6},{8,9},{9,8},{10,11... | collective-permute-start | bytes 2359304 | tf_op jit(solution)/shard_map/ppermute | solution.py:47
  135.6 11.8 %collective-permute-start.46 = (f16[64,2048]{1,0:T(8,128)(2,1)S(1)}, f16[64,2048]{1,0:T(8,128)(2,1)S(1)}, u32[]{:S(2)}, u32[]{:S(2)}) collective-permute-start(f16[64,2048]{1,0:T(8,128)(2,1)S(1)} %get-tuple-element.170), channel_id=1, source_target_pairs={{0,2},{2,4},{4,6},{6,0},{1,3},{3,5},{5,7},{7,1},{8,10},{10,12},{12... | collective-permute-start | bytes 786440 | tf_op jit(solution)/shard_map/ppermute | solution.py:51
  135.7 11.7 %collective-permute-start.47 = (f16[64,2048]{1,0:T(8,128)(2,1)S(1)}, f16[64,2048]{1,0:T(8,128)(2,1)S(1)}, u32[]{:S(2)}, u32[]{:S(2)}) collective-permute-start(f16[64,2048]{1,0:T(8,128)(2,1)S(1)} %get-tuple-element.169), channel_id=1, source_target_pairs={{0,6},{2,0},{4,2},{6,4},{1,7},{3,1},{5,3},{7,5},{8,14},{10,8},{12,... | collective-permute-start | bytes 786440 | tf_op jit(solution)/shard_map/ppermute | solution.py:55
  148.9 13.4 %collective-permute-start.50 = (f16[128,2048]{1,0:T(8,128)(2,1)S(1)}, f16[128,2048]{1,0:T(8,128)(2,1)S(1)}, u32[]{:S(2)}, u32[]{:S(2)}) collective-permute-start(f16[128,2048]{1,0:T(8,128)(2,1)S(1)} %pad_maximum_fusion.2), channel_id=1, source_target_pairs={{0,6},{2,0},{4,2},{6,4},{1,7},{3,1},{5,3},{7,5},{8,14},{10,8},{12,... | collective-permute-start | bytes 1572872 | tf_op jit(solution)/shard_map/ppermute | solution.py:55
  151.0 14.0 %collective-permute-start.49 = (f16[128,2048]{1,0:T(8,128)(2,1)S(1)}, f16[128,2048]{1,0:T(8,128)(2,1)S(1)}, u32[]{:S(2)}, u32[]{:S(2)}) collective-permute-start(f16[128,2048]{1,0:T(8,128)(2,1)S(1)} %pad_maximum_fusion.1), channel_id=1, source_target_pairs={{0,2},{2,4},{4,6},{6,0},{1,3},{3,5},{5,7},{7,1},{8,10},{10,12},{12... | collective-permute-start | bytes 1572872 | tf_op jit(solution)/shard_map/ppermute | solution.py:51
  (44 other events, 282.0 us)

commit v4 on v3

--- a/solution.py
+++ b/solution.py
@@ -72,9 +72,6 @@
 VMEM = pl.BlockSpec(memory_space=pltpu.VMEM)
 SMEM = pl.BlockSpec(memory_space=pltpu.SMEM)
 HBM = pl.BlockSpec(memory_space=pltpu.HBM)
-GRANT = 52
-
-
 def params(mib):
     return pltpu.CompilerParams(vmem_limit_bytes=mib << 20)
 
@@ -174,7 +171,7 @@
         functools.partial(scores_kernel, plan),
         out_shape=[jax.ShapeDtypeStruct((8 * N, a.shape[1]), jnp.float32) for a in blocks],
         in_specs=[pl.BlockSpec(memory_space=pl.ANY)] * (1 + len(blocks)),
-        out_specs=[HBM] * len(blocks),
+        out_specs=[pl.BlockSpec(memory_space=pl.ANY)] * len(blocks),
         scratch_shapes=[
             pltpu.VMEM((2, 8 * N, wide), jnp.bfloat16),
             pltpu.VMEM((len(plan), 2, 4 * N, wide), jnp.bfloat16),
@@ -195,37 +192,26 @@
     return same_u != same_v, (cross_u != cross_v) | hit, hit
 
 
-def gather_parts(parts, held, sems):
-    copies, at = [], 0
-    for n, (part, size) in enumerate(zip(parts, PARTS)):
-        copies.append(pltpu.make_async_copy(part, held.at[:, pl.ds(at, size)], sems.at[n]))
-        copies[n].start()
-        at += size
-    return copies
-
-
-HELD = [pltpu.VMEM((8 * N, J), jnp.float32), pltpu.SemaphoreType.DMA((len(PARTS),))]
+def scores_at(parts, at, count):
+    return jnp.concatenate([part[pl.ds(at, count), :] for part in parts], axis=1) * SCALE
 
 
 STATS = 16
 
 
 def stats_kernel(core, amax, *refs):
-    parts, (rows, cols, out, keep, held, sems) = refs[:-6], refs[-6:]
-    copies = gather_parts(parts, held, sems)
+    parts, (rows, cols, out, keep) = refs[:-4], refs[-4:]
     step = 32
     inc = core[0] == 1
     keep[...] = jnp.zeros_like(keep)
-    for copy in copies:
-        copy.wait()
 
     @pl.loop(0, 4 * N // step)
     def _(k):
         at = pl.multiple_of(k * step, step)
         keep_s, keep_c, hit = masks(rows, cols, at, step)
         keep_c = keep_c & inc
-        same = held[pl.ds(at, step), :] * SCALE
-        cross = held[pl.ds(pl.multiple_of(at + 4 * N, step), step), :] * SCALE
+        same = scores_at(parts, at, step)
+        cross = scores_at(parts, pl.multiple_of(at + 4 * N, step), step)
         same = jnp.where(keep_s, same, -BIG)
         hits = jnp.sum(jnp.where(hit & inc, cross, 0.0), axis=1, keepdims=True)
         cross = jnp.where(keep_c, cross, -BIG)
@@ -248,10 +234,10 @@
     return pl.pallas_call(
         stats_kernel,
         out_shape=jax.ShapeDtypeStruct((STATS, 128), jnp.float32),
-        in_specs=[SMEM] * 2 + [HBM] * len(parts) + [VMEM] * 2,
+        in_specs=[SMEM] * 2 + [VMEM] * (len(parts) + 2),
         out_specs=VMEM,
-        scratch_shapes=[pltpu.VMEM((12, 128, 128), jnp.float32)] + HELD,
-        compiler_params=params(GRANT),
+        scratch_shapes=[pltpu.VMEM((12, 128, 128), jnp.float32)],
+        compiler_params=params(8),
         cost_estimate=FREE,
     )(core, amax, *parts, rows, cols)
 
@@ -310,8 +296,7 @@
 
 
 def weights_kernel(first, count, core, *refs):
-    parts, (rows, cols, lse_i, *plane, out, bound, col, held, sems) = refs[:len(PARTS)], refs[len(PARTS):]
-    copies = gather_parts(parts, held, sems)
+    parts, (rows, cols, lse_i, *plane, out, bound, col) = refs[:len(PARTS)], refs[len(PARTS):]
     step = 32
     w = core[0]
     for g in range(4):
@@ -324,8 +309,6 @@
     loose = jnp.max(functools.reduce(jnp.maximum, [v[1:2] for v in ends]), axis=1, keepdims=True)
     most = jnp.max(functools.reduce(jnp.maximum, [v[2:3] for v in ends]), axis=1, keepdims=True)
     bound[...] = jnp.broadcast_to(jnp.maximum(loose, 1e-3) * jnp.maximum(most, 1e-20), (8, 128))
-    for copy in copies:
-        copy.wait()
 
     @pl.loop(0, count * N // step)
     def _(k):
@@ -333,8 +316,8 @@
         keep_s, keep_c, hit = masks(rows, cols, at, step)
         li = col[0, pl.ds(at, step), 0:1]
         lc = col[1, pl.ds(at, step), 0:1]
-        same = held[pl.ds(at, step), :] * SCALE
-        cross = held[pl.ds(pl.multiple_of(at + 4 * N, step), step), :] * SCALE
+        same = scores_at(parts, at, step)
+        cross = scores_at(parts, pl.multiple_of(at + 4 * N, step), step)
         m_s = jnp.where(keep_s, jnp.exp(same - li) + jnp.exp(same - lj), 0.0)
         m_c = jnp.where(keep_c, jnp.exp((cross - lc) - cross_j), 0.0) - jnp.where(hit, 1.0, 0.0)
         group = k // (N // step)
@@ -350,10 +333,10 @@
             jax.ShapeDtypeStruct((count * 2 * N, J), jnp.bfloat16),
             jax.ShapeDtypeStruct((8, 128), jnp.float32),
         ],
-        in_specs=[SMEM] + [HBM] * len(parts) + [VMEM] * 7,
+        in_specs=[SMEM] + [VMEM] * (len(parts) + 7),
         out_specs=[VMEM] * 2,
-        scratch_shapes=[pltpu.VMEM((2, 4 * N, 128), jnp.float32)] + HELD,
-        compiler_params=params(GRANT),
+        scratch_shapes=[pltpu.VMEM((2, 4 * N, 128), jnp.float32)],
+        compiler_params=params(8),
         cost_estimate=FREE,
     )(core, *parts, rows, cols, lse_i, *plane)
 
@@ -394,10 +377,10 @@
     return pl.pallas_call(
         functools.partial(product_kernel, scaled),
         out_shape=[jax.ShapeDtypeStruct((2 * N, wide), jnp.float32)] * outs,
-        in_specs=[VMEM] * 3 + [HBM] * (2 * len(PARTS)),
+        in_specs=[VMEM] * 3 + [pl.BlockSpec(memory_space=pl.ANY)] * (2 * len(PARTS)),
         out_specs=[VMEM] * outs,
         scratch_shapes=[pltpu.VMEM((2, J, wide), jnp.bfloat16), pltpu.SemaphoreType.DMA((2 * len(PARTS),))],
-        compiler_params=params(GRANT),
+        compiler_params=params(20),
         cost_estimate=FREE,
     )(bound, mine, theirs, *blocks, *others)
 
@@ -470,7 +453,7 @@
     parts, blocks = held[:3], held[3:]
     blocks += [gl, gr]
 
-    parts += scores_of(56, rows_i, ((0, 1),), gl, gr)
+    parts += scores_of(24, rows_i, ((0, 1),), gl, gr)
     found, *held = settle(stats_of(core, amax.reshape(1), parts, rows, cols), *others, swap(gl), swap(gr), *blocks)
     others, blocks = held[:5], held[5:]
     found = ring(found, line)

time: 168 us -> 160 us (0.952)
  Pallas kernels: 38.8 us -> 30.8 us
  local copies, waits for them, and re-layouts: 14 us -> 17.4 us
  other arithmetic: 10.7 us -> 8.25 us
    unnamed x39 -> x41, local copies, waits for them, and re-layouts: 7.4 us -> 10.9 us
    pallas_call x2, Pallas kernels: 4.65 us -> 2.12 us  [weights_of(): pl.pallas_call(functools.partial(weights_kernel, first, count), out_shape...]
    another operation x2, other arithmetic: 2.68 us -> 0.2 us
    pallas_call x2, Pallas kernels: 13.4 us -> 10.9 us  [product_of(): pl.pallas_call(functools.partial(product_kernel, scaled), out_shape=[jax....]
    ppermute x6, starting transfers between devices: 14.6 us -> 16.7 us  [down(): return lax.ppermute(value, 'x', DOWN)]
    ppermute x20, starting transfers between devices: 31.8 us -> 29.9 us  [along(): return lax.ppermute(value, GRID, moves)]
    pallas_call x2, Pallas kernels: 12.1 us -> 10.3 us  [scores_of(): pl.pallas_call(functools.partial(scores_kernel, plan), out_shape=[jax.Sha...]
  transfers between devices with their start and end apart: 51 -> 51, of which waited for: 18 -> 17; matrix products, arithmetic and copies ran while one was open for 8% -> 7% of each run, Pallas kernels for 21% -> 18%
where the time goes in v4:
time: 160 us
  starting transfers between devices  55.2 us (34%)
  waiting for transfers between devices  45.5 us (28%)
  Pallas kernels  30.8 us (19%)
  local copies, waits for them, and re-layouts  17.4 us (11%)
  other arithmetic  8.25 us (5%)
  between operations  2.39 us (1%)
    ppermute x20, starting transfers between devices, along(): return lax.ppermute(value, GRID, moves)  29.9 us
    ppermute x6, starting transfers between devices, down(): return lax.ppermute(value, 'x', DOWN)  16.7 us
    ppermute x20, waiting for transfers between devices, along(): return lax.ppermute(value, GRID, moves)  15.3 us
    pallas_call x2, Pallas kernels, product_of(): pl.pallas_call(functools.partial(product_kernel, scaled), out_shape=[jax....  10.9 us
    unnamed x41, local copies, waits for them, and re-layouts  10.9 us
    pallas_call x2, Pallas kernels, scores_of(): pl.pallas_call(functools.partial(scores_kernel, plan), out_shape=[jax.Sha...  10.3 us
    ppermute x6, waiting for transfers between devices, up(): return lax.ppermute(value, 'x', UP)  9.91 us
    ppermute x6, waiting for transfers between devices, down(): return lax.ppermute(value, 'x', DOWN)  9.33 us
  transfers between devices with their start and end apart: 51, of which 17 were waited for; matrix products, arithmetic and copies ran while one was open for 7% of the time, Pallas kernels for 18%

profile of v4, /device:TPU:0, one launch (start us, length us, event | category | flops | bytes accessed | tf_op | source)
XLA Modules:
  0.0 159.5 jit_solution(14649633314614960420)
XLA Ops:
  12.5 3.2 %collective-permute-done.5 = s32[2,64]{1,0:T(2,128)S(1)} collective-permute-done((s32[2,64]{1,0:T(2,128)S(1)}, s32[2,64]{1,0:T(2,128)S(1)}, u32[]{:S(2)}, u32[]{:S(2)}) %collective-permute-start.5) | collective-permute-done | bytes 544 | tf_op jit(solution)/shard_map/ppermute | solution.py:59
  17.1 2.8 %collective-permute-start.7 = (bf16[2,32,2048]{2,1,0:T(8,128)(2,1)S(1)}, bf16[2,32,2048]{2,1,0:T(8,128)(2,1)S(1)}, u32[]{:S(2)}, u32[]{:S(2)}) collective-permute-start(bf16[2,32,2048]{2,1,0:T(8,128)(2,1)S(1)} %slice.93), channel_id=1, source_target_pairs={{0,96},{1,25},{2,98},{3,27},{4,100},{5,29},{6,102},{7,31},{8,104},... | collective-permute-start | bytes 786440 | tf_op jit(solution)/shard_map/ppermute | solution.py:43
  21.6 3.2 %collective-permute-start.9 = (s32[4,2,64]{2,1,0:T(2,128)S(1)}, s32[4,2,64]{2,1,0:T(2,128)S(1)}, u32[]{:S(2)}, u32[]{:S(2)}) collective-permute-start(s32[4,2,64]{2,1,0:T(2,128)S(1)} %pad_add_fusion.2), channel_id=1, source_target_pairs={{0,96},{1,25},{2,98},{3,27},{4,100},{5,29},{6,102},{7,31},{8,104},... | collective-permute-start | bytes 6152 | tf_op jit(solution)/shard_map/ppermute | solution.py:43
  26.4 3.5 %collective-permute-done.10 = s32[4,2,64]{2,1,0:T(2,128)S(1)} collective-permute-done((s32[4,2,64]{2,1,0:T(2,128)S(1)}, s32[4,2,64]{2,1,0:T(2,128)S(1)}, u32[]{:S(2)}, u32[]{:S(2)}) %collective-permute-start.10) | collective-permute-done | bytes 2080 | tf_op jit(solution)/shard_map/ppermute | solution.py:43
  44.2 3.0 %collective-permute-start.17 = (bf16[2,64,2048]{2,1,0:T(8,128)(2,1)S(1)}, bf16[2,64,2048]{2,1,0:T(8,128)(2,1)}, u32[]{:S(2)}, u32[]{:S(2)}) collective-permute-start(bf16[2,64,2048]{2,1,0:T(8,128)(2,1)S(1)} %pad_maximum_fusion.refs_0_), channel_id=1, source_target_pairs={{0,6},{2,0},{4,2},{6,4},{1,7},{3,1},{5,3},{7,5},{8,14},{10,8},{12,... | collective-permute-start | bytes 1572872 | tf_op jit(solution)/shard_map/ppermute | solution.py:55
  51.2 3.1 %collective-permute-done.16.refs_1_ = bf16[2,64,2048]{2,1,0:T(8,128)(2,1)S(1)} collective-permute-done((bf16[2,64,2048]{2,1,0:T(8,128)(2,1)S(1)}, bf16[2,64,2048]{2,1,0:T(8,128)(2,1)S(1)}, u32[]{:S(2)}, u32[]{:S(2)}) %collective-permute-start.16) | collective-permute-done | bytes 524320 | tf_op jit(solution)/shard_map/ppermute | solution.py:51
  56.8 3.2 %collective-permute-start.19 = (bf16[2,32,2048]{2,1,0:T(8,128)(2,1)}, bf16[2,32,2048]{2,1,0:T(8,128)(2,1)}, u32[]{:S(2)}, u32[]{:S(2)}) collective-permute-start(bf16[2,32,2048]{2,1,0:T(8,128)(2,1)} %slice.129), channel_id=1, source_target_pairs={{0,6},{2,0},{4,2},{6,4},{1,7},{3,1},{5,3},{7,5},{8,14},{10,8},{12,... | collective-permute-start | bytes 786440 | tf_op jit(solution)/shard_map/ppermute | solution.py:55
  60.1 2.7 %collective-permute-done.18.refs_3_ = bf16[2,32,2048]{2,1,0:T(8,128)(2,1)S(1)} collective-permute-done((bf16[2,32,2048]{2,1,0:T(8,128)(2,1)}, bf16[2,32,2048]{2,1,0:T(8,128)(2,1)S(1)}, u32[]{:S(2)}, u32[]{:S(2)}) %collective-permute-start.18) | collective-permute-done | bytes 262176 | tf_op jit(solution)/shard_map/ppermute | solution.py:51
  71.0 2.8 %collective-permute-start.26 = (bf16[2,128,2048]{2,1,0:T(8,128)(2,1)S(1)}, bf16[2,128,2048]{2,1,0:T(8,128)(2,1)}, u32[]{:S(2)}, u32[]{:S(2)}) collective-permute-start(bf16[2,128,2048]{2,1,0:T(8,128)(2,1)S(1)} %shard_map.69), channel_id=1, source_target_pairs={{0,24},{1,97},{2,26},{3,99},{4,28},{5,101},{6,30},{7,103},{8,0},{9... | collective-permute-start | bytes 3145736 | tf_op jit(solution)/shard_map/ppermute | solution.py:43
  78.6 7.2 %shard_map.71 = (f32[512,256]{1,0:T(8,128)S(1)}, f32[512,256]{1,0:T(8,128)S(1)}, f32[512,256]{1,0:T(8,128)S(1)}) custom-call(bf16[2,512,2048]{2,1,0:T(8,128)(2,1)S(1)} %shard_map.70.refs_0_, bf16[2,256,2048]{2,1,0:T(8,128)(2,1)S(1)} %shard_map.67.refs_1_.refs_0_, bf16[2,256,2048]{2,1,0:T(8,128)(2,1)} %collective-permute-done.14.refs_0_.refs_2_.refs_1_, ...), custom_call_target="tpu_custom_call" | custom-call | tf_op jit(solution)/shard_map/pallas_call | solution.py:170
  91.1 3.1 %shard_map.72 = (f32[512,128]{1,0:T(8,128)S(1)}, f32[512,128]{1,0:T(8,128)S(1)}) custom-call(bf16[2,512,2048]{2,1,0:T(8,128)(2,1)S(1)} %copy-done.1, bf16[2,128,2048]{2,1,0:T(8,128)(2,1)S(1)} %collective-permute-done.25.refs_1_.refs_3_, bf16[2,128,2048]{2,1,0:T(8,128)(2,1)} %collective-permute-done.26.refs_2_.refs_4_), custom_call_target="tpu_custom_call" | custom-call | tf_op jit(solution)/shard_map/pallas_call | solution.py:170
  94.2 2.7 %shard_map.73.refs_0_ = f32[16,128]{1,0:T(8,128)S(1)} custom-call(s32[1]{0:T(128)} %bitcast.core, f32[1]{0:T(128)} %bitcast.25.amax, f32[512,256]{1,0:T(8,128)S(1)} %copy-done.3, f32[512,256]{1,0:T(8,128)S(1)} %copy-done.5, f32[512,256]{1,0:T(8,128)S(1)} %copy-done.7, f32[512,128]{1,0:T(8,128)S(1)} %get-tuple-element.128.refs_3_, ...), custom_call_target="tpu_custom_call" | custom-call | tf_op jit(solution)/shard_map/pallas_call | solution.py:234
  97.3 3.0 %collective-permute-start.33 = (f32[16,128]{1,0:T(8,128)S(1)}, f32[16,128]{1,0:T(8,128)S(1)}, u32[]{:S(2)}, u32[]{:S(2)}) collective-permute-start(f32[16,128]{1,0:T(8,128)S(1)} %shard_map.73.refs_0_), channel_id=1, source_target_pairs={{0,6},{2,0},{4,2},{6,4},{1,7},{3,1},{5,3},{7,5},{8,14},{10,8},{12,... | collective-permute-start | bytes 24584 | tf_op jit(solution)/shard_map/ppermute | solution.py:55
  102.4 3.0 %collective-permute-done.34.refs_3_ = f32[16,128]{1,0:T(8,128)S(1)} collective-permute-done((f32[16,128]{1,0:T(8,128)S(1)}, f32[16,128]{1,0:T(8,128)S(1)}, u32[]{:S(2)}, u32[]{:S(2)}) %collective-permute-start.34) | collective-permute-done | bytes 8224 | tf_op jit(solution)/shard_map/ppermute | solution.py:59
  106.8 3.2 %collective-permute-start.40 = (f32[8,128]{1,0:T(8,128)S(1)}, f32[8,128]{1,0:T(8,128)S(1)}, u32[]{:S(2)}, u32[]{:S(2)}) collective-permute-start(f32[8,128]{1,0:T(8,128)S(1)} %get-tuple-element.140), channel_id=1, source_target_pairs={{0,96},{1,25},{2,98},{3,27},{4,100},{5,29},{6,102},{7,31},{8,104},... | collective-permute-start | bytes 12296 | tf_op jit(solution)/shard_map/ppermute | solution.py:43
  111.6 3.5 %collective-permute-done.41 = f32[8,128]{1,0:T(8,128)S(1)} collective-permute-done((f32[8,128]{1,0:T(8,128)S(1)}, f32[8,128]{1,0:T(8,128)S(1)}, u32[]{:S(2)}, u32[]{:S(2)}) %collective-permute-start.41) | collective-permute-done | bytes 4128 | tf_op jit(solution)/shard_map/ppermute | solution.py:43
  115.1 3.2 %collective-permute-start.43 = (f32[32,128]{1,0:T(8,128)S(1)}, f32[32,128]{1,0:T(8,128)S(1)}, u32[]{:S(2)}, u32[]{:S(2)}) collective-permute-start(f32[32,128]{1,0:T(8,128)S(1)} %constant_dynamic-update-slice_fusion.4.refs_8_), channel_id=1, source_target_pairs={{0,24},{1,97},{2,26},{3,99},{4,28},{5,101},{6,30},{7,103},{8,0},{9... | collective-permute-start | bytes 49160 | tf_op jit(solution)/shard_map/ppermute | solution.py:43
  120.1 3.5 %collective-permute-done.44.refs_11_ = f32[32,128]{1,0:T(8,128)S(1)} collective-permute-done((f32[32,128]{1,0:T(8,128)S(1)}, f32[32,128]{1,0:T(8,128)S(1)}, u32[]{:S(2)}, u32[]{:S(2)}) %collective-permute-start.44) | collective-permute-done | bytes 16416 | tf_op jit(solution)/shard_map/ppermute | solution.py:43
  126.3 4.4 %shard_map.76 = f32[128,2048]{1,0:T(8,128)S(1)} custom-call(f32[8,128]{1,0:T(8,128)S(1)} %get-tuple-element.141.bound, bf16[128,1024]{1,0:T(8,128)(2,1)S(1)} %get-tuple-element.142.mine, bf16[128,1024]{1,0:T(8,128)(2,1)S(1)} %collective-permute-done.45.theirs, bf16[2,256,2048]{2,1,0:T(8,128)(2,1)S(1)} %shard_map.67.refs_1_.refs_0_, ...), custom_call_target="tpu_custom_call" | custom-call | tf_op jit(solution)/shard_map/pallas_call | solution.py:377
  131.0 3.2 %collective-permute-start.47 = (f16[64,2048]{1,0:T(8,128)(2,1)S(1)}, f16[64,2048]{1,0:T(8,128)(2,1)S(1)}, u32[]{:S(2)}, u32[]{:S(2)}) collective-permute-start(f16[64,2048]{1,0:T(8,128)(2,1)S(1)} %get-tuple-element.169), channel_id=1, source_target_pairs={{0,6},{2,0},{4,2},{6,4},{1,7},{3,1},{5,3},{7,5},{8,14},{10,8},{12,... | collective-permute-start | bytes 786440 | tf_op jit(solution)/shard_map/ppermute | solution.py:55
  134.2 6.5 %shard_map.78 = (f32[128,2048]{1,0:T(8,128)S(1)}, f32[128,2048]{1,0:T(8,128)S(1)}, f32[128,2048]{1,0:T(8,128)S(1)}) custom-call(f32[8,128]{1,0:T(8,128)S(1)} %get-tuple-element.141.bound, bf16[384,1024]{1,0:T(8,128)(2,1)S(1)} %get-tuple-element.154.mine, bf16[384,1024]{1,0:T(8,128)(2,1)S(1)} %collective-permute-done.48.theirs, ...), custom_call_target="tpu_custom_call" | custom-call | tf_op jit(solution)/shard_map/pallas_call | solution.py:377
  141.0 2.7 %collective-permute-start.50 = (f16[128,2048]{1,0:T(8,128)(2,1)S(1)}, f16[128,2048]{1,0:T(8,128)(2,1)S(1)}, u32[]{:S(2)}, u32[]{:S(2)}) collective-permute-start(f16[128,2048]{1,0:T(8,128)(2,1)S(1)} %pad_maximum_fusion.2), channel_id=1, source_target_pairs={{0,6},{2,0},{4,2},{6,4},{1,7},{3,1},{5,3},{7,5},{8,14},{10,8},{12,... | collective-permute-start | bytes 1572872 | tf_op jit(solution)/shard_map/ppermute | solution.py:55
  145.0 9.3 %collective-permute-done.50 = f16[128,2048]{1,0:T(8,128)(2,1)S(1)} collective-permute-done((f16[128,2048]{1,0:T(8,128)(2,1)S(1)}, f16[128,2048]{1,0:T(8,128)(2,1)S(1)}, u32[]{:S(2)}, u32[]{:S(2)}) %collective-permute-start.50) | collective-permute-done | bytes 524320 | tf_op jit(solution)/shard_map/ppermute | solution.py:55
  154.4 3.3 %collective-permute-done.49 = f16[128,2048]{1,0:T(8,128)(2,1)S(1)} collective-permute-done((f16[128,2048]{1,0:T(8,128)(2,1)S(1)}, f16[128,2048]{1,0:T(8,128)(2,1)S(1)}, u32[]{:S(2)}, u32[]{:S(2)}) %collective-permute-start.49) | collective-permute-done | bytes 524320 | tf_op jit(solution)/shard_map/ppermute | solution.py:51
  (195 shorter events, 67.7 us)
Async XLA Ops:
  3.4 12.3 %collective-permute-start.1 = (bf16[2,64,2048]{2,1,0:T(8,128)(2,1)S(1)}, bf16[2,64,2048]{2,1,0:T(8,128)(2,1)S(1)}, u32[]{:S(2)}, u32[]{:S(2)}) collective-permute-start(bf16[2,64,2048]{2,1,0:T(8,128)(2,1)S(1)} %pad_maximum_fusion.refs_0_), channel_id=1, source_target_pairs={{0,32},{1,9},{2,34},{3,11},{4,36},{5,13},{6,38},{7,15},{8,40},{9,1... | collective-permute-start | bytes 1572872 | tf_op jit(solution)/shard_map/ppermute | solution.py:43
  5.1 10.6 %collective-permute-start.2 = (bf16[2,64,2048]{2,1,0:T(8,128)(2,1)S(1)}, bf16[2,64,2048]{2,1,0:T(8,128)(2,1)S(1)}, u32[]{:S(2)}, u32[]{:S(2)}) collective-permute-start(bf16[2,64,2048]{2,1,0:T(8,128)(2,1)S(1)} %pad_maximum_fusion.refs_0_), channel_id=1, source_target_pairs={{0,96},{1,25},{2,98},{3,27},{4,100},{5,29},{6,102},{7,31},{8,104},... | collective-permute-start | bytes 1572872 | tf_op jit(solution)/shard_map/ppermute | solution.py:43
  15.7 14.2 %collective-permute-start.6 = (bf16[2,32,2048]{2,1,0:T(8,128)(2,1)S(1)}, bf16[2,32,2048]{2,1,0:T(8,128)(2,1)S(1)}, u32[]{:S(2)}, u32[]{:S(2)}) collective-permute-start(bf16[2,32,2048]{2,1,0:T(8,128)(2,1)S(1)} %slice.92), channel_id=1, source_target_pairs={{0,32},{1,9},{2,34},{3,11},{4,36},{5,13},{6,38},{7,15},{8,40},{9,1... | collective-permute-start | bytes 786440 | tf_op jit(solution)/shard_map/ppermute | solution.py:43
  17.1 12.9 %collective-permute-start.7 = (bf16[2,32,2048]{2,1,0:T(8,128)(2,1)S(1)}, bf16[2,32,2048]{2,1,0:T(8,128)(2,1)S(1)}, u32[]{:S(2)}, u32[]{:S(2)}) collective-permute-start(bf16[2,32,2048]{2,1,0:T(8,128)(2,1)S(1)} %slice.93), channel_id=1, source_target_pairs={{0,96},{1,25},{2,98},{3,27},{4,100},{5,29},{6,102},{7,31},{8,104},... | collective-permute-start | bytes 786440 | tf_op jit(solution)/shard_map/ppermute | solution.py:43
  30.7 9.9 %collective-permute-start.11 = (s32[4,4,2,64]{3,2,1,0:T(2,128)S(1)}, s32[4,4,2,64]{3,2,1,0:T(2,128)S(1)}, u32[]{:S(2)}, u32[]{:S(2)}) collective-permute-start(s32[4,4,2,64]{3,2,1,0:T(2,128)S(1)} %pad_add_fusion.1), channel_id=1, source_target_pairs={{0,8},{1,33},{2,10},{3,35},{4,12},{5,37},{6,14},{7,39},{8,16},{9,4... | collective-permute-start | bytes 24584 | tf_op jit(solution)/shard_map/ppermute | solution.py:43
  32.7 7.8 %collective-permute-start.12 = (s32[4,4,2,64]{3,2,1,0:T(2,128)S(1)}, s32[4,4,2,64]{3,2,1,0:T(2,128)S(1)}, u32[]{:S(2)}, u32[]{:S(2)}) collective-permute-start(s32[4,4,2,64]{3,2,1,0:T(2,128)S(1)} %pad_add_fusion.1), channel_id=1, source_target_pairs={{0,24},{1,97},{2,26},{3,99},{4,28},{5,101},{6,30},{7,103},{8,0},{9... | collective-permute-start | bytes 24584 | tf_op jit(solution)/shard_map/ppermute | solution.py:43
  40.6 27.4 %collective-permute-start.14 = (bf16[2,256,2048]{2,1,0:T(8,128)(2,1)S(1)}, bf16[2,256,2048]{2,1,0:T(8,128)(2,1)}, u32[]{:S(2)}, u32[]{:S(2)}) collective-permute-start(bf16[2,256,2048]{2,1,0:T(8,128)(2,1)S(1)} %shard_map.67.refs_1_.refs_0_), channel_id=1, source_target_pairs={{0,8},{1,33},{2,10},{3,35},{4,12},{5,37},{6,14},{7,39},{8,16},{9,4... | collective-permute-start | bytes 6291464 | tf_op jit(solution)/shard_map/ppermute | solution.py:43
  41.7 26.3 %collective-permute-start.15 = (bf16[2,256,2048]{2,1,0:T(8,128)(2,1)S(1)}, bf16[2,256,2048]{2,1,0:T(8,128)(2,1)}, u32[]{:S(2)}, u32[]{:S(2)}) collective-permute-start(bf16[2,256,2048]{2,1,0:T(8,128)(2,1)S(1)} %shard_map.67.refs_1_.refs_0_), channel_id=1, source_target_pairs={{0,24},{1,97},{2,26},{3,99},{4,28},{5,101},{6,30},{7,103},{8,0},{9... | collective-permute-start | bytes 6291464 | tf_op jit(solution)/shard_map/ppermute | solution.py:43
  43.9 10.4 %collective-permute-start.16 = (bf16[2,64,2048]{2,1,0:T(8,128)(2,1)S(1)}, bf16[2,64,2048]{2,1,0:T(8,128)(2,1)S(1)}, u32[]{:S(2)}, u32[]{:S(2)}) collective-permute-start(bf16[2,64,2048]{2,1,0:T(8,128)(2,1)S(1)} %pad_maximum_fusion.refs_0_), channel_id=1, source_target_pairs={{0,2},{2,4},{4,6},{6,0},{1,3},{3,5},{5,7},{7,1},{8,10},{10,12},{12... | collective-permute-start | bytes 1572872 | tf_op jit(solution)/shard_map/ppermute | solution.py:51
  44.2 11.0 %collective-permute-start.17 = (bf16[2,64,2048]{2,1,0:T(8,128)(2,1)S(1)}, bf16[2,64,2048]{2,1,0:T(8,128)(2,1)}, u32[]{:S(2)}, u32[]{:S(2)}) collective-permute-start(bf16[2,64,2048]{2,1,0:T(8,128)(2,1)S(1)} %pad_maximum_fusion.refs_0_), channel_id=1, source_target_pairs={{0,6},{2,0},{4,2},{6,4},{1,7},{3,1},{5,3},{7,5},{8,14},{10,8},{12,... | collective-permute-start | bytes 1572872 | tf_op jit(solution)/shard_map/ppermute | solution.py:55
  47.1 16.8 %collective-permute-start.20 = (bf16[2,64,2048]{2,1,0:T(8,128)(2,1)S(1)}, bf16[2,64,2048]{2,1,0:T(8,128)(2,1)}, u32[]{:S(2)}, u32[]{:S(2)}) collective-permute-start(bf16[2,64,2048]{2,1,0:T(8,128)(2,1)S(1)} %pad_maximum_fusion.refs_0_), channel_id=1, source_target_pairs={{0,1},{1,0},{2,3},{3,2},{4,5},{5,4},{6,7},{7,6},{8,9},{9,8},{10,11... | collective-permute-start | bytes 1572872 | tf_op jit(solution)/shard_map/ppermute | solution.py:47
  55.0 7.8 %collective-permute-start.18 = (bf16[2,32,2048]{2,1,0:T(8,128)(2,1)}, bf16[2,32,2048]{2,1,0:T(8,128)(2,1)S(1)}, u32[]{:S(2)}, u32[]{:S(2)}) collective-permute-start(bf16[2,32,2048]{2,1,0:T(8,128)(2,1)} %slice.128), channel_id=1, source_target_pairs={{0,2},{2,4},{4,6},{6,0},{1,3},{3,5},{5,7},{7,1},{8,10},{10,12},{12... | collective-permute-start | bytes 786440 | tf_op jit(solution)/shard_map/ppermute | solution.py:51
  69.2 19.0 %collective-permute-start.25 = (bf16[2,128,2048]{2,1,0:T(8,128)(2,1)S(1)}, bf16[2,128,2048]{2,1,0:T(8,128)(2,1)S(1)}, u32[]{:S(2)}, u32[]{:S(2)}) collective-permute-start(bf16[2,128,2048]{2,1,0:T(8,128)(2,1)S(1)} %shard_map.68), channel_id=1, source_target_pairs={{0,8},{1,33},{2,10},{3,35},{4,12},{5,37},{6,14},{7,39},{8,16},{9,4... | collective-permute-start | bytes 3145736 | tf_op jit(solution)/shard_map/ppermute | solution.py:43
  71.0 17.2 %collective-permute-start.26 = (bf16[2,128,2048]{2,1,0:T(8,128)(2,1)S(1)}, bf16[2,128,2048]{2,1,0:T(8,128)(2,1)}, u32[]{:S(2)}, u32[]{:S(2)}) collective-permute-start(bf16[2,128,2048]{2,1,0:T(8,128)(2,1)S(1)} %shard_map.69), channel_id=1, source_target_pairs={{0,24},{1,97},{2,26},{3,99},{4,28},{5,101},{6,30},{7,103},{8,0},{9... | collective-permute-start | bytes 3145736 | tf_op jit(solution)/shard_map/ppermute | solution.py:43
  78.0 19.0 %collective-permute-start.27 = (bf16[2,256,2048]{2,1,0:T(8,128)(2,1)S(1)}, bf16[2,256,2048]{2,1,0:T(8,128)(2,1)}, u32[]{:S(2)}, u32[]{:S(2)}) collective-permute-start(bf16[2,256,2048]{2,1,0:T(8,128)(2,1)S(1)} %shard_map.67.refs_1_.refs_0_), channel_id=1, source_target_pairs={{0,1},{1,0},{2,3},{3,2},{4,5},{5,4},{6,7},{7,6},{8,9},{9,8},{10,11... | collective-permute-start | bytes 6291464 | tf_op jit(solution)/shard_map/ppermute | solution.py:47
  78.1 18.9 %collective-permute-start.28 = (bf16[2,256,2048]{2,1,0:T(8,128)(2,1)}, bf16[2,256,2048]{2,1,0:T(8,128)(2,1)}, u32[]{:S(2)}, u32[]{:S(2)}) collective-permute-start(bf16[2,256,2048]{2,1,0:T(8,128)(2,1)} %collective-permute-done.14.refs_0_.refs_2_.refs_1_), channel_id=1, source_target_pairs={{0,1},{1,0},{2,3},{3,2},{4,5},{5,4},{6,7},{7,6},{8,9},{9,8},{10,11... | collective-permute-start | bytes 6291464 | tf_op jit(solution)/shard_map/ppermute | solution.py:47
  78.6 18.4 %collective-permute-start.29 = (bf16[2,256,2048]{2,1,0:T(8,128)(2,1)}, bf16[2,256,2048]{2,1,0:T(8,128)(2,1)}, u32[]{:S(2)}, u32[]{:S(2)}) collective-permute-start(bf16[2,256,2048]{2,1,0:T(8,128)(2,1)} %collective-permute-done.15.refs_0_.refs_3_.refs_2_), channel_id=1, source_target_pairs={{0,1},{1,0},{2,3},{3,2},{4,5},{5,4},{6,7},{7,6},{8,9},{9,8},{10,11... | collective-permute-start | bytes 6291464 | tf_op jit(solution)/shard_map/ppermute | solution.py:47
  88.2 8.7 %collective-permute-start.30 = (bf16[2,128,2048]{2,1,0:T(8,128)(2,1)S(1)}, bf16[2,128,2048]{2,1,0:T(8,128)(2,1)}, u32[]{:S(2)}, u32[]{:S(2)}) collective-permute-start(bf16[2,128,2048]{2,1,0:T(8,128)(2,1)S(1)} %collective-permute-done.25.refs_1_.refs_3_), channel_id=1, source_target_pairs={{0,1},{1,0},{2,3},{3,2},{4,5},{5,4},{6,7},{7,6},{8,9},{9,8},{10,11... | collective-permute-start | bytes 3145736 | tf_op jit(solution)/shard_map/ppermute | solution.py:47
  88.3 8.6 %collective-permute-start.31 = (bf16[2,128,2048]{2,1,0:T(8,128)(2,1)}, bf16[2,128,2048]{2,1,0:T(8,128)(2,1)}, u32[]{:S(2)}, u32[]{:S(2)}) collective-permute-start(bf16[2,128,2048]{2,1,0:T(8,128)(2,1)} %collective-permute-done.26.refs_2_.refs_4_), channel_id=1, source_target_pairs={{0,1},{1,0},{2,3},{3,2},{4,5},{5,4},{6,7},{7,6},{8,9},{9,8},{10,11... | collective-permute-start | bytes 3145736 | tf_op jit(solution)/shard_map/ppermute | solution.py:47
  125.8 8.4 %collective-permute-start.48 = (bf16[384,1024]{1,0:T(8,128)(2,1)S(1)}, bf16[384,1024]{1,0:T(8,128)(2,1)S(1)}, u32[]{:S(2)}, u32[]{:S(2)}) collective-permute-start(bf16[384,1024]{1,0:T(8,128)(2,1)S(1)} %get-tuple-element.154.mine), channel_id=1, source_target_pairs={{0,1},{1,0},{2,3},{3,2},{4,5},{5,4},{6,7},{7,6},{8,9},{9,8},{10,11... | collective-permute-start | bytes 2359304 | tf_op jit(solution)/shard_map/ppermute | solution.py:47
  130.9 9.8 %collective-permute-start.46 = (f16[64,2048]{1,0:T(8,128)(2,1)S(1)}, f16[64,2048]{1,0:T(8,128)(2,1)S(1)}, u32[]{:S(2)}, u32[]{:S(2)}) collective-permute-start(f16[64,2048]{1,0:T(8,128)(2,1)S(1)} %get-tuple-element.170), channel_id=1, source_target_pairs={{0,2},{2,4},{4,6},{6,0},{1,3},{3,5},{5,7},{7,1},{8,10},{10,12},{12... | collective-permute-start | bytes 786440 | tf_op jit(solution)/shard_map/ppermute | solution.py:51
  131.0 9.7 %collective-permute-start.47 = (f16[64,2048]{1,0:T(8,128)(2,1)S(1)}, f16[64,2048]{1,0:T(8,128)(2,1)S(1)}, u32[]{:S(2)}, u32[]{:S(2)}) collective-permute-start(f16[64,2048]{1,0:T(8,128)(2,1)S(1)} %get-tuple-element.169), channel_id=1, source_target_pairs={{0,6},{2,0},{4,2},{6,4},{1,7},{3,1},{5,3},{7,5},{8,14},{10,8},{12,... | collective-permute-start | bytes 786440 | tf_op jit(solution)/shard_map/ppermute | solution.py:55
  141.0 13.4 %collective-permute-start.50 = (f16[128,2048]{1,0:T(8,128)(2,1)S(1)}, f16[128,2048]{1,0:T(8,128)(2,1)S(1)}, u32[]{:S(2)}, u32[]{:S(2)}) collective-permute-start(f16[128,2048]{1,0:T(8,128)(2,1)S(1)} %pad_maximum_fusion.2), channel_id=1, source_target_pairs={{0,6},{2,0},{4,2},{6,4},{1,7},{3,1},{5,3},{7,5},{8,14},{10,8},{12,... | collective-permute-start | bytes 1572872 | tf_op jit(solution)/shard_map/ppermute | solution.py:55
  143.9 13.7 %collective-permute-start.49 = (f16[128,2048]{1,0:T(8,128)(2,1)S(1)}, f16[128,2048]{1,0:T(8,128)(2,1)S(1)}, u32[]{:S(2)}, u32[]{:S(2)}) collective-permute-start(f16[128,2048]{1,0:T(8,128)(2,1)S(1)} %pad_maximum_fusion.1), channel_id=1, source_target_pairs={{0,2},{2,4},{4,6},{6,0},{1,3},{3,5},{5,7},{7,1},{8,10},{10,12},{12... | collective-permute-start | bytes 1572872 | tf_op jit(solution)/shard_map/ppermute | solution.py:51
  (45 other events, 229.0 us)

commit v5 on v4

--- a/solution.py
+++ b/solution.py
@@ -71,7 +71,6 @@
 
 VMEM = pl.BlockSpec(memory_space=pltpu.VMEM)
 SMEM = pl.BlockSpec(memory_space=pltpu.SMEM)
-HBM = pl.BlockSpec(memory_space=pltpu.HBM)
 def params(mib):
     return pltpu.CompilerParams(vmem_limit_bytes=mib << 20)
 
@@ -132,8 +131,7 @@
 def scores_kernel(plan, *refs):
     blocks = sum(len(group) for group in plan)
     rows, parts, outs = refs[0], refs[1:1 + blocks], refs[1 + blocks:1 + 2 * blocks]
-    left, held, made, row_sems, sems, out_sems = refs[1 + 2 * blocks:]
-    row_copies = [pltpu.make_async_copy(rows.at[h], left.at[h], row_sems.at[h]) for h in (0, 1)]
+    held, made, sems, out_sems = refs[1 + 2 * blocks:]
     copies = []
     for n, group in enumerate(plan):
         at = 0
@@ -142,19 +140,13 @@
             count = parts[k].shape[1]
             copies[n].append(pltpu.make_async_copy(parts[k], held.at[n, :, pl.ds(at, count)], sems.at[k]))
             at += count
-    order = [row_copies[0]] + copies[0] + [row_copies[1]] + [copy for group in copies[1:] for copy in group]
-    for copy in order:
+    for copy in [copy for group in copies for copy in group]:
         copy.start()
     results = []
     for n, group in enumerate(plan):
         for copy in copies[n]:
             copy.wait()
-        if n == 0:
-            row_copies[0].wait()
-        total = inner(left[0], held[n, 0])
-        if n == 0:
-            row_copies[1].wait()
-        made[n] = total + inner(left[1], held[n, 1])
+        made[n] = inner(rows[0], held[n, 0]) + inner(rows[1], held[n, 1])
         at = 0
         for k in group:
             count = parts[k].shape[1]
@@ -170,13 +162,11 @@
     return pl.pallas_call(
         functools.partial(scores_kernel, plan),
         out_shape=[jax.ShapeDtypeStruct((8 * N, a.shape[1]), jnp.float32) for a in blocks],
-        in_specs=[pl.BlockSpec(memory_space=pl.ANY)] * (1 + len(blocks)),
+        in_specs=[VMEM] + [pl.BlockSpec(memory_space=pl.ANY)] * len(blocks),
         out_specs=[pl.BlockSpec(memory_space=pl.ANY)] * len(blocks),
         scratch_shapes=[
-            pltpu.VMEM((2, 8 * N, wide), jnp.bfloat16),
             pltpu.VMEM((len(plan), 2, 4 * N, wide), jnp.bfloat16),
             pltpu.VMEM((len(plan), 8 * N, 4 * N), jnp.float32),
-            pltpu.SemaphoreType.DMA((2,)),
             pltpu.SemaphoreType.DMA((len(blocks),)),
             pltpu.SemaphoreType.DMA((len(blocks),)),
         ],
@@ -447,13 +437,13 @@
     to_r = pack(tuple((0, k * N + H, H) for k in range(4)), dr)
     rows_i = rows_from([after(held[0], to_l, to_r)] + held[1:])
     blocks = [group, dl, dr]
-    parts = scores_of(24, rows_i, ((0,), (1,), (2,)), *blocks)
+    parts = scores_of(14, rows_i, ((0,), (1,), (2,)), *blocks)
     others = [swap(after(a, rows_i)) for a in blocks]
     gl, gr, *held = settle(along(to_l, SECOND[1]), along(to_r, SECOND[3]), *parts, *blocks)
     parts, blocks = held[:3], held[3:]
     blocks += [gl, gr]
 
-    parts += scores_of(24, rows_i, ((0, 1),), gl, gr)
+    parts += scores_of(9, rows_i, ((0, 1),), gl, gr)
     found, *held = settle(stats_of(core, amax.reshape(1), parts, rows, cols), *others, swap(gl), swap(gr), *blocks)
     others, blocks = held[:5], held[5:]
     found = ring(found, line)

time: 160 us -> 160 us (level)
  no operation moved by 1% of the time
where the time goes in v5:
time: 160 us; the launch traced here: 159 us
  starting transfers between devices  55.1 us (34%)
  waiting for transfers between devices  45.5 us (28%)
  Pallas kernels  30.4 us (19%)
  local copies, waits for them, and re-layouts  17.5 us (11%)
  other arithmetic  8.27 us (5%)
  between operations  2.4 us (2%)
    ppermute x20, starting transfers between devices, along(): return lax.ppermute(value, GRID, moves)  29.9 us
    ppermute x6, starting transfers between devices, down(): return lax.ppermute(value, 'x', DOWN)  16.7 us
    ppermute x20, waiting for transfers between devices, along(): return lax.ppermute(value, GRID, moves)  15.3 us
    pallas_call x2, Pallas kernels, product_of(): pl.pallas_call(functools.partial(product_kernel, scaled), out_shape=[jax....  10.9 us
    unnamed x41, local copies, waits for them, and re-layouts  10.9 us
    pallas_call x2, Pallas kernels, scores_of(): pl.pallas_call(functools.partial(scores_kernel, plan), out_shape=[jax.Sha...  9.92 us
    ppermute x6, waiting for transfers between devices, up(): return lax.ppermute(value, 'x', UP)  9.92 us
    ppermute x6, waiting for transfers between devices, down(): return lax.ppermute(value, 'x', DOWN)  9.32 us
  transfers between devices with their start and end apart: 51, of which 17 were waited for; matrix products, arithmetic and copies ran while one was open for 7% of the time, Pallas kernels for 18%

profile of v5, /device:TPU:0, one launch (start us, length us, event | category | flops | bytes accessed | tf_op | source)
XLA Modules:
  0.0 159.2 jit_solution(17812381747629929974)
XLA Ops:
  12.5 3.2 %collective-permute-done.5 = s32[2,64]{1,0:T(2,128)S(1)} collective-permute-done((s32[2,64]{1,0:T(2,128)S(1)}, s32[2,64]{1,0:T(2,128)S(1)}, u32[]{:S(2)}, u32[]{:S(2)}) %collective-permute-start.5) | collective-permute-done | bytes 544 | tf_op jit(solution)/shard_map/ppermute | solution.py:59
  17.1 2.8 %collective-permute-start.7 = (bf16[2,32,2048]{2,1,0:T(8,128)(2,1)S(1)}, bf16[2,32,2048]{2,1,0:T(8,128)(2,1)S(1)}, u32[]{:S(2)}, u32[]{:S(2)}) collective-permute-start(bf16[2,32,2048]{2,1,0:T(8,128)(2,1)S(1)} %slice.93), channel_id=1, source_target_pairs={{0,96},{1,25},{2,98},{3,27},{4,100},{5,29},{6,102},{7,31},{8,104},... | collective-permute-start | bytes 786440 | tf_op jit(solution)/shard_map/ppermute | solution.py:43
  21.6 3.2 %collective-permute-start.9 = (s32[4,2,64]{2,1,0:T(2,128)S(1)}, s32[4,2,64]{2,1,0:T(2,128)S(1)}, u32[]{:S(2)}, u32[]{:S(2)}) collective-permute-start(s32[4,2,64]{2,1,0:T(2,128)S(1)} %pad_add_fusion.2), channel_id=1, source_target_pairs={{0,96},{1,25},{2,98},{3,27},{4,100},{5,29},{6,102},{7,31},{8,104},... | collective-permute-start | bytes 6152 | tf_op jit(solution)/shard_map/ppermute | solution.py:43
  26.4 3.5 %collective-permute-done.10 = s32[4,2,64]{2,1,0:T(2,128)S(1)} collective-permute-done((s32[4,2,64]{2,1,0:T(2,128)S(1)}, s32[4,2,64]{2,1,0:T(2,128)S(1)}, u32[]{:S(2)}, u32[]{:S(2)}) %collective-permute-start.10) | collective-permute-done | bytes 2080 | tf_op jit(solution)/shard_map/ppermute | solution.py:43
  44.2 3.0 %collective-permute-start.17 = (bf16[2,64,2048]{2,1,0:T(8,128)(2,1)S(1)}, bf16[2,64,2048]{2,1,0:T(8,128)(2,1)}, u32[]{:S(2)}, u32[]{:S(2)}) collective-permute-start(bf16[2,64,2048]{2,1,0:T(8,128)(2,1)S(1)} %pad_maximum_fusion.refs_0_), channel_id=1, source_target_pairs={{0,6},{2,0},{4,2},{6,4},{1,7},{3,1},{5,3},{7,5},{8,14},{10,8},{12,... | collective-permute-start | bytes 1572872 | tf_op jit(solution)/shard_map/ppermute | solution.py:55
  51.2 3.1 %collective-permute-done.16.refs_1_ = bf16[2,64,2048]{2,1,0:T(8,128)(2,1)S(1)} collective-permute-done((bf16[2,64,2048]{2,1,0:T(8,128)(2,1)S(1)}, bf16[2,64,2048]{2,1,0:T(8,128)(2,1)S(1)}, u32[]{:S(2)}, u32[]{:S(2)}) %collective-permute-start.16) | collective-permute-done | bytes 524320 | tf_op jit(solution)/shard_map/ppermute | solution.py:51
  56.8 3.2 %collective-permute-start.19 = (bf16[2,32,2048]{2,1,0:T(8,128)(2,1)}, bf16[2,32,2048]{2,1,0:T(8,128)(2,1)}, u32[]{:S(2)}, u32[]{:S(2)}) collective-permute-start(bf16[2,32,2048]{2,1,0:T(8,128)(2,1)} %slice.129), channel_id=1, source_target_pairs={{0,6},{2,0},{4,2},{6,4},{1,7},{3,1},{5,3},{7,5},{8,14},{10,8},{12,... | collective-permute-start | bytes 786440 | tf_op jit(solution)/shard_map/ppermute | solution.py:55
  60.1 2.7 %collective-permute-done.18.refs_3_ = bf16[2,32,2048]{2,1,0:T(8,128)(2,1)S(1)} collective-permute-done((bf16[2,32,2048]{2,1,0:T(8,128)(2,1)}, bf16[2,32,2048]{2,1,0:T(8,128)(2,1)S(1)}, u32[]{:S(2)}, u32[]{:S(2)}) %collective-permute-start.18) | collective-permute-done | bytes 262176 | tf_op jit(solution)/shard_map/ppermute | solution.py:51
  71.0 2.8 %collective-permute-start.26 = (bf16[2,128,2048]{2,1,0:T(8,128)(2,1)S(1)}, bf16[2,128,2048]{2,1,0:T(8,128)(2,1)}, u32[]{:S(2)}, u32[]{:S(2)}) collective-permute-start(bf16[2,128,2048]{2,1,0:T(8,128)(2,1)S(1)} %shard_map.69), channel_id=1, source_target_pairs={{0,24},{1,97},{2,26},{3,99},{4,28},{5,101},{6,30},{7,103},{8,0},{9... | collective-permute-start | bytes 3145736 | tf_op jit(solution)/shard_map/ppermute | solution.py:43
  78.6 7.2 %shard_map.71 = (f32[512,256]{1,0:T(8,128)S(1)}, f32[512,256]{1,0:T(8,128)S(1)}, f32[512,256]{1,0:T(8,128)S(1)}) custom-call(bf16[2,512,2048]{2,1,0:T(8,128)(2,1)S(1)} %shard_map.70.refs_0_, bf16[2,256,2048]{2,1,0:T(8,128)(2,1)S(1)} %shard_map.67.refs_1_.refs_0_, bf16[2,256,2048]{2,1,0:T(8,128)(2,1)} %collective-permute-done.14.refs_0_.refs_2_.refs_1_, ...), custom_call_target="tpu_custom_call" | custom-call | tf_op jit(solution)/shard_map/pallas_call | solution.py:162
  91.1 2.8 %shard_map.72 = (f32[512,128]{1,0:T(8,128)S(1)}, f32[512,128]{1,0:T(8,128)S(1)}) custom-call(bf16[2,512,2048]{2,1,0:T(8,128)(2,1)S(1)} %copy-done.1, bf16[2,128,2048]{2,1,0:T(8,128)(2,1)S(1)} %collective-permute-done.25.refs_1_.refs_3_, bf16[2,128,2048]{2,1,0:T(8,128)(2,1)} %collective-permute-done.26.refs_2_.refs_4_), custom_call_target="tpu_custom_call" | custom-call | tf_op jit(solution)/shard_map/pallas_call | solution.py:162
  93.9 2.7 %shard_map.73.refs_0_ = f32[16,128]{1,0:T(8,128)S(1)} custom-call(s32[1]{0:T(128)} %bitcast.core, f32[1]{0:T(128)} %bitcast.25.amax, f32[512,256]{1,0:T(8,128)S(1)} %copy-done.3, f32[512,256]{1,0:T(8,128)S(1)} %copy-done.5, f32[512,256]{1,0:T(8,128)S(1)} %copy-done.7, f32[512,128]{1,0:T(8,128)S(1)} %get-tuple-element.128.refs_3_, ...), custom_call_target="tpu_custom_call" | custom-call | tf_op jit(solution)/shard_map/pallas_call | solution.py:224
  97.0 3.0 %collective-permute-start.33 = (f32[16,128]{1,0:T(8,128)S(1)}, f32[16,128]{1,0:T(8,128)S(1)}, u32[]{:S(2)}, u32[]{:S(2)}) collective-permute-start(f32[16,128]{1,0:T(8,128)S(1)} %shard_map.73.refs_0_), channel_id=1, source_target_pairs={{0,6},{2,0},{4,2},{6,4},{1,7},{3,1},{5,3},{7,5},{8,14},{10,8},{12,... | collective-permute-start | bytes 24584 | tf_op jit(solution)/shard_map/ppermute | solution.py:55
  102.1 3.0 %collective-permute-done.34.refs_3_ = f32[16,128]{1,0:T(8,128)S(1)} collective-permute-done((f32[16,128]{1,0:T(8,128)S(1)}, f32[16,128]{1,0:T(8,128)S(1)}, u32[]{:S(2)}, u32[]{:S(2)}) %collective-permute-start.34) | collective-permute-done | bytes 8224 | tf_op jit(solution)/shard_map/ppermute | solution.py:59
  106.4 3.2 %collective-permute-start.40 = (f32[8,128]{1,0:T(8,128)S(1)}, f32[8,128]{1,0:T(8,128)S(1)}, u32[]{:S(2)}, u32[]{:S(2)}) collective-permute-start(f32[8,128]{1,0:T(8,128)S(1)} %get-tuple-element.140), channel_id=1, source_target_pairs={{0,96},{1,25},{2,98},{3,27},{4,100},{5,29},{6,102},{7,31},{8,104},... | collective-permute-start | bytes 12296 | tf_op jit(solution)/shard_map/ppermute | solution.py:43
  111.2 3.5 %collective-permute-done.41 = f32[8,128]{1,0:T(8,128)S(1)} collective-permute-done((f32[8,128]{1,0:T(8,128)S(1)}, f32[8,128]{1,0:T(8,128)S(1)}, u32[]{:S(2)}, u32[]{:S(2)}) %collective-permute-start.41) | collective-permute-done | bytes 4128 | tf_op jit(solution)/shard_map/ppermute | solution.py:43
  114.8 3.2 %collective-permute-start.43 = (f32[32,128]{1,0:T(8,128)S(1)}, f32[32,128]{1,0:T(8,128)S(1)}, u32[]{:S(2)}, u32[]{:S(2)}) collective-permute-start(f32[32,128]{1,0:T(8,128)S(1)} %constant_dynamic-update-slice_fusion.4.refs_8_), channel_id=1, source_target_pairs={{0,24},{1,97},{2,26},{3,99},{4,28},{5,101},{6,30},{7,103},{8,0},{9... | collective-permute-start | bytes 49160 | tf_op jit(solution)/shard_map/ppermute | solution.py:43
  119.7 3.5 %collective-permute-done.44.refs_11_ = f32[32,128]{1,0:T(8,128)S(1)} collective-permute-done((f32[32,128]{1,0:T(8,128)S(1)}, f32[32,128]{1,0:T(8,128)S(1)}, u32[]{:S(2)}, u32[]{:S(2)}) %collective-permute-start.44) | collective-permute-done | bytes 16416 | tf_op jit(solution)/shard_map/ppermute | solution.py:43
  126.0 4.4 %shard_map.76 = f32[128,2048]{1,0:T(8,128)S(1)} custom-call(f32[8,128]{1,0:T(8,128)S(1)} %get-tuple-element.141.bound, bf16[128,1024]{1,0:T(8,128)(2,1)S(1)} %get-tuple-element.142.mine, bf16[128,1024]{1,0:T(8,128)(2,1)S(1)} %collective-permute-done.45.theirs, bf16[2,256,2048]{2,1,0:T(8,128)(2,1)S(1)} %shard_map.67.refs_1_.refs_0_, ...), custom_call_target="tpu_custom_call" | custom-call | tf_op jit(solution)/shard_map/pallas_call | solution.py:367
  130.7 3.2 %collective-permute-start.47 = (f16[64,2048]{1,0:T(8,128)(2,1)S(1)}, f16[64,2048]{1,0:T(8,128)(2,1)S(1)}, u32[]{:S(2)}, u32[]{:S(2)}) collective-permute-start(f16[64,2048]{1,0:T(8,128)(2,1)S(1)} %get-tuple-element.169), channel_id=1, source_target_pairs={{0,6},{2,0},{4,2},{6,4},{1,7},{3,1},{5,3},{7,5},{8,14},{10,8},{12,... | collective-permute-start | bytes 786440 | tf_op jit(solution)/shard_map/ppermute | solution.py:55
  133.9 6.5 %shard_map.78 = (f32[128,2048]{1,0:T(8,128)S(1)}, f32[128,2048]{1,0:T(8,128)S(1)}, f32[128,2048]{1,0:T(8,128)S(1)}) custom-call(f32[8,128]{1,0:T(8,128)S(1)} %get-tuple-element.141.bound, bf16[384,1024]{1,0:T(8,128)(2,1)S(1)} %get-tuple-element.154.mine, bf16[384,1024]{1,0:T(8,128)(2,1)S(1)} %collective-permute-done.48.theirs, ...), custom_call_target="tpu_custom_call" | custom-call | tf_op jit(solution)/shard_map/pallas_call | solution.py:367
  140.7 2.7 %collective-permute-start.50 = (f16[128,2048]{1,0:T(8,128)(2,1)S(1)}, f16[128,2048]{1,0:T(8,128)(2,1)S(1)}, u32[]{:S(2)}, u32[]{:S(2)}) collective-permute-start(f16[128,2048]{1,0:T(8,128)(2,1)S(1)} %pad_maximum_fusion.2), channel_id=1, source_target_pairs={{0,6},{2,0},{4,2},{6,4},{1,7},{3,1},{5,3},{7,5},{8,14},{10,8},{12,... | collective-permute-start | bytes 1572872 | tf_op jit(solution)/shard_map/ppermute | solution.py:55
  144.7 9.3 %collective-permute-done.50 = f16[128,2048]{1,0:T(8,128)(2,1)S(1)} collective-permute-done((f16[128,2048]{1,0:T(8,128)(2,1)S(1)}, f16[128,2048]{1,0:T(8,128)(2,1)S(1)}, u32[]{:S(2)}, u32[]{:S(2)}) %collective-permute-start.50) | collective-permute-done | bytes 524320 | tf_op jit(solution)/shard_map/ppermute | solution.py:55
  154.0 3.3 %collective-permute-done.49 = f16[128,2048]{1,0:T(8,128)(2,1)S(1)} collective-permute-done((f16[128,2048]{1,0:T(8,128)(2,1)S(1)}, f16[128,2048]{1,0:T(8,128)(2,1)S(1)}, u32[]{:S(2)}, u32[]{:S(2)}) %collective-permute-start.49) | collective-permute-done | bytes 524320 | tf_op jit(solution)/shard_map/ppermute | solution.py:51
  (195 shorter events, 67.7 us)
Async XLA Ops:
  3.4 12.3 %collective-permute-start.1 = (bf16[2,64,2048]{2,1,0:T(8,128)(2,1)S(1)}, bf16[2,64,2048]{2,1,0:T(8,128)(2,1)S(1)}, u32[]{:S(2)}, u32[]{:S(2)}) collective-permute-start(bf16[2,64,2048]{2,1,0:T(8,128)(2,1)S(1)} %pad_maximum_fusion.refs_0_), channel_id=1, source_target_pairs={{0,32},{1,9},{2,34},{3,11},{4,36},{5,13},{6,38},{7,15},{8,40},{9,1... | collective-permute-start | bytes 1572872 | tf_op jit(solution)/shard_map/ppermute | solution.py:43
  5.1 10.6 %collective-permute-start.2 = (bf16[2,64,2048]{2,1,0:T(8,128)(2,1)S(1)}, bf16[2,64,2048]{2,1,0:T(8,128)(2,1)S(1)}, u32[]{:S(2)}, u32[]{:S(2)}) collective-permute-start(bf16[2,64,2048]{2,1,0:T(8,128)(2,1)S(1)} %pad_maximum_fusion.refs_0_), channel_id=1, source_target_pairs={{0,96},{1,25},{2,98},{3,27},{4,100},{5,29},{6,102},{7,31},{8,104},... | collective-permute-start | bytes 1572872 | tf_op jit(solution)/shard_map/ppermute | solution.py:43
  15.7 14.2 %collective-permute-start.6 = (bf16[2,32,2048]{2,1,0:T(8,128)(2,1)S(1)}, bf16[2,32,2048]{2,1,0:T(8,128)(2,1)S(1)}, u32[]{:S(2)}, u32[]{:S(2)}) collective-permute-start(bf16[2,32,2048]{2,1,0:T(8,128)(2,1)S(1)} %slice.92), channel_id=1, source_target_pairs={{0,32},{1,9},{2,34},{3,11},{4,36},{5,13},{6,38},{7,15},{8,40},{9,1... | collective-permute-start | bytes 786440 | tf_op jit(solution)/shard_map/ppermute | solution.py:43
  17.1 12.9 %collective-permute-start.7 = (bf16[2,32,2048]{2,1,0:T(8,128)(2,1)S(1)}, bf16[2,32,2048]{2,1,0:T(8,128)(2,1)S(1)}, u32[]{:S(2)}, u32[]{:S(2)}) collective-permute-start(bf16[2,32,2048]{2,1,0:T(8,128)(2,1)S(1)} %slice.93), channel_id=1, source_target_pairs={{0,96},{1,25},{2,98},{3,27},{4,100},{5,29},{6,102},{7,31},{8,104},... | collective-permute-start | bytes 786440 | tf_op jit(solution)/shard_map/ppermute | solution.py:43
  30.7 9.9 %collective-permute-start.11 = (s32[4,4,2,64]{3,2,1,0:T(2,128)S(1)}, s32[4,4,2,64]{3,2,1,0:T(2,128)S(1)}, u32[]{:S(2)}, u32[]{:S(2)}) collective-permute-start(s32[4,4,2,64]{3,2,1,0:T(2,128)S(1)} %pad_add_fusion.1), channel_id=1, source_target_pairs={{0,8},{1,33},{2,10},{3,35},{4,12},{5,37},{6,14},{7,39},{8,16},{9,4... | collective-permute-start | bytes 24584 | tf_op jit(solution)/shard_map/ppermute | solution.py:43
  32.7 7.8 %collective-permute-start.12 = (s32[4,4,2,64]{3,2,1,0:T(2,128)S(1)}, s32[4,4,2,64]{3,2,1,0:T(2,128)S(1)}, u32[]{:S(2)}, u32[]{:S(2)}) collective-permute-start(s32[4,4,2,64]{3,2,1,0:T(2,128)S(1)} %pad_add_fusion.1), channel_id=1, source_target_pairs={{0,24},{1,97},{2,26},{3,99},{4,28},{5,101},{6,30},{7,103},{8,0},{9... | collective-permute-start | bytes 24584 | tf_op jit(solution)/shard_map/ppermute | solution.py:43
  40.6 27.4 %collective-permute-start.14 = (bf16[2,256,2048]{2,1,0:T(8,128)(2,1)S(1)}, bf16[2,256,2048]{2,1,0:T(8,128)(2,1)}, u32[]{:S(2)}, u32[]{:S(2)}) collective-permute-start(bf16[2,256,2048]{2,1,0:T(8,128)(2,1)S(1)} %shard_map.67.refs_1_.refs_0_), channel_id=1, source_target_pairs={{0,8},{1,33},{2,10},{3,35},{4,12},{5,37},{6,14},{7,39},{8,16},{9,4... | collective-permute-start | bytes 6291464 | tf_op jit(solution)/shard_map/ppermute | solution.py:43
  41.7 26.3 %collective-permute-start.15 = (bf16[2,256,2048]{2,1,0:T(8,128)(2,1)S(1)}, bf16[2,256,2048]{2,1,0:T(8,128)(2,1)}, u32[]{:S(2)}, u32[]{:S(2)}) collective-permute-start(bf16[2,256,2048]{2,1,0:T(8,128)(2,1)S(1)} %shard_map.67.refs_1_.refs_0_), channel_id=1, source_target_pairs={{0,24},{1,97},{2,26},{3,99},{4,28},{5,101},{6,30},{7,103},{8,0},{9... | collective-permute-start | bytes 6291464 | tf_op jit(solution)/shard_map/ppermute | solution.py:43
  43.9 10.4 %collective-permute-start.16 = (bf16[2,64,2048]{2,1,0:T(8,128)(2,1)S(1)}, bf16[2,64,2048]{2,1,0:T(8,128)(2,1)S(1)}, u32[]{:S(2)}, u32[]{:S(2)}) collective-permute-start(bf16[2,64,2048]{2,1,0:T(8,128)(2,1)S(1)} %pad_maximum_fusion.refs_0_), channel_id=1, source_target_pairs={{0,2},{2,4},{4,6},{6,0},{1,3},{3,5},{5,7},{7,1},{8,10},{10,12},{12... | collective-permute-start | bytes 1572872 | tf_op jit(solution)/shard_map/ppermute | solution.py:51
  44.2 11.0 %collective-permute-start.17 = (bf16[2,64,2048]{2,1,0:T(8,128)(2,1)S(1)}, bf16[2,64,2048]{2,1,0:T(8,128)(2,1)}, u32[]{:S(2)}, u32[]{:S(2)}) collective-permute-start(bf16[2,64,2048]{2,1,0:T(8,128)(2,1)S(1)} %pad_maximum_fusion.refs_0_), channel_id=1, source_target_pairs={{0,6},{2,0},{4,2},{6,4},{1,7},{3,1},{5,3},{7,5},{8,14},{10,8},{12,... | collective-permute-start | bytes 1572872 | tf_op jit(solution)/shard_map/ppermute | solution.py:55
  47.1 16.8 %collective-permute-start.20 = (bf16[2,64,2048]{2,1,0:T(8,128)(2,1)S(1)}, bf16[2,64,2048]{2,1,0:T(8,128)(2,1)}, u32[]{:S(2)}, u32[]{:S(2)}) collective-permute-start(bf16[2,64,2048]{2,1,0:T(8,128)(2,1)S(1)} %pad_maximum_fusion.refs_0_), channel_id=1, source_target_pairs={{0,1},{1,0},{2,3},{3,2},{4,5},{5,4},{6,7},{7,6},{8,9},{9,8},{10,11... | collective-permute-start | bytes 1572872 | tf_op jit(solution)/shard_map/ppermute | solution.py:47
  55.0 7.8 %collective-permute-start.18 = (bf16[2,32,2048]{2,1,0:T(8,128)(2,1)}, bf16[2,32,2048]{2,1,0:T(8,128)(2,1)S(1)}, u32[]{:S(2)}, u32[]{:S(2)}) collective-permute-start(bf16[2,32,2048]{2,1,0:T(8,128)(2,1)} %slice.128), channel_id=1, source_target_pairs={{0,2},{2,4},{4,6},{6,0},{1,3},{3,5},{5,7},{7,1},{8,10},{10,12},{12... | collective-permute-start | bytes 786440 | tf_op jit(solution)/shard_map/ppermute | solution.py:51
  69.2 19.0 %collective-permute-start.25 = (bf16[2,128,2048]{2,1,0:T(8,128)(2,1)S(1)}, bf16[2,128,2048]{2,1,0:T(8,128)(2,1)S(1)}, u32[]{:S(2)}, u32[]{:S(2)}) collective-permute-start(bf16[2,128,2048]{2,1,0:T(8,128)(2,1)S(1)} %shard_map.68), channel_id=1, source_target_pairs={{0,8},{1,33},{2,10},{3,35},{4,12},{5,37},{6,14},{7,39},{8,16},{9,4... | collective-permute-start | bytes 3145736 | tf_op jit(solution)/shard_map/ppermute | solution.py:43
  71.0 17.2 %collective-permute-start.26 = (bf16[2,128,2048]{2,1,0:T(8,128)(2,1)S(1)}, bf16[2,128,2048]{2,1,0:T(8,128)(2,1)}, u32[]{:S(2)}, u32[]{:S(2)}) collective-permute-start(bf16[2,128,2048]{2,1,0:T(8,128)(2,1)S(1)} %shard_map.69), channel_id=1, source_target_pairs={{0,24},{1,97},{2,26},{3,99},{4,28},{5,101},{6,30},{7,103},{8,0},{9... | collective-permute-start | bytes 3145736 | tf_op jit(solution)/shard_map/ppermute | solution.py:43
  78.0 18.6 %collective-permute-start.27 = (bf16[2,256,2048]{2,1,0:T(8,128)(2,1)S(1)}, bf16[2,256,2048]{2,1,0:T(8,128)(2,1)}, u32[]{:S(2)}, u32[]{:S(2)}) collective-permute-start(bf16[2,256,2048]{2,1,0:T(8,128)(2,1)S(1)} %shard_map.67.refs_1_.refs_0_), channel_id=1, source_target_pairs={{0,1},{1,0},{2,3},{3,2},{4,5},{5,4},{6,7},{7,6},{8,9},{9,8},{10,11... | collective-permute-start | bytes 6291464 | tf_op jit(solution)/shard_map/ppermute | solution.py:47
  78.1 18.5 %collective-permute-start.28 = (bf16[2,256,2048]{2,1,0:T(8,128)(2,1)}, bf16[2,256,2048]{2,1,0:T(8,128)(2,1)}, u32[]{:S(2)}, u32[]{:S(2)}) collective-permute-start(bf16[2,256,2048]{2,1,0:T(8,128)(2,1)} %collective-permute-done.14.refs_0_.refs_2_.refs_1_), channel_id=1, source_target_pairs={{0,1},{1,0},{2,3},{3,2},{4,5},{5,4},{6,7},{7,6},{8,9},{9,8},{10,11... | collective-permute-start | bytes 6291464 | tf_op jit(solution)/shard_map/ppermute | solution.py:47
  78.6 18.0 %collective-permute-start.29 = (bf16[2,256,2048]{2,1,0:T(8,128)(2,1)}, bf16[2,256,2048]{2,1,0:T(8,128)(2,1)}, u32[]{:S(2)}, u32[]{:S(2)}) collective-permute-start(bf16[2,256,2048]{2,1,0:T(8,128)(2,1)} %collective-permute-done.15.refs_0_.refs_3_.refs_2_), channel_id=1, source_target_pairs={{0,1},{1,0},{2,3},{3,2},{4,5},{5,4},{6,7},{7,6},{8,9},{9,8},{10,11... | collective-permute-start | bytes 6291464 | tf_op jit(solution)/shard_map/ppermute | solution.py:47
  88.2 8.4 %collective-permute-start.30 = (bf16[2,128,2048]{2,1,0:T(8,128)(2,1)S(1)}, bf16[2,128,2048]{2,1,0:T(8,128)(2,1)}, u32[]{:S(2)}, u32[]{:S(2)}) collective-permute-start(bf16[2,128,2048]{2,1,0:T(8,128)(2,1)S(1)} %collective-permute-done.25.refs_1_.refs_3_), channel_id=1, source_target_pairs={{0,1},{1,0},{2,3},{3,2},{4,5},{5,4},{6,7},{7,6},{8,9},{9,8},{10,11... | collective-permute-start | bytes 3145736 | tf_op jit(solution)/shard_map/ppermute | solution.py:47
  88.2 8.4 %collective-permute-start.31 = (bf16[2,128,2048]{2,1,0:T(8,128)(2,1)}, bf16[2,128,2048]{2,1,0:T(8,128)(2,1)}, u32[]{:S(2)}, u32[]{:S(2)}) collective-permute-start(bf16[2,128,2048]{2,1,0:T(8,128)(2,1)} %collective-permute-done.26.refs_2_.refs_4_), channel_id=1, source_target_pairs={{0,1},{1,0},{2,3},{3,2},{4,5},{5,4},{6,7},{7,6},{8,9},{9,8},{10,11... | collective-permute-start | bytes 3145736 | tf_op jit(solution)/shard_map/ppermute | solution.py:47
  125.5 8.4 %collective-permute-start.48 = (bf16[384,1024]{1,0:T(8,128)(2,1)S(1)}, bf16[384,1024]{1,0:T(8,128)(2,1)S(1)}, u32[]{:S(2)}, u32[]{:S(2)}) collective-permute-start(bf16[384,1024]{1,0:T(8,128)(2,1)S(1)} %get-tuple-element.154.mine), channel_id=1, source_target_pairs={{0,1},{1,0},{2,3},{3,2},{4,5},{5,4},{6,7},{7,6},{8,9},{9,8},{10,11... | collective-permute-start | bytes 2359304 | tf_op jit(solution)/shard_map/ppermute | solution.py:47
  130.6 9.8 %collective-permute-start.46 = (f16[64,2048]{1,0:T(8,128)(2,1)S(1)}, f16[64,2048]{1,0:T(8,128)(2,1)S(1)}, u32[]{:S(2)}, u32[]{:S(2)}) collective-permute-start(f16[64,2048]{1,0:T(8,128)(2,1)S(1)} %get-tuple-element.170), channel_id=1, source_target_pairs={{0,2},{2,4},{4,6},{6,0},{1,3},{3,5},{5,7},{7,1},{8,10},{10,12},{12... | collective-permute-start | bytes 786440 | tf_op jit(solution)/shard_map/ppermute | solution.py:51
  130.7 9.8 %collective-permute-start.47 = (f16[64,2048]{1,0:T(8,128)(2,1)S(1)}, f16[64,2048]{1,0:T(8,128)(2,1)S(1)}, u32[]{:S(2)}, u32[]{:S(2)}) collective-permute-start(f16[64,2048]{1,0:T(8,128)(2,1)S(1)} %get-tuple-element.169), channel_id=1, source_target_pairs={{0,6},{2,0},{4,2},{6,4},{1,7},{3,1},{5,3},{7,5},{8,14},{10,8},{12,... | collective-permute-start | bytes 786440 | tf_op jit(solution)/shard_map/ppermute | solution.py:55
  140.7 13.3 %collective-permute-start.50 = (f16[128,2048]{1,0:T(8,128)(2,1)S(1)}, f16[128,2048]{1,0:T(8,128)(2,1)S(1)}, u32[]{:S(2)}, u32[]{:S(2)}) collective-permute-start(f16[128,2048]{1,0:T(8,128)(2,1)S(1)} %pad_maximum_fusion.2), channel_id=1, source_target_pairs={{0,6},{2,0},{4,2},{6,4},{1,7},{3,1},{5,3},{7,5},{8,14},{10,8},{12,... | collective-permute-start | bytes 1572872 | tf_op jit(solution)/shard_map/ppermute | solution.py:55
  143.6 13.7 %collective-permute-start.49 = (f16[128,2048]{1,0:T(8,128)(2,1)S(1)}, f16[128,2048]{1,0:T(8,128)(2,1)S(1)}, u32[]{:S(2)}, u32[]{:S(2)}) collective-permute-start(f16[128,2048]{1,0:T(8,128)(2,1)S(1)} %pad_maximum_fusion.1), channel_id=1, source_target_pairs={{0,2},{2,4},{4,6},{6,0},{1,3},{3,5},{5,7},{7,1},{8,10},{10,12},{12... | collective-permute-start | bytes 1572872 | tf_op jit(solution)/shard_map/ppermute | solution.py:51
  (45 other events, 227.9 us)

commit v6 on v5

--- a/solution.py
+++ b/solution.py
@@ -101,6 +101,26 @@
         in_specs=[pl.BlockSpec(memory_space=pl.ANY)] * len(pieces),
         out_specs=VMEM,
         scratch_shapes=[pltpu.SemaphoreType.DMA((len(plan),))],
+        compiler_params=params(8),
+        cost_estimate=FREE,
+    )(*pieces)
+
+
+def place_kernel(plan, *refs):
+    pieces, out = refs[:-1], refs[-1]
+    at = 0
+    for k, start, count in plan:
+        out[:, at:at + count, :] = pieces[k][:, start:start + count, :]
+        at += count
+
+
+def place(plan, *pieces):
+    rows, wide = sum(count for _, _, count in plan), pieces[0].shape[2]
+    return pl.pallas_call(
+        functools.partial(place_kernel, plan),
+        out_shape=jax.ShapeDtypeStruct((2, rows, wide), jnp.bfloat16),
+        in_specs=[VMEM] * len(pieces),
+        out_specs=VMEM,
         compiler_params=params(8),
         cost_estimate=FREE,
     )(*pieces)
@@ -405,7 +425,7 @@
     f_low, f_high, own, fl, fr, *ints = settle(
         along(low(fl)[0], FIRST[1]), along(high(fr)[0], FIRST[3]), own, fl, fr, *ring(jnp.stack(ints), by_first)
     )
-    group = pack(((0, 0, N), (1, 0, N), (2, 0, N), (3, 0, H), (4, 0, H)), own, fl, fr, f_low, f_high)
+    group = place(((0, 0, N), (1, 0, N), (2, 0, N), (3, 0, H), (4, 0, H)), own, fl, fr, f_low, f_high)
     group, own, *ints = settle(group, own, *ring(jnp.stack(ints), by_second))
     ints = jnp.stack(ints)
     ids = ints[..., 0, :]

time: 160 us -> 160 us (level)
  no operation moved by 1% of the time
where the time goes in v6:
time: 160 us; the launch traced here: 159 us
  starting transfers between devices  55.1 us (34%)
  waiting for transfers between devices  45.5 us (28%)
  Pallas kernels  30.4 us (19%)
  local copies, waits for them, and re-layouts  17.5 us (11%)
  other arithmetic  8.27 us (5%)
  between operations  2.39 us (1%)
    ppermute x20, starting transfers between devices, along(): return lax.ppermute(value, GRID, moves)  29.9 us
    ppermute x6, starting transfers between devices, down(): return lax.ppermute(value, 'x', DOWN)  16.7 us
    ppermute x20, waiting for transfers between devices, along(): return lax.ppermute(value, GRID, moves)  15.3 us
    pallas_call x2, Pallas kernels, product_of(): pl.pallas_call(functools.partial(product_kernel, scaled), out_shape=[jax....  11 us
    unnamed x41, local copies, waits for them, and re-layouts  10.9 us
    pallas_call x2, Pallas kernels, scores_of(): pl.pallas_call(functools.partial(scores_kernel, plan), out_shape=[jax.Sha...  9.91 us
    ppermute x6, waiting for transfers between devices, up(): return lax.ppermute(value, 'x', UP)  9.89 us
    ppermute x6, waiting for transfers between devices, down(): return lax.ppermute(value, 'x', DOWN)  9.33 us
  transfers between devices with their start and end apart: 51, of which 17 were waited for; matrix products, arithmetic and copies ran while one was open for 7% of the time, Pallas kernels for 18%

profile of v6, /device:TPU:0, one launch (start us, length us, event | category | flops | bytes accessed | tf_op | source)
XLA Modules:
  0.0 159.1 jit_solution(18109736488102585762)
XLA Ops:
  12.5 3.2 %collective-permute-done.5 = s32[2,64]{1,0:T(2,128)S(1)} collective-permute-done((s32[2,64]{1,0:T(2,128)S(1)}, s32[2,64]{1,0:T(2,128)S(1)}, u32[]{:S(2)}, u32[]{:S(2)}) %collective-permute-start.5) | collective-permute-done | bytes 544 | tf_op jit(solution)/shard_map/ppermute | solution.py:59
  17.1 2.8 %collective-permute-start.7 = (bf16[2,32,2048]{2,1,0:T(8,128)(2,1)S(1)}, bf16[2,32,2048]{2,1,0:T(8,128)(2,1)S(1)}, u32[]{:S(2)}, u32[]{:S(2)}) collective-permute-start(bf16[2,32,2048]{2,1,0:T(8,128)(2,1)S(1)} %slice.93), channel_id=1, source_target_pairs={{0,96},{1,25},{2,98},{3,27},{4,100},{5,29},{6,102},{7,31},{8,104},... | collective-permute-start | bytes 786440 | tf_op jit(solution)/shard_map/ppermute | solution.py:43
  21.6 3.2 %collective-permute-start.9 = (s32[4,2,64]{2,1,0:T(2,128)S(1)}, s32[4,2,64]{2,1,0:T(2,128)S(1)}, u32[]{:S(2)}, u32[]{:S(2)}) collective-permute-start(s32[4,2,64]{2,1,0:T(2,128)S(1)} %pad_add_fusion.2), channel_id=1, source_target_pairs={{0,96},{1,25},{2,98},{3,27},{4,100},{5,29},{6,102},{7,31},{8,104},... | collective-permute-start | bytes 6152 | tf_op jit(solution)/shard_map/ppermute | solution.py:43
  26.4 3.5 %collective-permute-done.10 = s32[4,2,64]{2,1,0:T(2,128)S(1)} collective-permute-done((s32[4,2,64]{2,1,0:T(2,128)S(1)}, s32[4,2,64]{2,1,0:T(2,128)S(1)}, u32[]{:S(2)}, u32[]{:S(2)}) %collective-permute-start.10) | collective-permute-done | bytes 2080 | tf_op jit(solution)/shard_map/ppermute | solution.py:43
  44.1 3.0 %collective-permute-start.17 = (bf16[2,64,2048]{2,1,0:T(8,128)(2,1)S(1)}, bf16[2,64,2048]{2,1,0:T(8,128)(2,1)}, u32[]{:S(2)}, u32[]{:S(2)}) collective-permute-start(bf16[2,64,2048]{2,1,0:T(8,128)(2,1)S(1)} %pad_maximum_fusion.refs_0_), channel_id=1, source_target_pairs={{0,6},{2,0},{4,2},{6,4},{1,7},{3,1},{5,3},{7,5},{8,14},{10,8},{12,... | collective-permute-start | bytes 1572872 | tf_op jit(solution)/shard_map/ppermute | solution.py:55
  51.1 3.1 %collective-permute-done.16.refs_1_ = bf16[2,64,2048]{2,1,0:T(8,128)(2,1)S(1)} collective-permute-done((bf16[2,64,2048]{2,1,0:T(8,128)(2,1)S(1)}, bf16[2,64,2048]{2,1,0:T(8,128)(2,1)S(1)}, u32[]{:S(2)}, u32[]{:S(2)}) %collective-permute-start.16) | collective-permute-done | bytes 524320 | tf_op jit(solution)/shard_map/ppermute | solution.py:51
  56.7 3.2 %collective-permute-start.19 = (bf16[2,32,2048]{2,1,0:T(8,128)(2,1)}, bf16[2,32,2048]{2,1,0:T(8,128)(2,1)}, u32[]{:S(2)}, u32[]{:S(2)}) collective-permute-start(bf16[2,32,2048]{2,1,0:T(8,128)(2,1)} %slice.129), channel_id=1, source_target_pairs={{0,6},{2,0},{4,2},{6,4},{1,7},{3,1},{5,3},{7,5},{8,14},{10,8},{12,... | collective-permute-start | bytes 786440 | tf_op jit(solution)/shard_map/ppermute | solution.py:55
  60.0 2.7 %collective-permute-done.18.refs_3_ = bf16[2,32,2048]{2,1,0:T(8,128)(2,1)S(1)} collective-permute-done((bf16[2,32,2048]{2,1,0:T(8,128)(2,1)}, bf16[2,32,2048]{2,1,0:T(8,128)(2,1)S(1)}, u32[]{:S(2)}, u32[]{:S(2)}) %collective-permute-start.18) | collective-permute-done | bytes 262176 | tf_op jit(solution)/shard_map/ppermute | solution.py:51
  71.0 2.8 %collective-permute-start.26 = (bf16[2,128,2048]{2,1,0:T(8,128)(2,1)S(1)}, bf16[2,128,2048]{2,1,0:T(8,128)(2,1)}, u32[]{:S(2)}, u32[]{:S(2)}) collective-permute-start(bf16[2,128,2048]{2,1,0:T(8,128)(2,1)S(1)} %shard_map.69), channel_id=1, source_target_pairs={{0,24},{1,97},{2,26},{3,99},{4,28},{5,101},{6,30},{7,103},{8,0},{9... | collective-permute-start | bytes 3145736 | tf_op jit(solution)/shard_map/ppermute | solution.py:43
  78.6 7.2 %shard_map.71 = (f32[512,256]{1,0:T(8,128)S(1)}, f32[512,256]{1,0:T(8,128)S(1)}, f32[512,256]{1,0:T(8,128)S(1)}) custom-call(bf16[2,512,2048]{2,1,0:T(8,128)(2,1)S(1)} %shard_map.70.refs_0_, bf16[2,256,2048]{2,1,0:T(8,128)(2,1)S(1)} %shard_map.67.refs_1_.refs_0_, bf16[2,256,2048]{2,1,0:T(8,128)(2,1)} %collective-permute-done.14.refs_0_.refs_2_.refs_1_, ...), custom_call_target="tpu_custom_call" | custom-call | tf_op jit(solution)/shard_map/pallas_call | solution.py:182
  91.0 2.8 %shard_map.72 = (f32[512,128]{1,0:T(8,128)S(1)}, f32[512,128]{1,0:T(8,128)S(1)}) custom-call(bf16[2,512,2048]{2,1,0:T(8,128)(2,1)S(1)} %copy-done.1, bf16[2,128,2048]{2,1,0:T(8,128)(2,1)S(1)} %collective-permute-done.25.refs_1_.refs_3_, bf16[2,128,2048]{2,1,0:T(8,128)(2,1)} %collective-permute-done.26.refs_2_.refs_4_), custom_call_target="tpu_custom_call" | custom-call | tf_op jit(solution)/shard_map/pallas_call | solution.py:182
  93.8 2.7 %shard_map.73.refs_0_ = f32[16,128]{1,0:T(8,128)S(1)} custom-call(s32[1]{0:T(128)} %bitcast.core, f32[1]{0:T(128)} %bitcast.25.amax, f32[512,256]{1,0:T(8,128)S(1)} %copy-done.3, f32[512,256]{1,0:T(8,128)S(1)} %copy-done.5, f32[512,256]{1,0:T(8,128)S(1)} %copy-done.7, f32[512,128]{1,0:T(8,128)S(1)} %get-tuple-element.128.refs_3_, ...), custom_call_target="tpu_custom_call" | custom-call | tf_op jit(solution)/shard_map/pallas_call | solution.py:244
  96.9 3.0 %collective-permute-start.33 = (f32[16,128]{1,0:T(8,128)S(1)}, f32[16,128]{1,0:T(8,128)S(1)}, u32[]{:S(2)}, u32[]{:S(2)}) collective-permute-start(f32[16,128]{1,0:T(8,128)S(1)} %shard_map.73.refs_0_), channel_id=1, source_target_pairs={{0,6},{2,0},{4,2},{6,4},{1,7},{3,1},{5,3},{7,5},{8,14},{10,8},{12,... | collective-permute-start | bytes 24584 | tf_op jit(solution)/shard_map/ppermute | solution.py:55
  102.0 3.0 %collective-permute-done.34.refs_3_ = f32[16,128]{1,0:T(8,128)S(1)} collective-permute-done((f32[16,128]{1,0:T(8,128)S(1)}, f32[16,128]{1,0:T(8,128)S(1)}, u32[]{:S(2)}, u32[]{:S(2)}) %collective-permute-start.34) | collective-permute-done | bytes 8224 | tf_op jit(solution)/shard_map/ppermute | solution.py:59
  106.4 3.2 %collective-permute-start.40 = (f32[8,128]{1,0:T(8,128)S(1)}, f32[8,128]{1,0:T(8,128)S(1)}, u32[]{:S(2)}, u32[]{:S(2)}) collective-permute-start(f32[8,128]{1,0:T(8,128)S(1)} %get-tuple-element.140), channel_id=1, source_target_pairs={{0,96},{1,25},{2,98},{3,27},{4,100},{5,29},{6,102},{7,31},{8,104},... | collective-permute-start | bytes 12296 | tf_op jit(solution)/shard_map/ppermute | solution.py:43
  111.2 3.5 %collective-permute-done.41 = f32[8,128]{1,0:T(8,128)S(1)} collective-permute-done((f32[8,128]{1,0:T(8,128)S(1)}, f32[8,128]{1,0:T(8,128)S(1)}, u32[]{:S(2)}, u32[]{:S(2)}) %collective-permute-start.41) | collective-permute-done | bytes 4128 | tf_op jit(solution)/shard_map/ppermute | solution.py:43
  114.7 3.2 %collective-permute-start.43 = (f32[32,128]{1,0:T(8,128)S(1)}, f32[32,128]{1,0:T(8,128)S(1)}, u32[]{:S(2)}, u32[]{:S(2)}) collective-permute-start(f32[32,128]{1,0:T(8,128)S(1)} %constant_dynamic-update-slice_fusion.4.refs_8_), channel_id=1, source_target_pairs={{0,24},{1,97},{2,26},{3,99},{4,28},{5,101},{6,30},{7,103},{8,0},{9... | collective-permute-start | bytes 49160 | tf_op jit(solution)/shard_map/ppermute | solution.py:43
  119.7 3.5 %collective-permute-done.44.refs_11_ = f32[32,128]{1,0:T(8,128)S(1)} collective-permute-done((f32[32,128]{1,0:T(8,128)S(1)}, f32[32,128]{1,0:T(8,128)S(1)}, u32[]{:S(2)}, u32[]{:S(2)}) %collective-permute-start.44) | collective-permute-done | bytes 16416 | tf_op jit(solution)/shard_map/ppermute | solution.py:43
  125.9 4.4 %shard_map.76 = f32[128,2048]{1,0:T(8,128)S(1)} custom-call(f32[8,128]{1,0:T(8,128)S(1)} %get-tuple-element.141.bound, bf16[128,1024]{1,0:T(8,128)(2,1)S(1)} %get-tuple-element.142.mine, bf16[128,1024]{1,0:T(8,128)(2,1)S(1)} %collective-permute-done.45.theirs, bf16[2,256,2048]{2,1,0:T(8,128)(2,1)S(1)} %shard_map.67.refs_1_.refs_0_, ...), custom_call_target="tpu_custom_call" | custom-call | tf_op jit(solution)/shard_map/pallas_call | solution.py:387
  130.6 3.2 %collective-permute-start.47 = (f16[64,2048]{1,0:T(8,128)(2,1)S(1)}, f16[64,2048]{1,0:T(8,128)(2,1)S(1)}, u32[]{:S(2)}, u32[]{:S(2)}) collective-permute-start(f16[64,2048]{1,0:T(8,128)(2,1)S(1)} %get-tuple-element.169), channel_id=1, source_target_pairs={{0,6},{2,0},{4,2},{6,4},{1,7},{3,1},{5,3},{7,5},{8,14},{10,8},{12,... | collective-permute-start | bytes 786440 | tf_op jit(solution)/shard_map/ppermute | solution.py:55
  133.8 6.5 %shard_map.78 = (f32[128,2048]{1,0:T(8,128)S(1)}, f32[128,2048]{1,0:T(8,128)S(1)}, f32[128,2048]{1,0:T(8,128)S(1)}) custom-call(f32[8,128]{1,0:T(8,128)S(1)} %get-tuple-element.141.bound, bf16[384,1024]{1,0:T(8,128)(2,1)S(1)} %get-tuple-element.154.mine, bf16[384,1024]{1,0:T(8,128)(2,1)S(1)} %collective-permute-done.48.theirs, ...), custom_call_target="tpu_custom_call" | custom-call | tf_op jit(solution)/shard_map/pallas_call | solution.py:387
  140.6 2.7 %collective-permute-start.50 = (f16[128,2048]{1,0:T(8,128)(2,1)S(1)}, f16[128,2048]{1,0:T(8,128)(2,1)S(1)}, u32[]{:S(2)}, u32[]{:S(2)}) collective-permute-start(f16[128,2048]{1,0:T(8,128)(2,1)S(1)} %pad_maximum_fusion.2), channel_id=1, source_target_pairs={{0,6},{2,0},{4,2},{6,4},{1,7},{3,1},{5,3},{7,5},{8,14},{10,8},{12,... | collective-permute-start | bytes 1572872 | tf_op jit(solution)/shard_map/ppermute | solution.py:55
  144.7 9.3 %collective-permute-done.50 = f16[128,2048]{1,0:T(8,128)(2,1)S(1)} collective-permute-done((f16[128,2048]{1,0:T(8,128)(2,1)S(1)}, f16[128,2048]{1,0:T(8,128)(2,1)S(1)}, u32[]{:S(2)}, u32[]{:S(2)}) %collective-permute-start.50) | collective-permute-done | bytes 524320 | tf_op jit(solution)/shard_map/ppermute | solution.py:55
  154.0 3.2 %collective-permute-done.49 = f16[128,2048]{1,0:T(8,128)(2,1)S(1)} collective-permute-done((f16[128,2048]{1,0:T(8,128)(2,1)S(1)}, f16[128,2048]{1,0:T(8,128)(2,1)S(1)}, u32[]{:S(2)}, u32[]{:S(2)}) %collective-permute-start.49) | collective-permute-done | bytes 524320 | tf_op jit(solution)/shard_map/ppermute | solution.py:51
  (195 shorter events, 67.7 us)
Async XLA Ops:
  3.4 12.3 %collective-permute-start.1 = (bf16[2,64,2048]{2,1,0:T(8,128)(2,1)S(1)}, bf16[2,64,2048]{2,1,0:T(8,128)(2,1)S(1)}, u32[]{:S(2)}, u32[]{:S(2)}) collective-permute-start(bf16[2,64,2048]{2,1,0:T(8,128)(2,1)S(1)} %pad_maximum_fusion.refs_0_), channel_id=1, source_target_pairs={{0,32},{1,9},{2,34},{3,11},{4,36},{5,13},{6,38},{7,15},{8,40},{9,1... | collective-permute-start | bytes 1572872 | tf_op jit(solution)/shard_map/ppermute | solution.py:43
  5.1 10.6 %collective-permute-start.2 = (bf16[2,64,2048]{2,1,0:T(8,128)(2,1)S(1)}, bf16[2,64,2048]{2,1,0:T(8,128)(2,1)S(1)}, u32[]{:S(2)}, u32[]{:S(2)}) collective-permute-start(bf16[2,64,2048]{2,1,0:T(8,128)(2,1)S(1)} %pad_maximum_fusion.refs_0_), channel_id=1, source_target_pairs={{0,96},{1,25},{2,98},{3,27},{4,100},{5,29},{6,102},{7,31},{8,104},... | collective-permute-start | bytes 1572872 | tf_op jit(solution)/shard_map/ppermute | solution.py:43
  15.7 14.2 %collective-permute-start.6 = (bf16[2,32,2048]{2,1,0:T(8,128)(2,1)S(1)}, bf16[2,32,2048]{2,1,0:T(8,128)(2,1)S(1)}, u32[]{:S(2)}, u32[]{:S(2)}) collective-permute-start(bf16[2,32,2048]{2,1,0:T(8,128)(2,1)S(1)} %slice.92), channel_id=1, source_target_pairs={{0,32},{1,9},{2,34},{3,11},{4,36},{5,13},{6,38},{7,15},{8,40},{9,1... | collective-permute-start | bytes 786440 | tf_op jit(solution)/shard_map/ppermute | solution.py:43
  17.1 12.9 %collective-permute-start.7 = (bf16[2,32,2048]{2,1,0:T(8,128)(2,1)S(1)}, bf16[2,32,2048]{2,1,0:T(8,128)(2,1)S(1)}, u32[]{:S(2)}, u32[]{:S(2)}) collective-permute-start(bf16[2,32,2048]{2,1,0:T(8,128)(2,1)S(1)} %slice.93), channel_id=1, source_target_pairs={{0,96},{1,25},{2,98},{3,27},{4,100},{5,29},{6,102},{7,31},{8,104},... | collective-permute-start | bytes 786440 | tf_op jit(solution)/shard_map/ppermute | solution.py:43
  30.7 9.8 %collective-permute-start.11 = (s32[4,4,2,64]{3,2,1,0:T(2,128)S(1)}, s32[4,4,2,64]{3,2,1,0:T(2,128)S(1)}, u32[]{:S(2)}, u32[]{:S(2)}) collective-permute-start(s32[4,4,2,64]{3,2,1,0:T(2,128)S(1)} %pad_add_fusion.1), channel_id=1, source_target_pairs={{0,8},{1,33},{2,10},{3,35},{4,12},{5,37},{6,14},{7,39},{8,16},{9,4... | collective-permute-start | bytes 24584 | tf_op jit(solution)/shard_map/ppermute | solution.py:43
  32.7 7.8 %collective-permute-start.12 = (s32[4,4,2,64]{3,2,1,0:T(2,128)S(1)}, s32[4,4,2,64]{3,2,1,0:T(2,128)S(1)}, u32[]{:S(2)}, u32[]{:S(2)}) collective-permute-start(s32[4,4,2,64]{3,2,1,0:T(2,128)S(1)} %pad_add_fusion.1), channel_id=1, source_target_pairs={{0,24},{1,97},{2,26},{3,99},{4,28},{5,101},{6,30},{7,103},{8,0},{9... | collective-permute-start | bytes 24584 | tf_op jit(solution)/shard_map/ppermute | solution.py:43
  40.5 27.4 %collective-permute-start.14 = (bf16[2,256,2048]{2,1,0:T(8,128)(2,1)S(1)}, bf16[2,256,2048]{2,1,0:T(8,128)(2,1)}, u32[]{:S(2)}, u32[]{:S(2)}) collective-permute-start(bf16[2,256,2048]{2,1,0:T(8,128)(2,1)S(1)} %shard_map.67.refs_1_.refs_0_), channel_id=1, source_target_pairs={{0,8},{1,33},{2,10},{3,35},{4,12},{5,37},{6,14},{7,39},{8,16},{9,4... | collective-permute-start | bytes 6291464 | tf_op jit(solution)/shard_map/ppermute | solution.py:43
  41.6 26.3 %collective-permute-start.15 = (bf16[2,256,2048]{2,1,0:T(8,128)(2,1)S(1)}, bf16[2,256,2048]{2,1,0:T(8,128)(2,1)}, u32[]{:S(2)}, u32[]{:S(2)}) collective-permute-start(bf16[2,256,2048]{2,1,0:T(8,128)(2,1)S(1)} %shard_map.67.refs_1_.refs_0_), channel_id=1, source_target_pairs={{0,24},{1,97},{2,26},{3,99},{4,28},{5,101},{6,30},{7,103},{8,0},{9... | collective-permute-start | bytes 6291464 | tf_op jit(solution)/shard_map/ppermute | solution.py:43
  43.8 10.4 %collective-permute-start.16 = (bf16[2,64,2048]{2,1,0:T(8,128)(2,1)S(1)}, bf16[2,64,2048]{2,1,0:T(8,128)(2,1)S(1)}, u32[]{:S(2)}, u32[]{:S(2)}) collective-permute-start(bf16[2,64,2048]{2,1,0:T(8,128)(2,1)S(1)} %pad_maximum_fusion.refs_0_), channel_id=1, source_target_pairs={{0,2},{2,4},{4,6},{6,0},{1,3},{3,5},{5,7},{7,1},{8,10},{10,12},{12... | collective-permute-start | bytes 1572872 | tf_op jit(solution)/shard_map/ppermute | solution.py:51
  44.1 11.0 %collective-permute-start.17 = (bf16[2,64,2048]{2,1,0:T(8,128)(2,1)S(1)}, bf16[2,64,2048]{2,1,0:T(8,128)(2,1)}, u32[]{:S(2)}, u32[]{:S(2)}) collective-permute-start(bf16[2,64,2048]{2,1,0:T(8,128)(2,1)S(1)} %pad_maximum_fusion.refs_0_), channel_id=1, source_target_pairs={{0,6},{2,0},{4,2},{6,4},{1,7},{3,1},{5,3},{7,5},{8,14},{10,8},{12,... | collective-permute-start | bytes 1572872 | tf_op jit(solution)/shard_map/ppermute | solution.py:55
  47.1 16.8 %collective-permute-start.20 = (bf16[2,64,2048]{2,1,0:T(8,128)(2,1)S(1)}, bf16[2,64,2048]{2,1,0:T(8,128)(2,1)}, u32[]{:S(2)}, u32[]{:S(2)}) collective-permute-start(bf16[2,64,2048]{2,1,0:T(8,128)(2,1)S(1)} %pad_maximum_fusion.refs_0_), channel_id=1, source_target_pairs={{0,1},{1,0},{2,3},{3,2},{4,5},{5,4},{6,7},{7,6},{8,9},{9,8},{10,11... | collective-permute-start | bytes 1572872 | tf_op jit(solution)/shard_map/ppermute | solution.py:47
  55.0 7.8 %collective-permute-start.18 = (bf16[2,32,2048]{2,1,0:T(8,128)(2,1)}, bf16[2,32,2048]{2,1,0:T(8,128)(2,1)S(1)}, u32[]{:S(2)}, u32[]{:S(2)}) collective-permute-start(bf16[2,32,2048]{2,1,0:T(8,128)(2,1)} %slice.128), channel_id=1, source_target_pairs={{0,2},{2,4},{4,6},{6,0},{1,3},{3,5},{5,7},{7,1},{8,10},{10,12},{12... | collective-permute-start | bytes 786440 | tf_op jit(solution)/shard_map/ppermute | solution.py:51
  69.2 19.0 %collective-permute-start.25 = (bf16[2,128,2048]{2,1,0:T(8,128)(2,1)S(1)}, bf16[2,128,2048]{2,1,0:T(8,128)(2,1)S(1)}, u32[]{:S(2)}, u32[]{:S(2)}) collective-permute-start(bf16[2,128,2048]{2,1,0:T(8,128)(2,1)S(1)} %shard_map.68), channel_id=1, source_target_pairs={{0,8},{1,33},{2,10},{3,35},{4,12},{5,37},{6,14},{7,39},{8,16},{9,4... | collective-permute-start | bytes 3145736 | tf_op jit(solution)/shard_map/ppermute | solution.py:43
  71.0 17.2 %collective-permute-start.26 = (bf16[2,128,2048]{2,1,0:T(8,128)(2,1)S(1)}, bf16[2,128,2048]{2,1,0:T(8,128)(2,1)}, u32[]{:S(2)}, u32[]{:S(2)}) collective-permute-start(bf16[2,128,2048]{2,1,0:T(8,128)(2,1)S(1)} %shard_map.69), channel_id=1, source_target_pairs={{0,24},{1,97},{2,26},{3,99},{4,28},{5,101},{6,30},{7,103},{8,0},{9... | collective-permute-start | bytes 3145736 | tf_op jit(solution)/shard_map/ppermute | solution.py:43
  77.9 18.6 %collective-permute-start.27 = (bf16[2,256,2048]{2,1,0:T(8,128)(2,1)S(1)}, bf16[2,256,2048]{2,1,0:T(8,128)(2,1)}, u32[]{:S(2)}, u32[]{:S(2)}) collective-permute-start(bf16[2,256,2048]{2,1,0:T(8,128)(2,1)S(1)} %shard_map.67.refs_1_.refs_0_), channel_id=1, source_target_pairs={{0,1},{1,0},{2,3},{3,2},{4,5},{5,4},{6,7},{7,6},{8,9},{9,8},{10,11... | collective-permute-start | bytes 6291464 | tf_op jit(solution)/shard_map/ppermute | solution.py:47
  78.0 18.5 %collective-permute-start.28 = (bf16[2,256,2048]{2,1,0:T(8,128)(2,1)}, bf16[2,256,2048]{2,1,0:T(8,128)(2,1)}, u32[]{:S(2)}, u32[]{:S(2)}) collective-permute-start(bf16[2,256,2048]{2,1,0:T(8,128)(2,1)} %collective-permute-done.14.refs_0_.refs_2_.refs_1_), channel_id=1, source_target_pairs={{0,1},{1,0},{2,3},{3,2},{4,5},{5,4},{6,7},{7,6},{8,9},{9,8},{10,11... | collective-permute-start | bytes 6291464 | tf_op jit(solution)/shard_map/ppermute | solution.py:47
  78.5 18.0 %collective-permute-start.29 = (bf16[2,256,2048]{2,1,0:T(8,128)(2,1)}, bf16[2,256,2048]{2,1,0:T(8,128)(2,1)}, u32[]{:S(2)}, u32[]{:S(2)}) collective-permute-start(bf16[2,256,2048]{2,1,0:T(8,128)(2,1)} %collective-permute-done.15.refs_0_.refs_3_.refs_2_), channel_id=1, source_target_pairs={{0,1},{1,0},{2,3},{3,2},{4,5},{5,4},{6,7},{7,6},{8,9},{9,8},{10,11... | collective-permute-start | bytes 6291464 | tf_op jit(solution)/shard_map/ppermute | solution.py:47
  88.2 8.4 %collective-permute-start.30 = (bf16[2,128,2048]{2,1,0:T(8,128)(2,1)S(1)}, bf16[2,128,2048]{2,1,0:T(8,128)(2,1)}, u32[]{:S(2)}, u32[]{:S(2)}) collective-permute-start(bf16[2,128,2048]{2,1,0:T(8,128)(2,1)S(1)} %collective-permute-done.25.refs_1_.refs_3_), channel_id=1, source_target_pairs={{0,1},{1,0},{2,3},{3,2},{4,5},{5,4},{6,7},{7,6},{8,9},{9,8},{10,11... | collective-permute-start | bytes 3145736 | tf_op jit(solution)/shard_map/ppermute | solution.py:47
  88.2 8.4 %collective-permute-start.31 = (bf16[2,128,2048]{2,1,0:T(8,128)(2,1)}, bf16[2,128,2048]{2,1,0:T(8,128)(2,1)}, u32[]{:S(2)}, u32[]{:S(2)}) collective-permute-start(bf16[2,128,2048]{2,1,0:T(8,128)(2,1)} %collective-permute-done.26.refs_2_.refs_4_), channel_id=1, source_target_pairs={{0,1},{1,0},{2,3},{3,2},{4,5},{5,4},{6,7},{7,6},{8,9},{9,8},{10,11... | collective-permute-start | bytes 3145736 | tf_op jit(solution)/shard_map/ppermute | solution.py:47
  125.4 8.4 %collective-permute-start.48 = (bf16[384,1024]{1,0:T(8,128)(2,1)S(1)}, bf16[384,1024]{1,0:T(8,128)(2,1)S(1)}, u32[]{:S(2)}, u32[]{:S(2)}) collective-permute-start(bf16[384,1024]{1,0:T(8,128)(2,1)S(1)} %get-tuple-element.154.mine), channel_id=1, source_target_pairs={{0,1},{1,0},{2,3},{3,2},{4,5},{5,4},{6,7},{7,6},{8,9},{9,8},{10,11... | collective-permute-start | bytes 2359304 | tf_op jit(solution)/shard_map/ppermute | solution.py:47
  130.5 9.8 %collective-permute-start.46 = (f16[64,2048]{1,0:T(8,128)(2,1)S(1)}, f16[64,2048]{1,0:T(8,128)(2,1)S(1)}, u32[]{:S(2)}, u32[]{:S(2)}) collective-permute-start(f16[64,2048]{1,0:T(8,128)(2,1)S(1)} %get-tuple-element.170), channel_id=1, source_target_pairs={{0,2},{2,4},{4,6},{6,0},{1,3},{3,5},{5,7},{7,1},{8,10},{10,12},{12... | collective-permute-start | bytes 786440 | tf_op jit(solution)/shard_map/ppermute | solution.py:51
  130.6 9.8 %collective-permute-start.47 = (f16[64,2048]{1,0:T(8,128)(2,1)S(1)}, f16[64,2048]{1,0:T(8,128)(2,1)S(1)}, u32[]{:S(2)}, u32[]{:S(2)}) collective-permute-start(f16[64,2048]{1,0:T(8,128)(2,1)S(1)} %get-tuple-element.169), channel_id=1, source_target_pairs={{0,6},{2,0},{4,2},{6,4},{1,7},{3,1},{5,3},{7,5},{8,14},{10,8},{12,... | collective-permute-start | bytes 786440 | tf_op jit(solution)/shard_map/ppermute | solution.py:55
  140.6 13.3 %collective-permute-start.50 = (f16[128,2048]{1,0:T(8,128)(2,1)S(1)}, f16[128,2048]{1,0:T(8,128)(2,1)S(1)}, u32[]{:S(2)}, u32[]{:S(2)}) collective-permute-start(f16[128,2048]{1,0:T(8,128)(2,1)S(1)} %pad_maximum_fusion.2), channel_id=1, source_target_pairs={{0,6},{2,0},{4,2},{6,4},{1,7},{3,1},{5,3},{7,5},{8,14},{10,8},{12,... | collective-permute-start | bytes 1572872 | tf_op jit(solution)/shard_map/ppermute | solution.py:55
  143.6 13.7 %collective-permute-start.49 = (f16[128,2048]{1,0:T(8,128)(2,1)S(1)}, f16[128,2048]{1,0:T(8,128)(2,1)S(1)}, u32[]{:S(2)}, u32[]{:S(2)}) collective-permute-start(f16[128,2048]{1,0:T(8,128)(2,1)S(1)} %pad_maximum_fusion.1), channel_id=1, source_target_pairs={{0,2},{2,4},{4,6},{6,0},{1,3},{3,5},{5,7},{7,1},{8,10},{10,12},{12... | collective-permute-start | bytes 1572872 | tf_op jit(solution)/shard_map/ppermute | solution.py:51
  (45 other events, 227.8 us)

commit v7 on v6

--- a/solution.py
+++ b/solution.py
@@ -445,11 +445,11 @@
     i_tgt, j_tgt = look(i_pos), look(j_pos)
     rows = jnp.stack([pick(i_pair, i_id), pick(i_id, i_tgt), pick(i_pair, i_pos)] + [i_pair] * 5, axis=1)
     cols = jnp.stack([pick(j_pair, j_id), pick(j_tgt, j_id), pick(j_pos, j_pair)] + [j_pair] * 5)
-    amax = jnp.maximum(
-        jnp.max(jnp.abs(queries.astype(jnp.float32))), jnp.max(jnp.abs(passages.astype(jnp.float32)))
-    )
     xl, xr = up(own), down(own)
     mine = [own, xl, xr, up(low(xl)[0]), down(high(xr)[0])]
+    amax = jnp.maximum(
+        *[jnp.max(jnp.abs(after(a, group, ids).astype(jnp.float32))) for a in (queries, passages)]
+    )
     dl, dr, group, rows, cols, amax, *held = settle(
         along(group, SECOND[1]), along(group, SECOND[3]), group, rows, cols, amax, *mine, *[swap(a) for a in mine]
     )

time: 160 us -> 158 us (0.988)
  waiting for transfers between devices: 45.5 us -> 43.4 us
    ppermute x6, waiting for transfers between devices: 9.89 us -> 8.13 us  [up(): return lax.ppermute(value, 'x', UP)]
  transfers between devices with their start and end apart: 51 -> 51, of which waited for: 17 -> 18; matrix products, arithmetic and copies ran while one was open for 7% -> 7% of each run, Pallas kernels for 18% -> 18%
where the time goes in v7:
time: 158 us; the launch traced here: 157 us
  starting transfers between devices  55 us (35%)
  waiting for transfers between devices  43.4 us (27%)
  Pallas kernels  30.4 us (19%)
  local copies, waits for them, and re-layouts  17.5 us (11%)
  other arithmetic  8.27 us (5%)
  between operations  2.38 us (2%)
    ppermute x20, starting transfers between devices, along(): return lax.ppermute(value, GRID, moves)  29.8 us
    ppermute x6, starting transfers between devices, down(): return lax.ppermute(value, 'x', DOWN)  16.6 us
    ppermute x20, waiting for transfers between devices, along(): return lax.ppermute(value, GRID, moves)  16.2 us
    pallas_call x2, Pallas kernels, product_of(): pl.pallas_call(functools.partial(product_kernel, scaled), out_shape=[jax....  11 us
    unnamed x41, local copies, waits for them, and re-layouts  10.9 us
    pallas_call x2, Pallas kernels, scores_of(): pl.pallas_call(functools.partial(scores_kernel, plan), out_shape=[jax.Sha...  9.91 us
    ppermute x6, waiting for transfers between devices, down(): return lax.ppermute(value, 'x', DOWN)  9.33 us
    ppermute x6, waiting for transfers between devices, up(): return lax.ppermute(value, 'x', UP)  8.13 us
  transfers between devices with their start and end apart: 51, of which 18 were waited for; matrix products, arithmetic and copies ran while one was open for 7% of the time, Pallas kernels for 18%

profile of v7, /device:TPU:0, one launch (start us, length us, event | category | flops | bytes accessed | tf_op | source)
XLA Modules:
  0.0 157.0 jit_solution(10109578766217558716)
XLA Ops:
  12.5 3.2 %collective-permute-done.5 = s32[2,64]{1,0:T(2,128)S(1)} collective-permute-done((s32[2,64]{1,0:T(2,128)S(1)}, s32[2,64]{1,0:T(2,128)S(1)}, u32[]{:S(2)}, u32[]{:S(2)}) %collective-permute-start.5) | collective-permute-done | bytes 544 | tf_op jit(solution)/shard_map/ppermute | solution.py:59
  17.1 2.8 %collective-permute-start.7 = (bf16[2,32,2048]{2,1,0:T(8,128)(2,1)S(1)}, bf16[2,32,2048]{2,1,0:T(8,128)(2,1)S(1)}, u32[]{:S(2)}, u32[]{:S(2)}) collective-permute-start(bf16[2,32,2048]{2,1,0:T(8,128)(2,1)S(1)} %slice.93), channel_id=1, source_target_pairs={{0,96},{1,25},{2,98},{3,27},{4,100},{5,29},{6,102},{7,31},{8,104},... | collective-permute-start | bytes 786440 | tf_op jit(solution)/shard_map/ppermute | solution.py:43
  19.9 3.2 %collective-permute-start.9 = (s32[4,2,64]{2,1,0:T(2,128)S(1)}, s32[4,2,64]{2,1,0:T(2,128)S(1)}, u32[]{:S(2)}, u32[]{:S(2)}) collective-permute-start(s32[4,2,64]{2,1,0:T(2,128)S(1)} %pad_add_fusion.2), channel_id=1, source_target_pairs={{0,96},{1,25},{2,98},{3,27},{4,100},{5,29},{6,102},{7,31},{8,104},... | collective-permute-start | bytes 6152 | tf_op jit(solution)/shard_map/ppermute | solution.py:43
  24.7 3.5 %collective-permute-done.10 = s32[4,2,64]{2,1,0:T(2,128)S(1)} collective-permute-done((s32[4,2,64]{2,1,0:T(2,128)S(1)}, s32[4,2,64]{2,1,0:T(2,128)S(1)}, u32[]{:S(2)}, u32[]{:S(2)}) %collective-permute-start.10) | collective-permute-done | bytes 2080 | tf_op jit(solution)/shard_map/ppermute | solution.py:43
  38.6 3.1 %collective-permute-start.15 = (bf16[2,256,2048]{2,1,0:T(8,128)(2,1)S(1)}, bf16[2,256,2048]{2,1,0:T(8,128)(2,1)}, u32[]{:S(2)}, u32[]{:S(2)}) collective-permute-start(bf16[2,256,2048]{2,1,0:T(8,128)(2,1)S(1)} %shard_map.67.refs_1_.refs_0_), channel_id=1, source_target_pairs={{0,24},{1,97},{2,26},{3,99},{4,28},{5,101},{6,30},{7,103},{8,0},{9... | collective-permute-start | bytes 6291464 | tf_op jit(solution)/shard_map/ppermute | solution.py:43
  42.0 2.9 %collective-permute-start.17 = (bf16[2,64,2048]{2,1,0:T(8,128)(2,1)S(1)}, bf16[2,64,2048]{2,1,0:T(8,128)(2,1)}, u32[]{:S(2)}, u32[]{:S(2)}) collective-permute-start(bf16[2,64,2048]{2,1,0:T(8,128)(2,1)S(1)} %pad_maximum_fusion.refs_0_), channel_id=1, source_target_pairs={{0,6},{2,0},{4,2},{6,4},{1,7},{3,1},{5,3},{7,5},{8,14},{10,8},{12,... | collective-permute-start | bytes 1572872 | tf_op jit(solution)/shard_map/ppermute | solution.py:55
  49.1 3.0 %collective-permute-done.16.refs_1_ = bf16[2,64,2048]{2,1,0:T(8,128)(2,1)S(1)} collective-permute-done((bf16[2,64,2048]{2,1,0:T(8,128)(2,1)S(1)}, bf16[2,64,2048]{2,1,0:T(8,128)(2,1)S(1)}, u32[]{:S(2)}, u32[]{:S(2)}) %collective-permute-start.16) | collective-permute-done | bytes 524320 | tf_op jit(solution)/shard_map/ppermute | solution.py:51
  54.6 3.2 %collective-permute-start.19 = (bf16[2,32,2048]{2,1,0:T(8,128)(2,1)}, bf16[2,32,2048]{2,1,0:T(8,128)(2,1)}, u32[]{:S(2)}, u32[]{:S(2)}) collective-permute-start(bf16[2,32,2048]{2,1,0:T(8,128)(2,1)} %slice.129), channel_id=1, source_target_pairs={{0,6},{2,0},{4,2},{6,4},{1,7},{3,1},{5,3},{7,5},{8,14},{10,8},{12,... | collective-permute-start | bytes 786440 | tf_op jit(solution)/shard_map/ppermute | solution.py:55
  68.8 2.8 %collective-permute-start.26 = (bf16[2,128,2048]{2,1,0:T(8,128)(2,1)S(1)}, bf16[2,128,2048]{2,1,0:T(8,128)(2,1)}, u32[]{:S(2)}, u32[]{:S(2)}) collective-permute-start(bf16[2,128,2048]{2,1,0:T(8,128)(2,1)S(1)} %shard_map.69), channel_id=1, source_target_pairs={{0,24},{1,97},{2,26},{3,99},{4,28},{5,101},{6,30},{7,103},{8,0},{9... | collective-permute-start | bytes 3145736 | tf_op jit(solution)/shard_map/ppermute | solution.py:43
  76.4 7.2 %shard_map.71 = (f32[512,256]{1,0:T(8,128)S(1)}, f32[512,256]{1,0:T(8,128)S(1)}, f32[512,256]{1,0:T(8,128)S(1)}) custom-call(bf16[2,512,2048]{2,1,0:T(8,128)(2,1)S(1)} %shard_map.70.refs_0_, bf16[2,256,2048]{2,1,0:T(8,128)(2,1)S(1)} %shard_map.67.refs_1_.refs_0_, bf16[2,256,2048]{2,1,0:T(8,128)(2,1)} %collective-permute-done.14.refs_0_.refs_2_.refs_1_, ...), custom_call_target="tpu_custom_call" | custom-call | tf_op jit(solution)/shard_map/pallas_call | solution.py:182
  88.8 2.8 %shard_map.72 = (f32[512,128]{1,0:T(8,128)S(1)}, f32[512,128]{1,0:T(8,128)S(1)}) custom-call(bf16[2,512,2048]{2,1,0:T(8,128)(2,1)S(1)} %copy-done.1, bf16[2,128,2048]{2,1,0:T(8,128)(2,1)S(1)} %collective-permute-done.25.refs_1_.refs_3_, bf16[2,128,2048]{2,1,0:T(8,128)(2,1)} %collective-permute-done.26.refs_2_.refs_4_), custom_call_target="tpu_custom_call" | custom-call | tf_op jit(solution)/shard_map/pallas_call | solution.py:182
  91.6 2.7 %shard_map.73.refs_0_ = f32[16,128]{1,0:T(8,128)S(1)} custom-call(s32[1]{0:T(128)} %bitcast.core, f32[1]{0:T(128)} %bitcast.25.amax, f32[512,256]{1,0:T(8,128)S(1)} %copy-done.3, f32[512,256]{1,0:T(8,128)S(1)} %copy-done.5, f32[512,256]{1,0:T(8,128)S(1)} %copy-done.7, f32[512,128]{1,0:T(8,128)S(1)} %get-tuple-element.132.refs_3_, ...), custom_call_target="tpu_custom_call" | custom-call | tf_op jit(solution)/shard_map/pallas_call | solution.py:244
  94.8 2.9 %collective-permute-start.33 = (f32[16,128]{1,0:T(8,128)S(1)}, f32[16,128]{1,0:T(8,128)S(1)}, u32[]{:S(2)}, u32[]{:S(2)}) collective-permute-start(f32[16,128]{1,0:T(8,128)S(1)} %shard_map.73.refs_0_), channel_id=1, source_target_pairs={{0,6},{2,0},{4,2},{6,4},{1,7},{3,1},{5,3},{7,5},{8,14},{10,8},{12,... | collective-permute-start | bytes 24584 | tf_op jit(solution)/shard_map/ppermute | solution.py:55
  99.9 3.0 %collective-permute-done.34.refs_3_ = f32[16,128]{1,0:T(8,128)S(1)} collective-permute-done((f32[16,128]{1,0:T(8,128)S(1)}, f32[16,128]{1,0:T(8,128)S(1)}, u32[]{:S(2)}, u32[]{:S(2)}) %collective-permute-start.34) | collective-permute-done | bytes 8224 | tf_op jit(solution)/shard_map/ppermute | solution.py:59
  104.2 3.2 %collective-permute-start.40 = (f32[8,128]{1,0:T(8,128)S(1)}, f32[8,128]{1,0:T(8,128)S(1)}, u32[]{:S(2)}, u32[]{:S(2)}) collective-permute-start(f32[8,128]{1,0:T(8,128)S(1)} %get-tuple-element.144), channel_id=1, source_target_pairs={{0,96},{1,25},{2,98},{3,27},{4,100},{5,29},{6,102},{7,31},{8,104},... | collective-permute-start | bytes 12296 | tf_op jit(solution)/shard_map/ppermute | solution.py:43
  109.0 3.5 %collective-permute-done.41 = f32[8,128]{1,0:T(8,128)S(1)} collective-permute-done((f32[8,128]{1,0:T(8,128)S(1)}, f32[8,128]{1,0:T(8,128)S(1)}, u32[]{:S(2)}, u32[]{:S(2)}) %collective-permute-start.41) | collective-permute-done | bytes 4128 | tf_op jit(solution)/shard_map/ppermute | solution.py:43
  112.5 3.2 %collective-permute-start.43 = (f32[32,128]{1,0:T(8,128)S(1)}, f32[32,128]{1,0:T(8,128)S(1)}, u32[]{:S(2)}, u32[]{:S(2)}) collective-permute-start(f32[32,128]{1,0:T(8,128)S(1)} %constant_dynamic-update-slice_fusion.4.refs_8_), channel_id=1, source_target_pairs={{0,24},{1,97},{2,26},{3,99},{4,28},{5,101},{6,30},{7,103},{8,0},{9... | collective-permute-start | bytes 49160 | tf_op jit(solution)/shard_map/ppermute | solution.py:43
  117.5 3.5 %collective-permute-done.44.refs_11_ = f32[32,128]{1,0:T(8,128)S(1)} collective-permute-done((f32[32,128]{1,0:T(8,128)S(1)}, f32[32,128]{1,0:T(8,128)S(1)}, u32[]{:S(2)}, u32[]{:S(2)}) %collective-permute-start.44) | collective-permute-done | bytes 16416 | tf_op jit(solution)/shard_map/ppermute | solution.py:43
  123.7 4.4 %shard_map.76 = f32[128,2048]{1,0:T(8,128)S(1)} custom-call(f32[8,128]{1,0:T(8,128)S(1)} %get-tuple-element.145.bound, bf16[128,1024]{1,0:T(8,128)(2,1)S(1)} %get-tuple-element.146.mine, bf16[128,1024]{1,0:T(8,128)(2,1)S(1)} %collective-permute-done.45.theirs, bf16[2,256,2048]{2,1,0:T(8,128)(2,1)S(1)} %shard_map.67.refs_1_.refs_0_, ...), custom_call_target="tpu_custom_call" | custom-call | tf_op jit(solution)/shard_map/pallas_call | solution.py:387
  128.5 3.2 %collective-permute-start.47 = (f16[64,2048]{1,0:T(8,128)(2,1)S(1)}, f16[64,2048]{1,0:T(8,128)(2,1)S(1)}, u32[]{:S(2)}, u32[]{:S(2)}) collective-permute-start(f16[64,2048]{1,0:T(8,128)(2,1)S(1)} %get-tuple-element.173), channel_id=1, source_target_pairs={{0,6},{2,0},{4,2},{6,4},{1,7},{3,1},{5,3},{7,5},{8,14},{10,8},{12,... | collective-permute-start | bytes 786440 | tf_op jit(solution)/shard_map/ppermute | solution.py:55
  131.7 6.5 %shard_map.78 = (f32[128,2048]{1,0:T(8,128)S(1)}, f32[128,2048]{1,0:T(8,128)S(1)}, f32[128,2048]{1,0:T(8,128)S(1)}) custom-call(f32[8,128]{1,0:T(8,128)S(1)} %get-tuple-element.145.bound, bf16[384,1024]{1,0:T(8,128)(2,1)S(1)} %get-tuple-element.158.mine, bf16[384,1024]{1,0:T(8,128)(2,1)S(1)} %collective-permute-done.48.theirs, ...), custom_call_target="tpu_custom_call" | custom-call | tf_op jit(solution)/shard_map/pallas_call | solution.py:387
  138.5 2.7 %collective-permute-start.50 = (f16[128,2048]{1,0:T(8,128)(2,1)S(1)}, f16[128,2048]{1,0:T(8,128)(2,1)S(1)}, u32[]{:S(2)}, u32[]{:S(2)}) collective-permute-start(f16[128,2048]{1,0:T(8,128)(2,1)S(1)} %pad_maximum_fusion.2), channel_id=1, source_target_pairs={{0,6},{2,0},{4,2},{6,4},{1,7},{3,1},{5,3},{7,5},{8,14},{10,8},{12,... | collective-permute-start | bytes 1572872 | tf_op jit(solution)/shard_map/ppermute | solution.py:55
  142.5 9.3 %collective-permute-done.50 = f16[128,2048]{1,0:T(8,128)(2,1)S(1)} collective-permute-done((f16[128,2048]{1,0:T(8,128)(2,1)S(1)}, f16[128,2048]{1,0:T(8,128)(2,1)S(1)}, u32[]{:S(2)}, u32[]{:S(2)}) %collective-permute-start.50) | collective-permute-done | bytes 524320 | tf_op jit(solution)/shard_map/ppermute | solution.py:55
  151.8 3.2 %collective-permute-done.49 = f16[128,2048]{1,0:T(8,128)(2,1)S(1)} collective-permute-done((f16[128,2048]{1,0:T(8,128)(2,1)S(1)}, f16[128,2048]{1,0:T(8,128)(2,1)S(1)}, u32[]{:S(2)}, u32[]{:S(2)}) %collective-permute-start.49) | collective-permute-done | bytes 524320 | tf_op jit(solution)/shard_map/ppermute | solution.py:51
  (195 shorter events, 65.4 us)
Async XLA Ops:
  3.4 12.3 %collective-permute-start.1 = (bf16[2,64,2048]{2,1,0:T(8,128)(2,1)S(1)}, bf16[2,64,2048]{2,1,0:T(8,128)(2,1)S(1)}, u32[]{:S(2)}, u32[]{:S(2)}) collective-permute-start(bf16[2,64,2048]{2,1,0:T(8,128)(2,1)S(1)} %pad_maximum_fusion.refs_0_), channel_id=1, source_target_pairs={{0,32},{1,9},{2,34},{3,11},{4,36},{5,13},{6,38},{7,15},{8,40},{9,1... | collective-permute-start | bytes 1572872 | tf_op jit(solution)/shard_map/ppermute | solution.py:43
  5.1 10.6 %collective-permute-start.2 = (bf16[2,64,2048]{2,1,0:T(8,128)(2,1)S(1)}, bf16[2,64,2048]{2,1,0:T(8,128)(2,1)S(1)}, u32[]{:S(2)}, u32[]{:S(2)}) collective-permute-start(bf16[2,64,2048]{2,1,0:T(8,128)(2,1)S(1)} %pad_maximum_fusion.refs_0_), channel_id=1, source_target_pairs={{0,96},{1,25},{2,98},{3,27},{4,100},{5,29},{6,102},{7,31},{8,104},... | collective-permute-start | bytes 1572872 | tf_op jit(solution)/shard_map/ppermute | solution.py:43
  15.7 12.5 %collective-permute-start.6 = (bf16[2,32,2048]{2,1,0:T(8,128)(2,1)S(1)}, bf16[2,32,2048]{2,1,0:T(8,128)(2,1)S(1)}, u32[]{:S(2)}, u32[]{:S(2)}) collective-permute-start(bf16[2,32,2048]{2,1,0:T(8,128)(2,1)S(1)} %slice.92), channel_id=1, source_target_pairs={{0,32},{1,9},{2,34},{3,11},{4,36},{5,13},{6,38},{7,15},{8,40},{9,1... | collective-permute-start | bytes 786440 | tf_op jit(solution)/shard_map/ppermute | solution.py:43
  17.1 11.1 %collective-permute-start.7 = (bf16[2,32,2048]{2,1,0:T(8,128)(2,1)S(1)}, bf16[2,32,2048]{2,1,0:T(8,128)(2,1)S(1)}, u32[]{:S(2)}, u32[]{:S(2)}) collective-permute-start(bf16[2,32,2048]{2,1,0:T(8,128)(2,1)S(1)} %slice.93), channel_id=1, source_target_pairs={{0,96},{1,25},{2,98},{3,27},{4,100},{5,29},{6,102},{7,31},{8,104},... | collective-permute-start | bytes 786440 | tf_op jit(solution)/shard_map/ppermute | solution.py:43
  28.9 8.6 %collective-permute-start.11 = (s32[4,4,2,64]{3,2,1,0:T(2,128)S(1)}, s32[4,4,2,64]{3,2,1,0:T(2,128)S(1)}, u32[]{:S(2)}, u32[]{:S(2)}) collective-permute-start(s32[4,4,2,64]{3,2,1,0:T(2,128)S(1)} %pad_add_fusion.1), channel_id=1, source_target_pairs={{0,8},{1,33},{2,10},{3,35},{4,12},{5,37},{6,14},{7,39},{8,16},{9,4... | collective-permute-start | bytes 24584 | tf_op jit(solution)/shard_map/ppermute | solution.py:43
  38.4 27.4 %collective-permute-start.14 = (bf16[2,256,2048]{2,1,0:T(8,128)(2,1)S(1)}, bf16[2,256,2048]{2,1,0:T(8,128)(2,1)}, u32[]{:S(2)}, u32[]{:S(2)}) collective-permute-start(bf16[2,256,2048]{2,1,0:T(8,128)(2,1)S(1)} %shard_map.67.refs_1_.refs_0_), channel_id=1, source_target_pairs={{0,8},{1,33},{2,10},{3,35},{4,12},{5,37},{6,14},{7,39},{8,16},{9,4... | collective-permute-start | bytes 6291464 | tf_op jit(solution)/shard_map/ppermute | solution.py:43
  38.6 27.2 %collective-permute-start.15 = (bf16[2,256,2048]{2,1,0:T(8,128)(2,1)S(1)}, bf16[2,256,2048]{2,1,0:T(8,128)(2,1)}, u32[]{:S(2)}, u32[]{:S(2)}) collective-permute-start(bf16[2,256,2048]{2,1,0:T(8,128)(2,1)S(1)} %shard_map.67.refs_1_.refs_0_), channel_id=1, source_target_pairs={{0,24},{1,97},{2,26},{3,99},{4,28},{5,101},{6,30},{7,103},{8,0},{9... | collective-permute-start | bytes 6291464 | tf_op jit(solution)/shard_map/ppermute | solution.py:43
  41.7 10.4 %collective-permute-start.16 = (bf16[2,64,2048]{2,1,0:T(8,128)(2,1)S(1)}, bf16[2,64,2048]{2,1,0:T(8,128)(2,1)S(1)}, u32[]{:S(2)}, u32[]{:S(2)}) collective-permute-start(bf16[2,64,2048]{2,1,0:T(8,128)(2,1)S(1)} %pad_maximum_fusion.refs_0_), channel_id=1, source_target_pairs={{0,2},{2,4},{4,6},{6,0},{1,3},{3,5},{5,7},{7,1},{8,10},{10,12},{12... | collective-permute-start | bytes 1572872 | tf_op jit(solution)/shard_map/ppermute | solution.py:51
  42.0 10.9 %collective-permute-start.17 = (bf16[2,64,2048]{2,1,0:T(8,128)(2,1)S(1)}, bf16[2,64,2048]{2,1,0:T(8,128)(2,1)}, u32[]{:S(2)}, u32[]{:S(2)}) collective-permute-start(bf16[2,64,2048]{2,1,0:T(8,128)(2,1)S(1)} %pad_maximum_fusion.refs_0_), channel_id=1, source_target_pairs={{0,6},{2,0},{4,2},{6,4},{1,7},{3,1},{5,3},{7,5},{8,14},{10,8},{12,... | collective-permute-start | bytes 1572872 | tf_op jit(solution)/shard_map/ppermute | solution.py:55
  44.9 16.8 %collective-permute-start.20 = (bf16[2,64,2048]{2,1,0:T(8,128)(2,1)S(1)}, bf16[2,64,2048]{2,1,0:T(8,128)(2,1)}, u32[]{:S(2)}, u32[]{:S(2)}) collective-permute-start(bf16[2,64,2048]{2,1,0:T(8,128)(2,1)S(1)} %pad_maximum_fusion.refs_0_), channel_id=1, source_target_pairs={{0,1},{1,0},{2,3},{3,2},{4,5},{5,4},{6,7},{7,6},{8,9},{9,8},{10,11... | collective-permute-start | bytes 1572872 | tf_op jit(solution)/shard_map/ppermute | solution.py:47
  52.8 7.8 %collective-permute-start.18 = (bf16[2,32,2048]{2,1,0:T(8,128)(2,1)}, bf16[2,32,2048]{2,1,0:T(8,128)(2,1)S(1)}, u32[]{:S(2)}, u32[]{:S(2)}) collective-permute-start(bf16[2,32,2048]{2,1,0:T(8,128)(2,1)} %slice.128), channel_id=1, source_target_pairs={{0,2},{2,4},{4,6},{6,0},{1,3},{3,5},{5,7},{7,1},{8,10},{10,12},{12... | collective-permute-start | bytes 786440 | tf_op jit(solution)/shard_map/ppermute | solution.py:51
  54.6 7.6 %collective-permute-start.19 = (bf16[2,32,2048]{2,1,0:T(8,128)(2,1)}, bf16[2,32,2048]{2,1,0:T(8,128)(2,1)}, u32[]{:S(2)}, u32[]{:S(2)}) collective-permute-start(bf16[2,32,2048]{2,1,0:T(8,128)(2,1)} %slice.129), channel_id=1, source_target_pairs={{0,6},{2,0},{4,2},{6,4},{1,7},{3,1},{5,3},{7,5},{8,14},{10,8},{12,... | collective-permute-start | bytes 786440 | tf_op jit(solution)/shard_map/ppermute | solution.py:55
  67.0 19.0 %collective-permute-start.25 = (bf16[2,128,2048]{2,1,0:T(8,128)(2,1)S(1)}, bf16[2,128,2048]{2,1,0:T(8,128)(2,1)S(1)}, u32[]{:S(2)}, u32[]{:S(2)}) collective-permute-start(bf16[2,128,2048]{2,1,0:T(8,128)(2,1)S(1)} %shard_map.68), channel_id=1, source_target_pairs={{0,8},{1,33},{2,10},{3,35},{4,12},{5,37},{6,14},{7,39},{8,16},{9,4... | collective-permute-start | bytes 3145736 | tf_op jit(solution)/shard_map/ppermute | solution.py:43
  68.8 17.2 %collective-permute-start.26 = (bf16[2,128,2048]{2,1,0:T(8,128)(2,1)S(1)}, bf16[2,128,2048]{2,1,0:T(8,128)(2,1)}, u32[]{:S(2)}, u32[]{:S(2)}) collective-permute-start(bf16[2,128,2048]{2,1,0:T(8,128)(2,1)S(1)} %shard_map.69), channel_id=1, source_target_pairs={{0,24},{1,97},{2,26},{3,99},{4,28},{5,101},{6,30},{7,103},{8,0},{9... | collective-permute-start | bytes 3145736 | tf_op jit(solution)/shard_map/ppermute | solution.py:43
  75.7 18.6 %collective-permute-start.27 = (bf16[2,256,2048]{2,1,0:T(8,128)(2,1)S(1)}, bf16[2,256,2048]{2,1,0:T(8,128)(2,1)}, u32[]{:S(2)}, u32[]{:S(2)}) collective-permute-start(bf16[2,256,2048]{2,1,0:T(8,128)(2,1)S(1)} %shard_map.67.refs_1_.refs_0_), channel_id=1, source_target_pairs={{0,1},{1,0},{2,3},{3,2},{4,5},{5,4},{6,7},{7,6},{8,9},{9,8},{10,11... | collective-permute-start | bytes 6291464 | tf_op jit(solution)/shard_map/ppermute | solution.py:47
  75.8 18.5 %collective-permute-start.28 = (bf16[2,256,2048]{2,1,0:T(8,128)(2,1)}, bf16[2,256,2048]{2,1,0:T(8,128)(2,1)}, u32[]{:S(2)}, u32[]{:S(2)}) collective-permute-start(bf16[2,256,2048]{2,1,0:T(8,128)(2,1)} %collective-permute-done.14.refs_0_.refs_2_.refs_1_), channel_id=1, source_target_pairs={{0,1},{1,0},{2,3},{3,2},{4,5},{5,4},{6,7},{7,6},{8,9},{9,8},{10,11... | collective-permute-start | bytes 6291464 | tf_op jit(solution)/shard_map/ppermute | solution.py:47
  76.3 18.0 %collective-permute-start.29 = (bf16[2,256,2048]{2,1,0:T(8,128)(2,1)}, bf16[2,256,2048]{2,1,0:T(8,128)(2,1)}, u32[]{:S(2)}, u32[]{:S(2)}) collective-permute-start(bf16[2,256,2048]{2,1,0:T(8,128)(2,1)} %collective-permute-done.15.refs_0_.refs_3_.refs_2_), channel_id=1, source_target_pairs={{0,1},{1,0},{2,3},{3,2},{4,5},{5,4},{6,7},{7,6},{8,9},{9,8},{10,11... | collective-permute-start | bytes 6291464 | tf_op jit(solution)/shard_map/ppermute | solution.py:47
  86.0 8.4 %collective-permute-start.30 = (bf16[2,128,2048]{2,1,0:T(8,128)(2,1)S(1)}, bf16[2,128,2048]{2,1,0:T(8,128)(2,1)}, u32[]{:S(2)}, u32[]{:S(2)}) collective-permute-start(bf16[2,128,2048]{2,1,0:T(8,128)(2,1)S(1)} %collective-permute-done.25.refs_1_.refs_3_), channel_id=1, source_target_pairs={{0,1},{1,0},{2,3},{3,2},{4,5},{5,4},{6,7},{7,6},{8,9},{9,8},{10,11... | collective-permute-start | bytes 3145736 | tf_op jit(solution)/shard_map/ppermute | solution.py:47
  86.0 8.4 %collective-permute-start.31 = (bf16[2,128,2048]{2,1,0:T(8,128)(2,1)}, bf16[2,128,2048]{2,1,0:T(8,128)(2,1)}, u32[]{:S(2)}, u32[]{:S(2)}) collective-permute-start(bf16[2,128,2048]{2,1,0:T(8,128)(2,1)} %collective-permute-done.26.refs_2_.refs_4_), channel_id=1, source_target_pairs={{0,1},{1,0},{2,3},{3,2},{4,5},{5,4},{6,7},{7,6},{8,9},{9,8},{10,11... | collective-permute-start | bytes 3145736 | tf_op jit(solution)/shard_map/ppermute | solution.py:47
  123.2 8.4 %collective-permute-start.48 = (bf16[384,1024]{1,0:T(8,128)(2,1)S(1)}, bf16[384,1024]{1,0:T(8,128)(2,1)S(1)}, u32[]{:S(2)}, u32[]{:S(2)}) collective-permute-start(bf16[384,1024]{1,0:T(8,128)(2,1)S(1)} %get-tuple-element.158.mine), channel_id=1, source_target_pairs={{0,1},{1,0},{2,3},{3,2},{4,5},{5,4},{6,7},{7,6},{8,9},{9,8},{10,11... | collective-permute-start | bytes 2359304 | tf_op jit(solution)/shard_map/ppermute | solution.py:47
  128.4 9.8 %collective-permute-start.46 = (f16[64,2048]{1,0:T(8,128)(2,1)S(1)}, f16[64,2048]{1,0:T(8,128)(2,1)S(1)}, u32[]{:S(2)}, u32[]{:S(2)}) collective-permute-start(f16[64,2048]{1,0:T(8,128)(2,1)S(1)} %get-tuple-element.174), channel_id=1, source_target_pairs={{0,2},{2,4},{4,6},{6,0},{1,3},{3,5},{5,7},{7,1},{8,10},{10,12},{12... | collective-permute-start | bytes 786440 | tf_op jit(solution)/shard_map/ppermute | solution.py:51
  128.5 9.8 %collective-permute-start.47 = (f16[64,2048]{1,0:T(8,128)(2,1)S(1)}, f16[64,2048]{1,0:T(8,128)(2,1)S(1)}, u32[]{:S(2)}, u32[]{:S(2)}) collective-permute-start(f16[64,2048]{1,0:T(8,128)(2,1)S(1)} %get-tuple-element.173), channel_id=1, source_target_pairs={{0,6},{2,0},{4,2},{6,4},{1,7},{3,1},{5,3},{7,5},{8,14},{10,8},{12,... | collective-permute-start | bytes 786440 | tf_op jit(solution)/shard_map/ppermute | solution.py:55
  138.5 13.3 %collective-permute-start.50 = (f16[128,2048]{1,0:T(8,128)(2,1)S(1)}, f16[128,2048]{1,0:T(8,128)(2,1)S(1)}, u32[]{:S(2)}, u32[]{:S(2)}) collective-permute-start(f16[128,2048]{1,0:T(8,128)(2,1)S(1)} %pad_maximum_fusion.2), channel_id=1, source_target_pairs={{0,6},{2,0},{4,2},{6,4},{1,7},{3,1},{5,3},{7,5},{8,14},{10,8},{12,... | collective-permute-start | bytes 1572872 | tf_op jit(solution)/shard_map/ppermute | solution.py:55
  141.4 13.7 %collective-permute-start.49 = (f16[128,2048]{1,0:T(8,128)(2,1)S(1)}, f16[128,2048]{1,0:T(8,128)(2,1)S(1)}, u32[]{:S(2)}, u32[]{:S(2)}) collective-permute-start(f16[128,2048]{1,0:T(8,128)(2,1)S(1)} %pad_maximum_fusion.1), channel_id=1, source_target_pairs={{0,2},{2,4},{4,6},{6,0},{1,3},{3,5},{5,7},{7,1},{8,10},{10,12},{12... | collective-permute-start | bytes 1572872 | tf_op jit(solution)/shard_map/ppermute | solution.py:51
  (45 other events, 222.9 us)

commit v8 on v7

--- a/solution.py
+++ b/solution.py
@@ -475,14 +475,16 @@
     args = (parts, rows, cols, lse_i, plane)
     m_far, bound = weights_of(3, 1, core, *args)
     m_far_o = swap(m_far)
-    m_rest, _ = weights_of(0, 3, after(core, m_far), *args)
+    m_near, _ = weights_of(1, 2, after(core, m_far), *args)
     (opposite,) = product_of(0, bound, m_far, m_far_o, blocks, others)
     opposite = opposite.astype(f16)
-    got_q, got_p, here, to_down, to_up = settle(
-        up(opposite[:N]), down(opposite[N:]), *product_of(1, bound, m_rest, swap(m_rest), blocks, others)
+    got_q, got_p, to_down, to_up = settle(
+        up(opposite[:N]), down(opposite[N:]), *product_of(0, bound, m_near, swap(m_near), blocks, others)
     )
     below = up(jnp.concatenate([to_up[:N] + got_q.astype(f32), to_up[N:]]).astype(f16))
     above = down(jnp.concatenate([to_down[:N], to_down[N:] + got_p.astype(f32)]).astype(f16))
+    m_own, _ = weights_of(0, 1, after(core, to_up), *args)
+    (here,) = product_of(1, bound, m_own, swap(m_own), blocks, others)
     grad = here + (below.astype(f32) + above.astype(f32)) * bound[0, 0]
     grad_q, grad_p = grad[:N], grad[N:]
     return loss, grad_q, grad_p

time: 158 us -> 157 us (level)
  waiting for transfers between devices: 43.4 us -> 38.8 us
  Pallas kernels: 30.4 us -> 34.4 us
    ppermute x6, waiting for transfers between devices: 9.33 us -> 2.94 us  [down(): return lax.ppermute(value, 'x', DOWN)]
    pallas_call x2 -> x3, Pallas kernels: 11 us -> 14.3 us  [product_of(): pl.pallas_call(functools.partial(product_kernel, scaled), out_shape=[jax....]
    ppermute x17 -> x18, waiting for transfers between devices: 3.56 us -> 4.13 us  [swap(): return lax.ppermute(value, 'w', [(0, 1), (1, 0)])]
    ppermute x17 -> x18, starting transfers between devices: 3.47 us -> 3.47 us  [swap(): return lax.ppermute(value, 'w', [(0, 1), (1, 0)])]
  transfers between devices with their start and end apart: 51 -> 52, of which waited for: 18 -> 20; matrix products, arithmetic and copies ran while one was open for 7% -> 7% of each run, Pallas kernels for 18% -> 21%
where the time goes in v8:
time: 157 us
  starting transfers between devices  55.4 us (35%)
  waiting for transfers between devices  38.8 us (25%)
  Pallas kernels  34.4 us (22%)
  local copies, waits for them, and re-layouts  17.5 us (11%)
  other arithmetic  8.26 us (5%)
  between operations  2.3 us (1%)
    ppermute x20, starting transfers between devices, along(): return lax.ppermute(value, GRID, moves)  29.8 us
    ppermute x6, starting transfers between devices, down(): return lax.ppermute(value, 'x', DOWN)  17 us
    ppermute x20, waiting for transfers between devices, along(): return lax.ppermute(value, GRID, moves)  16.2 us
    pallas_call x3, Pallas kernels, product_of(): pl.pallas_call(functools.partial(product_kernel, scaled), out_shape=[jax....  14.3 us
    unnamed x41, local copies, waits for them, and re-layouts  10.9 us
    pallas_call x2, Pallas kernels, scores_of(): pl.pallas_call(functools.partial(scores_kernel, plan), out_shape=[jax.Sha...  9.92 us
    ppermute x6, waiting for transfers between devices, up(): return lax.ppermute(value, 'x', UP)  9.37 us
    ppermute x2, waiting for transfers between devices, far(): return lax.ppermute(value, 'x', FAR)  6.18 us
  transfers between devices with their start and end apart: 52, of which 20 were waited for; matrix products, arithmetic and copies ran while one was open for 7% of the time, Pallas kernels for 21%

profile of v8, /device:TPU:0, one launch (start us, length us, event | category | flops | bytes accessed | tf_op | source)
XLA Modules:
  0.0 156.7 jit_solution(14122495257129084792)
XLA Ops:
  12.5 3.2 %collective-permute-done.5 = s32[2,64]{1,0:T(2,128)S(1)} collective-permute-done((s32[2,64]{1,0:T(2,128)S(1)}, s32[2,64]{1,0:T(2,128)S(1)}, u32[]{:S(2)}, u32[]{:S(2)}) %collective-permute-start.5) | collective-permute-done | bytes 544 | tf_op jit(solution)/shard_map/ppermute | solution.py:59
  17.1 2.8 %collective-permute-start.7 = (bf16[2,32,2048]{2,1,0:T(8,128)(2,1)S(1)}, bf16[2,32,2048]{2,1,0:T(8,128)(2,1)S(1)}, u32[]{:S(2)}, u32[]{:S(2)}) collective-permute-start(bf16[2,32,2048]{2,1,0:T(8,128)(2,1)S(1)} %slice.93), channel_id=1, source_target_pairs={{0,96},{1,25},{2,98},{3,27},{4,100},{5,29},{6,102},{7,31},{8,104},... | collective-permute-start | bytes 786440 | tf_op jit(solution)/shard_map/ppermute | solution.py:43
  19.9 3.2 %collective-permute-start.9 = (s32[4,2,64]{2,1,0:T(2,128)S(1)}, s32[4,2,64]{2,1,0:T(2,128)S(1)}, u32[]{:S(2)}, u32[]{:S(2)}) collective-permute-start(s32[4,2,64]{2,1,0:T(2,128)S(1)} %pad_add_fusion.2), channel_id=1, source_target_pairs={{0,96},{1,25},{2,98},{3,27},{4,100},{5,29},{6,102},{7,31},{8,104},... | collective-permute-start | bytes 6152 | tf_op jit(solution)/shard_map/ppermute | solution.py:43
  24.7 3.5 %collective-permute-done.10 = s32[4,2,64]{2,1,0:T(2,128)S(1)} collective-permute-done((s32[4,2,64]{2,1,0:T(2,128)S(1)}, s32[4,2,64]{2,1,0:T(2,128)S(1)}, u32[]{:S(2)}, u32[]{:S(2)}) %collective-permute-start.10) | collective-permute-done | bytes 2080 | tf_op jit(solution)/shard_map/ppermute | solution.py:43
  38.6 3.1 %collective-permute-start.15 = (bf16[2,256,2048]{2,1,0:T(8,128)(2,1)S(1)}, bf16[2,256,2048]{2,1,0:T(8,128)(2,1)}, u32[]{:S(2)}, u32[]{:S(2)}) collective-permute-start(bf16[2,256,2048]{2,1,0:T(8,128)(2,1)S(1)} %shard_map.67.refs_1_.refs_0_), channel_id=1, source_target_pairs={{0,24},{1,97},{2,26},{3,99},{4,28},{5,101},{6,30},{7,103},{8,0},{9... | collective-permute-start | bytes 6291464 | tf_op jit(solution)/shard_map/ppermute | solution.py:43
  42.0 2.9 %collective-permute-start.17 = (bf16[2,64,2048]{2,1,0:T(8,128)(2,1)S(1)}, bf16[2,64,2048]{2,1,0:T(8,128)(2,1)}, u32[]{:S(2)}, u32[]{:S(2)}) collective-permute-start(bf16[2,64,2048]{2,1,0:T(8,128)(2,1)S(1)} %pad_maximum_fusion.refs_0_), channel_id=1, source_target_pairs={{0,6},{2,0},{4,2},{6,4},{1,7},{3,1},{5,3},{7,5},{8,14},{10,8},{12,... | collective-permute-start | bytes 1572872 | tf_op jit(solution)/shard_map/ppermute | solution.py:55
  49.1 3.0 %collective-permute-done.16.refs_1_ = bf16[2,64,2048]{2,1,0:T(8,128)(2,1)S(1)} collective-permute-done((bf16[2,64,2048]{2,1,0:T(8,128)(2,1)S(1)}, bf16[2,64,2048]{2,1,0:T(8,128)(2,1)S(1)}, u32[]{:S(2)}, u32[]{:S(2)}) %collective-permute-start.16) | collective-permute-done | bytes 524320 | tf_op jit(solution)/shard_map/ppermute | solution.py:51
  54.6 3.2 %collective-permute-start.19 = (bf16[2,32,2048]{2,1,0:T(8,128)(2,1)}, bf16[2,32,2048]{2,1,0:T(8,128)(2,1)}, u32[]{:S(2)}, u32[]{:S(2)}) collective-permute-start(bf16[2,32,2048]{2,1,0:T(8,128)(2,1)} %slice.129), channel_id=1, source_target_pairs={{0,6},{2,0},{4,2},{6,4},{1,7},{3,1},{5,3},{7,5},{8,14},{10,8},{12,... | collective-permute-start | bytes 786440 | tf_op jit(solution)/shard_map/ppermute | solution.py:55
  68.9 2.8 %collective-permute-start.26 = (bf16[2,128,2048]{2,1,0:T(8,128)(2,1)S(1)}, bf16[2,128,2048]{2,1,0:T(8,128)(2,1)}, u32[]{:S(2)}, u32[]{:S(2)}) collective-permute-start(bf16[2,128,2048]{2,1,0:T(8,128)(2,1)S(1)} %shard_map.69), channel_id=1, source_target_pairs={{0,24},{1,97},{2,26},{3,99},{4,28},{5,101},{6,30},{7,103},{8,0},{9... | collective-permute-start | bytes 3145736 | tf_op jit(solution)/shard_map/ppermute | solution.py:43
  76.4 7.2 %shard_map.71 = (f32[512,256]{1,0:T(8,128)S(1)}, f32[512,256]{1,0:T(8,128)S(1)}, f32[512,256]{1,0:T(8,128)S(1)}) custom-call(bf16[2,512,2048]{2,1,0:T(8,128)(2,1)S(1)} %shard_map.70.refs_0_, bf16[2,256,2048]{2,1,0:T(8,128)(2,1)S(1)} %shard_map.67.refs_1_.refs_0_, bf16[2,256,2048]{2,1,0:T(8,128)(2,1)} %collective-permute-done.14.refs_0_.refs_2_.refs_1_, ...), custom_call_target="tpu_custom_call" | custom-call | tf_op jit(solution)/shard_map/pallas_call | solution.py:182
  88.8 2.8 %shard_map.72 = (f32[512,128]{1,0:T(8,128)S(1)}, f32[512,128]{1,0:T(8,128)S(1)}) custom-call(bf16[2,512,2048]{2,1,0:T(8,128)(2,1)S(1)} %copy-done.1, bf16[2,128,2048]{2,1,0:T(8,128)(2,1)S(1)} %collective-permute-done.25.refs_1_.refs_3_, bf16[2,128,2048]{2,1,0:T(8,128)(2,1)} %collective-permute-done.26.refs_2_.refs_4_), custom_call_target="tpu_custom_call" | custom-call | tf_op jit(solution)/shard_map/pallas_call | solution.py:182
  94.8 2.9 %collective-permute-start.33 = (f32[16,128]{1,0:T(8,128)S(1)}, f32[16,128]{1,0:T(8,128)S(1)}, u32[]{:S(2)}, u32[]{:S(2)}) collective-permute-start(f32[16,128]{1,0:T(8,128)S(1)} %shard_map.73.refs_0_), channel_id=1, source_target_pairs={{0,6},{2,0},{4,2},{6,4},{1,7},{3,1},{5,3},{7,5},{8,14},{10,8},{12,... | collective-permute-start | bytes 24584 | tf_op jit(solution)/shard_map/ppermute | solution.py:55
  99.9 3.0 %collective-permute-done.34.refs_3_ = f32[16,128]{1,0:T(8,128)S(1)} collective-permute-done((f32[16,128]{1,0:T(8,128)S(1)}, f32[16,128]{1,0:T(8,128)S(1)}, u32[]{:S(2)}, u32[]{:S(2)}) %collective-permute-start.34) | collective-permute-done | bytes 8224 | tf_op jit(solution)/shard_map/ppermute | solution.py:59
  104.2 3.2 %collective-permute-start.40 = (f32[8,128]{1,0:T(8,128)S(1)}, f32[8,128]{1,0:T(8,128)S(1)}, u32[]{:S(2)}, u32[]{:S(2)}) collective-permute-start(f32[8,128]{1,0:T(8,128)S(1)} %get-tuple-element.144), channel_id=1, source_target_pairs={{0,96},{1,25},{2,98},{3,27},{4,100},{5,29},{6,102},{7,31},{8,104},... | collective-permute-start | bytes 12296 | tf_op jit(solution)/shard_map/ppermute | solution.py:43
  109.0 3.5 %collective-permute-done.41 = f32[8,128]{1,0:T(8,128)S(1)} collective-permute-done((f32[8,128]{1,0:T(8,128)S(1)}, f32[8,128]{1,0:T(8,128)S(1)}, u32[]{:S(2)}, u32[]{:S(2)}) %collective-permute-start.41) | collective-permute-done | bytes 4128 | tf_op jit(solution)/shard_map/ppermute | solution.py:43
  112.5 3.2 %collective-permute-start.43 = (f32[32,128]{1,0:T(8,128)S(1)}, f32[32,128]{1,0:T(8,128)S(1)}, u32[]{:S(2)}, u32[]{:S(2)}) collective-permute-start(f32[32,128]{1,0:T(8,128)S(1)} %constant_dynamic-update-slice_fusion.4.refs_8_), channel_id=1, source_target_pairs={{0,24},{1,97},{2,26},{3,99},{4,28},{5,101},{6,30},{7,103},{8,0},{9... | collective-permute-start | bytes 49160 | tf_op jit(solution)/shard_map/ppermute | solution.py:43
  117.5 3.5 %collective-permute-done.44.refs_11_ = f32[32,128]{1,0:T(8,128)S(1)} collective-permute-done((f32[32,128]{1,0:T(8,128)S(1)}, f32[32,128]{1,0:T(8,128)S(1)}, u32[]{:S(2)}, u32[]{:S(2)}) %collective-permute-start.44) | collective-permute-done | bytes 16416 | tf_op jit(solution)/shard_map/ppermute | solution.py:43
  123.4 4.4 %shard_map.76 = f32[128,2048]{1,0:T(8,128)S(1)} custom-call(f32[8,128]{1,0:T(8,128)S(1)} %get-tuple-element.145.bound, bf16[128,1024]{1,0:T(8,128)(2,1)S(1)} %get-tuple-element.146.mine, bf16[128,1024]{1,0:T(8,128)(2,1)S(1)} %collective-permute-done.45.theirs, bf16[2,256,2048]{2,1,0:T(8,128)(2,1)S(1)} %shard_map.67.refs_1_.refs_0_, ...), custom_call_target="tpu_custom_call" | custom-call | tf_op jit(solution)/shard_map/pallas_call | solution.py:387
  128.1 3.2 %collective-permute-start.47 = (f16[64,2048]{1,0:T(8,128)(2,1)S(1)}, f16[64,2048]{1,0:T(8,128)(2,1)S(1)}, u32[]{:S(2)}, u32[]{:S(2)}) collective-permute-start(f16[64,2048]{1,0:T(8,128)(2,1)S(1)} %get-tuple-element.173), channel_id=1, source_target_pairs={{0,6},{2,0},{4,2},{6,4},{1,7},{3,1},{5,3},{7,5},{8,14},{10,8},{12,... | collective-permute-start | bytes 786440 | tf_op jit(solution)/shard_map/ppermute | solution.py:55
  131.3 5.4 %shard_map.78 = (f32[128,2048]{1,0:T(8,128)S(1)}, f32[128,2048]{1,0:T(8,128)S(1)}) custom-call(f32[8,128]{1,0:T(8,128)S(1)} %get-tuple-element.145.bound, bf16[256,1024]{1,0:T(8,128)(2,1)S(1)} %get-tuple-element.158.mine, bf16[256,1024]{1,0:T(8,128)(2,1)S(1)} %collective-permute-done.48.theirs, bf16[2,256,2048]{2,1,0:T(8,128)(2,1)S(1)} %shard_map.67.refs_1_.refs_0_, ...), custom_call_target="tpu_custom_call" | custom-call | tf_op jit(solution)/shard_map/pallas_call | solution.py:387
  137.8 3.0 %collective-permute-start.51 = (f16[128,2048]{1,0:T(8,128)(2,1)S(1)}, f16[128,2048]{1,0:T(8,128)(2,1)S(1)}, u32[]{:S(2)}, u32[]{:S(2)}) collective-permute-start(f16[128,2048]{1,0:T(8,128)(2,1)S(1)} %pad_maximum_fusion.2), channel_id=1, source_target_pairs={{0,6},{2,0},{4,2},{6,4},{1,7},{3,1},{5,3},{7,5},{8,14},{10,8},{12,... | collective-permute-start | bytes 1572872 | tf_op jit(solution)/shard_map/ppermute | solution.py:55
  143.7 4.4 %shard_map.80 = f32[128,2048]{1,0:T(8,128)S(1)} custom-call(f32[8,128]{1,0:T(8,128)S(1)} %get-tuple-element.145.bound, bf16[128,1024]{1,0:T(8,128)(2,1)S(1)} %get-tuple-element.163.mine, bf16[128,1024]{1,0:T(8,128)(2,1)S(1)} %collective-permute-done.49.theirs, bf16[2,256,2048]{2,1,0:T(8,128)(2,1)S(1)} %shard_map.67.refs_1_.refs_0_, ...), custom_call_target="tpu_custom_call" | custom-call | tf_op jit(solution)/shard_map/pallas_call | solution.py:387
  148.1 2.9 %collective-permute-done.51 = f16[128,2048]{1,0:T(8,128)(2,1)S(1)} collective-permute-done((f16[128,2048]{1,0:T(8,128)(2,1)S(1)}, f16[128,2048]{1,0:T(8,128)(2,1)S(1)}, u32[]{:S(2)}, u32[]{:S(2)}) %collective-permute-start.51) | collective-permute-done | bytes 524320 | tf_op jit(solution)/shard_map/ppermute | solution.py:55
  151.0 3.7 %collective-permute-done.50 = f16[128,2048]{1,0:T(8,128)(2,1)S(1)} collective-permute-done((f16[128,2048]{1,0:T(8,128)(2,1)S(1)}, f16[128,2048]{1,0:T(8,128)(2,1)S(1)}, u32[]{:S(2)}, u32[]{:S(2)}) %collective-permute-start.50) | collective-permute-done | bytes 524320 | tf_op jit(solution)/shard_map/ppermute | solution.py:51
  (199 shorter events, 70.1 us)
Async XLA Ops:
  3.4 12.3 %collective-permute-start.1 = (bf16[2,64,2048]{2,1,0:T(8,128)(2,1)S(1)}, bf16[2,64,2048]{2,1,0:T(8,128)(2,1)S(1)}, u32[]{:S(2)}, u32[]{:S(2)}) collective-permute-start(bf16[2,64,2048]{2,1,0:T(8,128)(2,1)S(1)} %pad_maximum_fusion.refs_0_), channel_id=1, source_target_pairs={{0,32},{1,9},{2,34},{3,11},{4,36},{5,13},{6,38},{7,15},{8,40},{9,1... | collective-permute-start | bytes 1572872 | tf_op jit(solution)/shard_map/ppermute | solution.py:43
  5.1 10.6 %collective-permute-start.2 = (bf16[2,64,2048]{2,1,0:T(8,128)(2,1)S(1)}, bf16[2,64,2048]{2,1,0:T(8,128)(2,1)S(1)}, u32[]{:S(2)}, u32[]{:S(2)}) collective-permute-start(bf16[2,64,2048]{2,1,0:T(8,128)(2,1)S(1)} %pad_maximum_fusion.refs_0_), channel_id=1, source_target_pairs={{0,96},{1,25},{2,98},{3,27},{4,100},{5,29},{6,102},{7,31},{8,104},... | collective-permute-start | bytes 1572872 | tf_op jit(solution)/shard_map/ppermute | solution.py:43
  15.7 12.5 %collective-permute-start.6 = (bf16[2,32,2048]{2,1,0:T(8,128)(2,1)S(1)}, bf16[2,32,2048]{2,1,0:T(8,128)(2,1)S(1)}, u32[]{:S(2)}, u32[]{:S(2)}) collective-permute-start(bf16[2,32,2048]{2,1,0:T(8,128)(2,1)S(1)} %slice.92), channel_id=1, source_target_pairs={{0,32},{1,9},{2,34},{3,11},{4,36},{5,13},{6,38},{7,15},{8,40},{9,1... | collective-permute-start | bytes 786440 | tf_op jit(solution)/shard_map/ppermute | solution.py:43
  17.1 11.1 %collective-permute-start.7 = (bf16[2,32,2048]{2,1,0:T(8,128)(2,1)S(1)}, bf16[2,32,2048]{2,1,0:T(8,128)(2,1)S(1)}, u32[]{:S(2)}, u32[]{:S(2)}) collective-permute-start(bf16[2,32,2048]{2,1,0:T(8,128)(2,1)S(1)} %slice.93), channel_id=1, source_target_pairs={{0,96},{1,25},{2,98},{3,27},{4,100},{5,29},{6,102},{7,31},{8,104},... | collective-permute-start | bytes 786440 | tf_op jit(solution)/shard_map/ppermute | solution.py:43
  28.9 8.6 %collective-permute-start.11 = (s32[4,4,2,64]{3,2,1,0:T(2,128)S(1)}, s32[4,4,2,64]{3,2,1,0:T(2,128)S(1)}, u32[]{:S(2)}, u32[]{:S(2)}) collective-permute-start(s32[4,4,2,64]{3,2,1,0:T(2,128)S(1)} %pad_add_fusion.1), channel_id=1, source_target_pairs={{0,8},{1,33},{2,10},{3,35},{4,12},{5,37},{6,14},{7,39},{8,16},{9,4... | collective-permute-start | bytes 24584 | tf_op jit(solution)/shard_map/ppermute | solution.py:43
  38.4 27.4 %collective-permute-start.14 = (bf16[2,256,2048]{2,1,0:T(8,128)(2,1)S(1)}, bf16[2,256,2048]{2,1,0:T(8,128)(2,1)}, u32[]{:S(2)}, u32[]{:S(2)}) collective-permute-start(bf16[2,256,2048]{2,1,0:T(8,128)(2,1)S(1)} %shard_map.67.refs_1_.refs_0_), channel_id=1, source_target_pairs={{0,8},{1,33},{2,10},{3,35},{4,12},{5,37},{6,14},{7,39},{8,16},{9,4... | collective-permute-start | bytes 6291464 | tf_op jit(solution)/shard_map/ppermute | solution.py:43
  38.6 27.2 %collective-permute-start.15 = (bf16[2,256,2048]{2,1,0:T(8,128)(2,1)S(1)}, bf16[2,256,2048]{2,1,0:T(8,128)(2,1)}, u32[]{:S(2)}, u32[]{:S(2)}) collective-permute-start(bf16[2,256,2048]{2,1,0:T(8,128)(2,1)S(1)} %shard_map.67.refs_1_.refs_0_), channel_id=1, source_target_pairs={{0,24},{1,97},{2,26},{3,99},{4,28},{5,101},{6,30},{7,103},{8,0},{9... | collective-permute-start | bytes 6291464 | tf_op jit(solution)/shard_map/ppermute | solution.py:43
  41.7 10.4 %collective-permute-start.16 = (bf16[2,64,2048]{2,1,0:T(8,128)(2,1)S(1)}, bf16[2,64,2048]{2,1,0:T(8,128)(2,1)S(1)}, u32[]{:S(2)}, u32[]{:S(2)}) collective-permute-start(bf16[2,64,2048]{2,1,0:T(8,128)(2,1)S(1)} %pad_maximum_fusion.refs_0_), channel_id=1, source_target_pairs={{0,2},{2,4},{4,6},{6,0},{1,3},{3,5},{5,7},{7,1},{8,10},{10,12},{12... | collective-permute-start | bytes 1572872 | tf_op jit(solution)/shard_map/ppermute | solution.py:51
  42.0 10.9 %collective-permute-start.17 = (bf16[2,64,2048]{2,1,0:T(8,128)(2,1)S(1)}, bf16[2,64,2048]{2,1,0:T(8,128)(2,1)}, u32[]{:S(2)}, u32[]{:S(2)}) collective-permute-start(bf16[2,64,2048]{2,1,0:T(8,128)(2,1)S(1)} %pad_maximum_fusion.refs_0_), channel_id=1, source_target_pairs={{0,6},{2,0},{4,2},{6,4},{1,7},{3,1},{5,3},{7,5},{8,14},{10,8},{12,... | collective-permute-start | bytes 1572872 | tf_op jit(solution)/shard_map/ppermute | solution.py:55
  44.9 16.8 %collective-permute-start.20 = (bf16[2,64,2048]{2,1,0:T(8,128)(2,1)S(1)}, bf16[2,64,2048]{2,1,0:T(8,128)(2,1)}, u32[]{:S(2)}, u32[]{:S(2)}) collective-permute-start(bf16[2,64,2048]{2,1,0:T(8,128)(2,1)S(1)} %pad_maximum_fusion.refs_0_), channel_id=1, source_target_pairs={{0,1},{1,0},{2,3},{3,2},{4,5},{5,4},{6,7},{7,6},{8,9},{9,8},{10,11... | collective-permute-start | bytes 1572872 | tf_op jit(solution)/shard_map/ppermute | solution.py:47
  52.8 7.8 %collective-permute-start.18 = (bf16[2,32,2048]{2,1,0:T(8,128)(2,1)}, bf16[2,32,2048]{2,1,0:T(8,128)(2,1)S(1)}, u32[]{:S(2)}, u32[]{:S(2)}) collective-permute-start(bf16[2,32,2048]{2,1,0:T(8,128)(2,1)} %slice.128), channel_id=1, source_target_pairs={{0,2},{2,4},{4,6},{6,0},{1,3},{3,5},{5,7},{7,1},{8,10},{10,12},{12... | collective-permute-start | bytes 786440 | tf_op jit(solution)/shard_map/ppermute | solution.py:51
  54.6 7.6 %collective-permute-start.19 = (bf16[2,32,2048]{2,1,0:T(8,128)(2,1)}, bf16[2,32,2048]{2,1,0:T(8,128)(2,1)}, u32[]{:S(2)}, u32[]{:S(2)}) collective-permute-start(bf16[2,32,2048]{2,1,0:T(8,128)(2,1)} %slice.129), channel_id=1, source_target_pairs={{0,6},{2,0},{4,2},{6,4},{1,7},{3,1},{5,3},{7,5},{8,14},{10,8},{12,... | collective-permute-start | bytes 786440 | tf_op jit(solution)/shard_map/ppermute | solution.py:55
  67.0 19.0 %collective-permute-start.25 = (bf16[2,128,2048]{2,1,0:T(8,128)(2,1)S(1)}, bf16[2,128,2048]{2,1,0:T(8,128)(2,1)S(1)}, u32[]{:S(2)}, u32[]{:S(2)}) collective-permute-start(bf16[2,128,2048]{2,1,0:T(8,128)(2,1)S(1)} %shard_map.68), channel_id=1, source_target_pairs={{0,8},{1,33},{2,10},{3,35},{4,12},{5,37},{6,14},{7,39},{8,16},{9,4... | collective-permute-start | bytes 3145736 | tf_op jit(solution)/shard_map/ppermute | solution.py:43
  68.9 17.2 %collective-permute-start.26 = (bf16[2,128,2048]{2,1,0:T(8,128)(2,1)S(1)}, bf16[2,128,2048]{2,1,0:T(8,128)(2,1)}, u32[]{:S(2)}, u32[]{:S(2)}) collective-permute-start(bf16[2,128,2048]{2,1,0:T(8,128)(2,1)S(1)} %shard_map.69), channel_id=1, source_target_pairs={{0,24},{1,97},{2,26},{3,99},{4,28},{5,101},{6,30},{7,103},{8,0},{9... | collective-permute-start | bytes 3145736 | tf_op jit(solution)/shard_map/ppermute | solution.py:43
  75.7 18.6 %collective-permute-start.27 = (bf16[2,256,2048]{2,1,0:T(8,128)(2,1)S(1)}, bf16[2,256,2048]{2,1,0:T(8,128)(2,1)}, u32[]{:S(2)}, u32[]{:S(2)}) collective-permute-start(bf16[2,256,2048]{2,1,0:T(8,128)(2,1)S(1)} %shard_map.67.refs_1_.refs_0_), channel_id=1, source_target_pairs={{0,1},{1,0},{2,3},{3,2},{4,5},{5,4},{6,7},{7,6},{8,9},{9,8},{10,11... | collective-permute-start | bytes 6291464 | tf_op jit(solution)/shard_map/ppermute | solution.py:47
  75.8 18.5 %collective-permute-start.28 = (bf16[2,256,2048]{2,1,0:T(8,128)(2,1)}, bf16[2,256,2048]{2,1,0:T(8,128)(2,1)}, u32[]{:S(2)}, u32[]{:S(2)}) collective-permute-start(bf16[2,256,2048]{2,1,0:T(8,128)(2,1)} %collective-permute-done.14.refs_0_.refs_2_.refs_1_), channel_id=1, source_target_pairs={{0,1},{1,0},{2,3},{3,2},{4,5},{5,4},{6,7},{7,6},{8,9},{9,8},{10,11... | collective-permute-start | bytes 6291464 | tf_op jit(solution)/shard_map/ppermute | solution.py:47
  76.3 18.0 %collective-permute-start.29 = (bf16[2,256,2048]{2,1,0:T(8,128)(2,1)}, bf16[2,256,2048]{2,1,0:T(8,128)(2,1)}, u32[]{:S(2)}, u32[]{:S(2)}) collective-permute-start(bf16[2,256,2048]{2,1,0:T(8,128)(2,1)} %collective-permute-done.15.refs_0_.refs_3_.refs_2_), channel_id=1, source_target_pairs={{0,1},{1,0},{2,3},{3,2},{4,5},{5,4},{6,7},{7,6},{8,9},{9,8},{10,11... | collective-permute-start | bytes 6291464 | tf_op jit(solution)/shard_map/ppermute | solution.py:47
  86.0 8.4 %collective-permute-start.30 = (bf16[2,128,2048]{2,1,0:T(8,128)(2,1)S(1)}, bf16[2,128,2048]{2,1,0:T(8,128)(2,1)}, u32[]{:S(2)}, u32[]{:S(2)}) collective-permute-start(bf16[2,128,2048]{2,1,0:T(8,128)(2,1)S(1)} %collective-permute-done.25.refs_1_.refs_3_), channel_id=1, source_target_pairs={{0,1},{1,0},{2,3},{3,2},{4,5},{5,4},{6,7},{7,6},{8,9},{9,8},{10,11... | collective-permute-start | bytes 3145736 | tf_op jit(solution)/shard_map/ppermute | solution.py:47
  86.0 8.4 %collective-permute-start.31 = (bf16[2,128,2048]{2,1,0:T(8,128)(2,1)}, bf16[2,128,2048]{2,1,0:T(8,128)(2,1)}, u32[]{:S(2)}, u32[]{:S(2)}) collective-permute-start(bf16[2,128,2048]{2,1,0:T(8,128)(2,1)} %collective-permute-done.26.refs_2_.refs_4_), channel_id=1, source_target_pairs={{0,1},{1,0},{2,3},{3,2},{4,5},{5,4},{6,7},{7,6},{8,9},{9,8},{10,11... | collective-permute-start | bytes 3145736 | tf_op jit(solution)/shard_map/ppermute | solution.py:47
  122.9 8.4 %collective-permute-start.48 = (bf16[256,1024]{1,0:T(8,128)(2,1)S(1)}, bf16[256,1024]{1,0:T(8,128)(2,1)S(1)}, u32[]{:S(2)}, u32[]{:S(2)}) collective-permute-start(bf16[256,1024]{1,0:T(8,128)(2,1)S(1)} %get-tuple-element.158.mine), channel_id=1, source_target_pairs={{0,1},{1,0},{2,3},{3,2},{4,5},{5,4},{6,7},{7,6},{8,9},{9,8},{10,11... | collective-permute-start | bytes 1572872 | tf_op jit(solution)/shard_map/ppermute | solution.py:47
  128.0 9.5 %collective-permute-start.46 = (f16[64,2048]{1,0:T(8,128)(2,1)S(1)}, f16[64,2048]{1,0:T(8,128)(2,1)S(1)}, u32[]{:S(2)}, u32[]{:S(2)}) collective-permute-start(f16[64,2048]{1,0:T(8,128)(2,1)S(1)} %get-tuple-element.174), channel_id=1, source_target_pairs={{0,2},{2,4},{4,6},{6,0},{1,3},{3,5},{5,7},{7,1},{8,10},{10,12},{12... | collective-permute-start | bytes 786440 | tf_op jit(solution)/shard_map/ppermute | solution.py:51
  128.1 9.4 %collective-permute-start.47 = (f16[64,2048]{1,0:T(8,128)(2,1)S(1)}, f16[64,2048]{1,0:T(8,128)(2,1)S(1)}, u32[]{:S(2)}, u32[]{:S(2)}) collective-permute-start(f16[64,2048]{1,0:T(8,128)(2,1)S(1)} %get-tuple-element.173), channel_id=1, source_target_pairs={{0,6},{2,0},{4,2},{6,4},{1,7},{3,1},{5,3},{7,5},{8,14},{10,8},{12,... | collective-permute-start | bytes 786440 | tf_op jit(solution)/shard_map/ppermute | solution.py:55
  137.8 13.2 %collective-permute-start.51 = (f16[128,2048]{1,0:T(8,128)(2,1)S(1)}, f16[128,2048]{1,0:T(8,128)(2,1)S(1)}, u32[]{:S(2)}, u32[]{:S(2)}) collective-permute-start(f16[128,2048]{1,0:T(8,128)(2,1)S(1)} %pad_maximum_fusion.2), channel_id=1, source_target_pairs={{0,6},{2,0},{4,2},{6,4},{1,7},{3,1},{5,3},{7,5},{8,14},{10,8},{12,... | collective-permute-start | bytes 1572872 | tf_op jit(solution)/shard_map/ppermute | solution.py:55
  141.1 13.7 %collective-permute-start.50 = (f16[128,2048]{1,0:T(8,128)(2,1)S(1)}, f16[128,2048]{1,0:T(8,128)(2,1)S(1)}, u32[]{:S(2)}, u32[]{:S(2)}) collective-permute-start(f16[128,2048]{1,0:T(8,128)(2,1)S(1)} %pad_maximum_fusion.1), channel_id=1, source_target_pairs={{0,2},{2,4},{4,6},{6,0},{1,3},{3,5},{5,7},{7,1},{8,10},{10,12},{12... | collective-permute-start | bytes 1572872 | tf_op jit(solution)/shard_map/ppermute | solution.py:51
  (46 other events, 224.1 us)

commit v9 on v8

--- a/solution.py
+++ b/solution.py
@@ -473,20 +473,22 @@
 
     f16, f32 = jnp.float16, jnp.float32
     args = (parts, rows, cols, lse_i, plane)
-    m_far, bound = weights_of(3, 1, core, *args)
-    m_far_o = swap(m_far)
-    m_near, _ = weights_of(1, 2, after(core, m_far), *args)
-    (opposite,) = product_of(0, bound, m_far, m_far_o, blocks, others)
-    opposite = opposite.astype(f16)
-    got_q, got_p, to_down, to_up = settle(
-        up(opposite[:N]), down(opposite[N:]), *product_of(0, bound, m_near, swap(m_near), blocks, others)
-    )
-    below = up(jnp.concatenate([to_up[:N] + got_q.astype(f32), to_up[N:]]).astype(f16))
-    above = down(jnp.concatenate([to_down[:N], to_down[N:] + got_p.astype(f32)]).astype(f16))
-    m_own, _ = weights_of(0, 1, after(core, to_up), *args)
+    m_near, bound = weights_of(1, 3, core, *args)
+    m_out = jnp.concatenate([m_near[4 * N:], m_near[:N], m_near[3 * N:4 * N]])
+    m_mid = m_near[N:3 * N]
+    opposite, free = product_of(0, bound, m_out, swap(m_out), blocks, others)
+    opposite, free = opposite.astype(f16), free.astype(f16)
+    got_q, got_p, above_q, below_p, mid = settle(
+        up(opposite[:N]), down(opposite[N:]), down(free[:N]), up(free[N:]),
+        *product_of(0, bound, m_mid, swap(m_mid), blocks, others),
+    )
+    above_p = down((mid[:N] + got_p.astype(f32)).astype(f16))
+    below_q = up((mid[N:] + got_q.astype(f32)).astype(f16))
+    m_own, _ = weights_of(0, 1, after(core, mid), *args)
     (here,) = product_of(1, bound, m_own, swap(m_own), blocks, others)
-    grad = here + (below.astype(f32) + above.astype(f32)) * bound[0, 0]
-    grad_q, grad_p = grad[:N], grad[N:]
+    grow = bound[0, 0]
+    grad_q = here[:N] + (below_q.astype(f32) + above_q.astype(f32)) * grow
+    grad_p = here[N:] + (below_p.astype(f32) + above_p.astype(f32)) * grow
     return loss, grad_q, grad_p
 
 

time: 157 us -> 162 us (1.032)
  waiting for transfers between devices: 38.8 us -> 41.4 us
  starting transfers between devices: 55.4 us -> 57.5 us
    ppermute x6 -> x7, waiting for transfers between devices: 2.94 us -> 4.78 us  [down(): return lax.ppermute(value, 'x', DOWN)]
    ppermute x6 -> x7, starting transfers between devices: 2.43 us -> 4.21 us  [up(): return lax.ppermute(value, 'x', UP)]
    ppermute x6 -> x7, starting transfers between devices: 17 us -> 17.2 us  [down(): return lax.ppermute(value, 'x', DOWN)]
    ppermute x6 -> x7, waiting for transfers between devices: 9.37 us -> 9.36 us  [up(): return lax.ppermute(value, 'x', UP)]
  transfers between devices with their start and end apart: 52 -> 54, of which waited for: 20 -> 22; matrix products, arithmetic and copies ran while one was open for 7% -> 7% of each run, Pallas kernels for 21% -> 19%
where the time goes in v9:
time: 162 us; the launch traced here: 161 us
  starting transfers between devices  57.5 us (35%)
  waiting for transfers between devices  41.4 us (26%)
  Pallas kernels  33.7 us (21%)
  local copies, waits for them, and re-layouts  16.7 us (10%)
  other arithmetic  9.11 us (6%)
  between operations  2.44 us (2%)
    ppermute x20, starting transfers between devices, along(): return lax.ppermute(value, GRID, moves)  29.8 us
    ppermute x7, starting transfers between devices, down(): return lax.ppermute(value, 'x', DOWN)  17.2 us
    ppermute x20, waiting for transfers between devices, along(): return lax.ppermute(value, GRID, moves)  16.2 us
    pallas_call x3, Pallas kernels, product_of(): pl.pallas_call(functools.partial(product_kernel, scaled), out_shape=[jax....  14.3 us
    unnamed x41, local copies, waits for them, and re-layouts  10.9 us
    pallas_call x2, Pallas kernels, scores_of(): pl.pallas_call(functools.partial(scores_kernel, plan), out_shape=[jax.Sha...  9.92 us
    ppermute x7, waiting for transfers between devices, up(): return lax.ppermute(value, 'x', UP)  9.36 us
    ppermute x2, waiting for transfers between devices, far(): return lax.ppermute(value, 'x', FAR)  6.18 us
  transfers between devices with their start and end apart: 54, of which 22 were waited for; matrix products, arithmetic and copies ran while one was open for 7% of the time, Pallas kernels for 19%

profile of v9, /device:TPU:0, one launch (start us, length us, event | category | flops | bytes accessed | tf_op | source)
XLA Modules:
  0.0 160.8 jit_solution(1016009834795879111)
XLA Ops:
  12.5 3.2 %collective-permute-done.5 = s32[2,64]{1,0:T(2,128)S(1)} collective-permute-done((s32[2,64]{1,0:T(2,128)S(1)}, s32[2,64]{1,0:T(2,128)S(1)}, u32[]{:S(2)}, u32[]{:S(2)}) %collective-permute-start.5) | collective-permute-done | bytes 544 | tf_op jit(solution)/shard_map/ppermute | solution.py:59
  17.1 2.8 %collective-permute-start.7 = (bf16[2,32,2048]{2,1,0:T(8,128)(2,1)S(1)}, bf16[2,32,2048]{2,1,0:T(8,128)(2,1)S(1)}, u32[]{:S(2)}, u32[]{:S(2)}) collective-permute-start(bf16[2,32,2048]{2,1,0:T(8,128)(2,1)S(1)} %slice.103), channel_id=1, source_target_pairs={{0,96},{1,25},{2,98},{3,27},{4,100},{5,29},{6,102},{7,31},{8,104},... | collective-permute-start | bytes 786440 | tf_op jit(solution)/shard_map/ppermute | solution.py:43
  19.9 3.2 %collective-permute-start.9 = (s32[4,2,64]{2,1,0:T(2,128)S(1)}, s32[4,2,64]{2,1,0:T(2,128)S(1)}, u32[]{:S(2)}, u32[]{:S(2)}) collective-permute-start(s32[4,2,64]{2,1,0:T(2,128)S(1)} %pad_add_fusion.2), channel_id=1, source_target_pairs={{0,96},{1,25},{2,98},{3,27},{4,100},{5,29},{6,102},{7,31},{8,104},... | collective-permute-start | bytes 6152 | tf_op jit(solution)/shard_map/ppermute | solution.py:43
  24.7 3.5 %collective-permute-done.10 = s32[4,2,64]{2,1,0:T(2,128)S(1)} collective-permute-done((s32[4,2,64]{2,1,0:T(2,128)S(1)}, s32[4,2,64]{2,1,0:T(2,128)S(1)}, u32[]{:S(2)}, u32[]{:S(2)}) %collective-permute-start.10) | collective-permute-done | bytes 2080 | tf_op jit(solution)/shard_map/ppermute | solution.py:43
  38.6 3.1 %collective-permute-start.15 = (bf16[2,256,2048]{2,1,0:T(8,128)(2,1)S(1)}, bf16[2,256,2048]{2,1,0:T(8,128)(2,1)}, u32[]{:S(2)}, u32[]{:S(2)}) collective-permute-start(bf16[2,256,2048]{2,1,0:T(8,128)(2,1)S(1)} %shard_map.67.refs_1_.refs_0_), channel_id=1, source_target_pairs={{0,24},{1,97},{2,26},{3,99},{4,28},{5,101},{6,30},{7,103},{8,0},{9... | collective-permute-start | bytes 6291464 | tf_op jit(solution)/shard_map/ppermute | solution.py:43
  42.0 2.9 %collective-permute-start.17 = (bf16[2,64,2048]{2,1,0:T(8,128)(2,1)S(1)}, bf16[2,64,2048]{2,1,0:T(8,128)(2,1)}, u32[]{:S(2)}, u32[]{:S(2)}) collective-permute-start(bf16[2,64,2048]{2,1,0:T(8,128)(2,1)S(1)} %pad_maximum_fusion.refs_0_), channel_id=1, source_target_pairs={{0,6},{2,0},{4,2},{6,4},{1,7},{3,1},{5,3},{7,5},{8,14},{10,8},{12,... | collective-permute-start | bytes 1572872 | tf_op jit(solution)/shard_map/ppermute | solution.py:55
  49.1 3.0 %collective-permute-done.16.refs_1_ = bf16[2,64,2048]{2,1,0:T(8,128)(2,1)S(1)} collective-permute-done((bf16[2,64,2048]{2,1,0:T(8,128)(2,1)S(1)}, bf16[2,64,2048]{2,1,0:T(8,128)(2,1)S(1)}, u32[]{:S(2)}, u32[]{:S(2)}) %collective-permute-start.16) | collective-permute-done | bytes 524320 | tf_op jit(solution)/shard_map/ppermute | solution.py:51
  54.6 3.2 %collective-permute-start.19 = (bf16[2,32,2048]{2,1,0:T(8,128)(2,1)}, bf16[2,32,2048]{2,1,0:T(8,128)(2,1)}, u32[]{:S(2)}, u32[]{:S(2)}) collective-permute-start(bf16[2,32,2048]{2,1,0:T(8,128)(2,1)} %slice.143), channel_id=1, source_target_pairs={{0,6},{2,0},{4,2},{6,4},{1,7},{3,1},{5,3},{7,5},{8,14},{10,8},{12,... | collective-permute-start | bytes 786440 | tf_op jit(solution)/shard_map/ppermute | solution.py:55
  68.8 2.8 %collective-permute-start.26 = (bf16[2,128,2048]{2,1,0:T(8,128)(2,1)S(1)}, bf16[2,128,2048]{2,1,0:T(8,128)(2,1)}, u32[]{:S(2)}, u32[]{:S(2)}) collective-permute-start(bf16[2,128,2048]{2,1,0:T(8,128)(2,1)S(1)} %shard_map.69), channel_id=1, source_target_pairs={{0,24},{1,97},{2,26},{3,99},{4,28},{5,101},{6,30},{7,103},{8,0},{9... | collective-permute-start | bytes 3145736 | tf_op jit(solution)/shard_map/ppermute | solution.py:43
  76.4 7.2 %shard_map.71 = (f32[512,256]{1,0:T(8,128)S(1)}, f32[512,256]{1,0:T(8,128)S(1)}, f32[512,256]{1,0:T(8,128)S(1)}) custom-call(bf16[2,512,2048]{2,1,0:T(8,128)(2,1)S(1)} %shard_map.70.refs_0_, bf16[2,256,2048]{2,1,0:T(8,128)(2,1)S(1)} %shard_map.67.refs_1_.refs_0_, bf16[2,256,2048]{2,1,0:T(8,128)(2,1)} %collective-permute-done.14.refs_0_.refs_2_.refs_1_, ...), custom_call_target="tpu_custom_call" | custom-call | tf_op jit(solution)/shard_map/pallas_call | solution.py:182
  88.8 2.8 %shard_map.72 = (f32[512,128]{1,0:T(8,128)S(1)}, f32[512,128]{1,0:T(8,128)S(1)}) custom-call(bf16[2,512,2048]{2,1,0:T(8,128)(2,1)S(1)} %copy-done.1, bf16[2,128,2048]{2,1,0:T(8,128)(2,1)S(1)} %collective-permute-done.25.refs_1_.refs_3_, bf16[2,128,2048]{2,1,0:T(8,128)(2,1)} %collective-permute-done.26.refs_2_.refs_4_), custom_call_target="tpu_custom_call" | custom-call | tf_op jit(solution)/shard_map/pallas_call | solution.py:182
  94.8 2.9 %collective-permute-start.33 = (f32[16,128]{1,0:T(8,128)S(1)}, f32[16,128]{1,0:T(8,128)S(1)}, u32[]{:S(2)}, u32[]{:S(2)}) collective-permute-start(f32[16,128]{1,0:T(8,128)S(1)} %shard_map.73.refs_0_), channel_id=1, source_target_pairs={{0,6},{2,0},{4,2},{6,4},{1,7},{3,1},{5,3},{7,5},{8,14},{10,8},{12,... | collective-permute-start | bytes 24584 | tf_op jit(solution)/shard_map/ppermute | solution.py:55
  99.8 3.0 %collective-permute-done.34.refs_3_ = f32[16,128]{1,0:T(8,128)S(1)} collective-permute-done((f32[16,128]{1,0:T(8,128)S(1)}, f32[16,128]{1,0:T(8,128)S(1)}, u32[]{:S(2)}, u32[]{:S(2)}) %collective-permute-start.34) | collective-permute-done | bytes 8224 | tf_op jit(solution)/shard_map/ppermute | solution.py:59
  104.2 3.2 %collective-permute-start.40 = (f32[8,128]{1,0:T(8,128)S(1)}, f32[8,128]{1,0:T(8,128)S(1)}, u32[]{:S(2)}, u32[]{:S(2)}) collective-permute-start(f32[8,128]{1,0:T(8,128)S(1)} %get-tuple-element.143), channel_id=1, source_target_pairs={{0,96},{1,25},{2,98},{3,27},{4,100},{5,29},{6,102},{7,31},{8,104},... | collective-permute-start | bytes 12296 | tf_op jit(solution)/shard_map/ppermute | solution.py:43
  109.0 3.5 %collective-permute-done.41 = f32[8,128]{1,0:T(8,128)S(1)} collective-permute-done((f32[8,128]{1,0:T(8,128)S(1)}, f32[8,128]{1,0:T(8,128)S(1)}, u32[]{:S(2)}, u32[]{:S(2)}) %collective-permute-start.41) | collective-permute-done | bytes 4128 | tf_op jit(solution)/shard_map/ppermute | solution.py:43
  112.5 3.2 %collective-permute-start.43 = (f32[32,128]{1,0:T(8,128)S(1)}, f32[32,128]{1,0:T(8,128)S(1)}, u32[]{:S(2)}, u32[]{:S(2)}) collective-permute-start(f32[32,128]{1,0:T(8,128)S(1)} %constant_dynamic-update-slice_fusion.4.refs_8_), channel_id=1, source_target_pairs={{0,24},{1,97},{2,26},{3,99},{4,28},{5,101},{6,30},{7,103},{8,0},{9... | collective-permute-start | bytes 49160 | tf_op jit(solution)/shard_map/ppermute | solution.py:43
  117.5 3.5 %collective-permute-done.44.refs_11_ = f32[32,128]{1,0:T(8,128)S(1)} collective-permute-done((f32[32,128]{1,0:T(8,128)S(1)}, f32[32,128]{1,0:T(8,128)S(1)}, u32[]{:S(2)}, u32[]{:S(2)}) %collective-permute-start.44) | collective-permute-done | bytes 16416 | tf_op jit(solution)/shard_map/ppermute | solution.py:43
  124.3 5.4 %shard_map.76 = (f32[128,2048]{1,0:T(8,128)S(1)}, f32[128,2048]{1,0:T(8,128)S(1)}) custom-call(f32[8,128]{1,0:T(8,128)S(1)} %get-tuple-element.144.bound, bf16[256,1024]{1,0:T(8,128)(2,1)S(1)} %pad_maximum_fusion.1.mine, bf16[256,1024]{1,0:T(8,128)(2,1)S(1)} %collective-permute-done.45.theirs, bf16[2,256,2048]{2,1,0:T(8,128)(2,1)S(1)} %shard_map.67.refs_1_.refs_0_, ...), custom_call_target="tpu_custom_call" | custom-call | tf_op jit(solution)/shard_map/pallas_call | solution.py:387
  129.9 3.2 %collective-permute-start.47 = (f16[64,2048]{1,0:T(8,128)(2,1)S(1)}, f16[64,2048]{1,0:T(8,128)(2,1)S(1)}, u32[]{:S(2)}, u32[]{:S(2)}) collective-permute-start(f16[64,2048]{1,0:T(8,128)(2,1)S(1)} %get-tuple-element.175), channel_id=1, source_target_pairs={{0,6},{2,0},{4,2},{6,4},{1,7},{3,1},{5,3},{7,5},{8,14},{10,8},{12,... | collective-permute-start | bytes 786440 | tf_op jit(solution)/shard_map/ppermute | solution.py:55
  135.4 4.4 %shard_map.77 = f32[128,2048]{1,0:T(8,128)S(1)} custom-call(f32[8,128]{1,0:T(8,128)S(1)} %get-tuple-element.144.bound, bf16[128,1024]{1,0:T(8,128)(2,1)S(1)} %get-tuple-element.169.mine, bf16[128,1024]{1,0:T(8,128)(2,1)S(1)} %collective-permute-done.50.theirs, bf16[2,256,2048]{2,1,0:T(8,128)(2,1)S(1)} %shard_map.67.refs_1_.refs_0_, ...), custom_call_target="tpu_custom_call" | custom-call | tf_op jit(solution)/shard_map/pallas_call | solution.py:387
  140.3 4.1 %collective-permute-done.48 = f16[64,2048]{1,0:T(8,128)(2,1)S(1)} collective-permute-done((f16[64,2048]{1,0:T(8,128)(2,1)S(1)}, f16[64,2048]{1,0:T(8,128)(2,1)S(1)}, u32[]{:S(2)}, u32[]{:S(2)}) %collective-permute-start.48) | collective-permute-done | bytes 262176 | tf_op jit(solution)/shard_map/ppermute | solution.py:55
  146.2 3.0 %collective-permute-start.53 = (f16[64,2048]{1,0:T(8,128)(2,1)S(1)}, f16[64,2048]{1,0:T(8,128)(2,1)S(1)}, u32[]{:S(2)}, u32[]{:S(2)}) collective-permute-start(f16[64,2048]{1,0:T(8,128)(2,1)S(1)} %get-tuple-element.167), channel_id=1, source_target_pairs={{0,6},{2,0},{4,2},{6,4},{1,7},{3,1},{5,3},{7,5},{8,14},{10,8},{12,... | collective-permute-start | bytes 786440 | tf_op jit(solution)/shard_map/ppermute | solution.py:55
  150.4 4.4 %shard_map.79 = f32[128,2048]{1,0:T(8,128)S(1)} custom-call(f32[8,128]{1,0:T(8,128)S(1)} %get-tuple-element.144.bound, bf16[128,1024]{1,0:T(8,128)(2,1)S(1)} %get-tuple-element.160.mine, bf16[128,1024]{1,0:T(8,128)(2,1)S(1)} %collective-permute-done.51.theirs, bf16[2,256,2048]{2,1,0:T(8,128)(2,1)S(1)} %shard_map.67.refs_1_.refs_0_, ...), custom_call_target="tpu_custom_call" | custom-call | tf_op jit(solution)/shard_map/pallas_call | solution.py:387
  155.5 3.4 %collective-permute-done.52 = f16[64,2048]{1,0:T(8,128)(2,1)S(1)} collective-permute-done((f16[64,2048]{1,0:T(8,128)(2,1)S(1)}, f16[64,2048]{1,0:T(8,128)(2,1)S(1)}, u32[]{:S(2)}, u32[]{:S(2)}) %collective-permute-start.52) | collective-permute-done | bytes 262176 | tf_op jit(solution)/shard_map/ppermute | solution.py:51
  (203 shorter events, 73.3 us)
Async XLA Ops:
  3.4 12.3 %collective-permute-start.1 = (bf16[2,64,2048]{2,1,0:T(8,128)(2,1)S(1)}, bf16[2,64,2048]{2,1,0:T(8,128)(2,1)S(1)}, u32[]{:S(2)}, u32[]{:S(2)}) collective-permute-start(bf16[2,64,2048]{2,1,0:T(8,128)(2,1)S(1)} %pad_maximum_fusion.refs_0_), channel_id=1, source_target_pairs={{0,32},{1,9},{2,34},{3,11},{4,36},{5,13},{6,38},{7,15},{8,40},{9,1... | collective-permute-start | bytes 1572872 | tf_op jit(solution)/shard_map/ppermute | solution.py:43
  5.1 10.6 %collective-permute-start.2 = (bf16[2,64,2048]{2,1,0:T(8,128)(2,1)S(1)}, bf16[2,64,2048]{2,1,0:T(8,128)(2,1)S(1)}, u32[]{:S(2)}, u32[]{:S(2)}) collective-permute-start(bf16[2,64,2048]{2,1,0:T(8,128)(2,1)S(1)} %pad_maximum_fusion.refs_0_), channel_id=1, source_target_pairs={{0,96},{1,25},{2,98},{3,27},{4,100},{5,29},{6,102},{7,31},{8,104},... | collective-permute-start | bytes 1572872 | tf_op jit(solution)/shard_map/ppermute | solution.py:43
  15.7 12.5 %collective-permute-start.6 = (bf16[2,32,2048]{2,1,0:T(8,128)(2,1)S(1)}, bf16[2,32,2048]{2,1,0:T(8,128)(2,1)S(1)}, u32[]{:S(2)}, u32[]{:S(2)}) collective-permute-start(bf16[2,32,2048]{2,1,0:T(8,128)(2,1)S(1)} %slice.102), channel_id=1, source_target_pairs={{0,32},{1,9},{2,34},{3,11},{4,36},{5,13},{6,38},{7,15},{8,40},{9,1... | collective-permute-start | bytes 786440 | tf_op jit(solution)/shard_map/ppermute | solution.py:43
  17.1 11.1 %collective-permute-start.7 = (bf16[2,32,2048]{2,1,0:T(8,128)(2,1)S(1)}, bf16[2,32,2048]{2,1,0:T(8,128)(2,1)S(1)}, u32[]{:S(2)}, u32[]{:S(2)}) collective-permute-start(bf16[2,32,2048]{2,1,0:T(8,128)(2,1)S(1)} %slice.103), channel_id=1, source_target_pairs={{0,96},{1,25},{2,98},{3,27},{4,100},{5,29},{6,102},{7,31},{8,104},... | collective-permute-start | bytes 786440 | tf_op jit(solution)/shard_map/ppermute | solution.py:43
  28.9 8.6 %collective-permute-start.11 = (s32[4,4,2,64]{3,2,1,0:T(2,128)S(1)}, s32[4,4,2,64]{3,2,1,0:T(2,128)S(1)}, u32[]{:S(2)}, u32[]{:S(2)}) collective-permute-start(s32[4,4,2,64]{3,2,1,0:T(2,128)S(1)} %pad_add_fusion.1), channel_id=1, source_target_pairs={{0,8},{1,33},{2,10},{3,35},{4,12},{5,37},{6,14},{7,39},{8,16},{9,4... | collective-permute-start | bytes 24584 | tf_op jit(solution)/shard_map/ppermute | solution.py:43
  38.4 27.4 %collective-permute-start.14 = (bf16[2,256,2048]{2,1,0:T(8,128)(2,1)S(1)}, bf16[2,256,2048]{2,1,0:T(8,128)(2,1)}, u32[]{:S(2)}, u32[]{:S(2)}) collective-permute-start(bf16[2,256,2048]{2,1,0:T(8,128)(2,1)S(1)} %shard_map.67.refs_1_.refs_0_), channel_id=1, source_target_pairs={{0,8},{1,33},{2,10},{3,35},{4,12},{5,37},{6,14},{7,39},{8,16},{9,4... | collective-permute-start | bytes 6291464 | tf_op jit(solution)/shard_map/ppermute | solution.py:43
  38.6 27.2 %collective-permute-start.15 = (bf16[2,256,2048]{2,1,0:T(8,128)(2,1)S(1)}, bf16[2,256,2048]{2,1,0:T(8,128)(2,1)}, u32[]{:S(2)}, u32[]{:S(2)}) collective-permute-start(bf16[2,256,2048]{2,1,0:T(8,128)(2,1)S(1)} %shard_map.67.refs_1_.refs_0_), channel_id=1, source_target_pairs={{0,24},{1,97},{2,26},{3,99},{4,28},{5,101},{6,30},{7,103},{8,0},{9... | collective-permute-start | bytes 6291464 | tf_op jit(solution)/shard_map/ppermute | solution.py:43
  41.7 10.4 %collective-permute-start.16 = (bf16[2,64,2048]{2,1,0:T(8,128)(2,1)S(1)}, bf16[2,64,2048]{2,1,0:T(8,128)(2,1)S(1)}, u32[]{:S(2)}, u32[]{:S(2)}) collective-permute-start(bf16[2,64,2048]{2,1,0:T(8,128)(2,1)S(1)} %pad_maximum_fusion.refs_0_), channel_id=1, source_target_pairs={{0,2},{2,4},{4,6},{6,0},{1,3},{3,5},{5,7},{7,1},{8,10},{10,12},{12... | collective-permute-start | bytes 1572872 | tf_op jit(solution)/shard_map/ppermute | solution.py:51
  42.0 10.9 %collective-permute-start.17 = (bf16[2,64,2048]{2,1,0:T(8,128)(2,1)S(1)}, bf16[2,64,2048]{2,1,0:T(8,128)(2,1)}, u32[]{:S(2)}, u32[]{:S(2)}) collective-permute-start(bf16[2,64,2048]{2,1,0:T(8,128)(2,1)S(1)} %pad_maximum_fusion.refs_0_), channel_id=1, source_target_pairs={{0,6},{2,0},{4,2},{6,4},{1,7},{3,1},{5,3},{7,5},{8,14},{10,8},{12,... | collective-permute-start | bytes 1572872 | tf_op jit(solution)/shard_map/ppermute | solution.py:55
  44.9 16.8 %collective-permute-start.20 = (bf16[2,64,2048]{2,1,0:T(8,128)(2,1)S(1)}, bf16[2,64,2048]{2,1,0:T(8,128)(2,1)}, u32[]{:S(2)}, u32[]{:S(2)}) collective-permute-start(bf16[2,64,2048]{2,1,0:T(8,128)(2,1)S(1)} %pad_maximum_fusion.refs_0_), channel_id=1, source_target_pairs={{0,1},{1,0},{2,3},{3,2},{4,5},{5,4},{6,7},{7,6},{8,9},{9,8},{10,11... | collective-permute-start | bytes 1572872 | tf_op jit(solution)/shard_map/ppermute | solution.py:47
  67.0 19.0 %collective-permute-start.25 = (bf16[2,128,2048]{2,1,0:T(8,128)(2,1)S(1)}, bf16[2,128,2048]{2,1,0:T(8,128)(2,1)S(1)}, u32[]{:S(2)}, u32[]{:S(2)}) collective-permute-start(bf16[2,128,2048]{2,1,0:T(8,128)(2,1)S(1)} %shard_map.68), channel_id=1, source_target_pairs={{0,8},{1,33},{2,10},{3,35},{4,12},{5,37},{6,14},{7,39},{8,16},{9,4... | collective-permute-start | bytes 3145736 | tf_op jit(solution)/shard_map/ppermute | solution.py:43
  68.8 17.1 %collective-permute-start.26 = (bf16[2,128,2048]{2,1,0:T(8,128)(2,1)S(1)}, bf16[2,128,2048]{2,1,0:T(8,128)(2,1)}, u32[]{:S(2)}, u32[]{:S(2)}) collective-permute-start(bf16[2,128,2048]{2,1,0:T(8,128)(2,1)S(1)} %shard_map.69), channel_id=1, source_target_pairs={{0,24},{1,97},{2,26},{3,99},{4,28},{5,101},{6,30},{7,103},{8,0},{9... | collective-permute-start | bytes 3145736 | tf_op jit(solution)/shard_map/ppermute | solution.py:43
  75.7 18.6 %collective-permute-start.27 = (bf16[2,256,2048]{2,1,0:T(8,128)(2,1)S(1)}, bf16[2,256,2048]{2,1,0:T(8,128)(2,1)}, u32[]{:S(2)}, u32[]{:S(2)}) collective-permute-start(bf16[2,256,2048]{2,1,0:T(8,128)(2,1)S(1)} %shard_map.67.refs_1_.refs_0_), channel_id=1, source_target_pairs={{0,1},{1,0},{2,3},{3,2},{4,5},{5,4},{6,7},{7,6},{8,9},{9,8},{10,11... | collective-permute-start | bytes 6291464 | tf_op jit(solution)/shard_map/ppermute | solution.py:47
  75.8 18.5 %collective-permute-start.28 = (bf16[2,256,2048]{2,1,0:T(8,128)(2,1)}, bf16[2,256,2048]{2,1,0:T(8,128)(2,1)}, u32[]{:S(2)}, u32[]{:S(2)}) collective-permute-start(bf16[2,256,2048]{2,1,0:T(8,128)(2,1)} %collective-permute-done.14.refs_0_.refs_2_.refs_1_), channel_id=1, source_target_pairs={{0,1},{1,0},{2,3},{3,2},{4,5},{5,4},{6,7},{7,6},{8,9},{9,8},{10,11... | collective-permute-start | bytes 6291464 | tf_op jit(solution)/shard_map/ppermute | solution.py:47
  76.3 18.0 %collective-permute-start.29 = (bf16[2,256,2048]{2,1,0:T(8,128)(2,1)}, bf16[2,256,2048]{2,1,0:T(8,128)(2,1)}, u32[]{:S(2)}, u32[]{:S(2)}) collective-permute-start(bf16[2,256,2048]{2,1,0:T(8,128)(2,1)} %collective-permute-done.15.refs_0_.refs_3_.refs_2_), channel_id=1, source_target_pairs={{0,1},{1,0},{2,3},{3,2},{4,5},{5,4},{6,7},{7,6},{8,9},{9,8},{10,11... | collective-permute-start | bytes 6291464 | tf_op jit(solution)/shard_map/ppermute | solution.py:47
  86.0 8.4 %collective-permute-start.30 = (bf16[2,128,2048]{2,1,0:T(8,128)(2,1)S(1)}, bf16[2,128,2048]{2,1,0:T(8,128)(2,1)}, u32[]{:S(2)}, u32[]{:S(2)}) collective-permute-start(bf16[2,128,2048]{2,1,0:T(8,128)(2,1)S(1)} %collective-permute-done.25.refs_1_.refs_3_), channel_id=1, source_target_pairs={{0,1},{1,0},{2,3},{3,2},{4,5},{5,4},{6,7},{7,6},{8,9},{9,8},{10,11... | collective-permute-start | bytes 3145736 | tf_op jit(solution)/shard_map/ppermute | solution.py:47
  86.0 8.4 %collective-permute-start.31 = (bf16[2,128,2048]{2,1,0:T(8,128)(2,1)}, bf16[2,128,2048]{2,1,0:T(8,128)(2,1)}, u32[]{:S(2)}, u32[]{:S(2)}) collective-permute-start(bf16[2,128,2048]{2,1,0:T(8,128)(2,1)} %collective-permute-done.26.refs_2_.refs_4_), channel_id=1, source_target_pairs={{0,1},{1,0},{2,3},{3,2},{4,5},{5,4},{6,7},{7,6},{8,9},{9,8},{10,11... | collective-permute-start | bytes 3145736 | tf_op jit(solution)/shard_map/ppermute | solution.py:47
  122.4 13.0 %collective-permute-start.50 = (bf16[128,1024]{1,0:T(8,128)(2,1)S(1)}, bf16[128,1024]{1,0:T(8,128)(2,1)S(1)}, u32[]{:S(2)}, u32[]{:S(2)}) collective-permute-start(bf16[128,1024]{1,0:T(8,128)(2,1)S(1)} %get-tuple-element.169.mine), channel_id=1, source_target_pairs={{0,1},{1,0},{2,3},{3,2},{4,5},{5,4},{6,7},{7,6},{8,9},{9,8},{10,11... | collective-permute-start | bytes 786440 | tf_op jit(solution)/shard_map/ppermute | solution.py:47
  129.8 10.4 %collective-permute-start.46 = (f16[64,2048]{1,0:T(8,128)(2,1)S(1)}, f16[64,2048]{1,0:T(8,128)(2,1)S(1)}, u32[]{:S(2)}, u32[]{:S(2)}) collective-permute-start(f16[64,2048]{1,0:T(8,128)(2,1)S(1)} %get-tuple-element.176), channel_id=1, source_target_pairs={{0,2},{2,4},{4,6},{6,0},{1,3},{3,5},{5,7},{7,1},{8,10},{10,12},{12... | collective-permute-start | bytes 786440 | tf_op jit(solution)/shard_map/ppermute | solution.py:51
  129.9 10.4 %collective-permute-start.47 = (f16[64,2048]{1,0:T(8,128)(2,1)S(1)}, f16[64,2048]{1,0:T(8,128)(2,1)S(1)}, u32[]{:S(2)}, u32[]{:S(2)}) collective-permute-start(f16[64,2048]{1,0:T(8,128)(2,1)S(1)} %get-tuple-element.175), channel_id=1, source_target_pairs={{0,6},{2,0},{4,2},{6,4},{1,7},{3,1},{5,3},{7,5},{8,14},{10,8},{12,... | collective-permute-start | bytes 786440 | tf_op jit(solution)/shard_map/ppermute | solution.py:55
  133.3 11.0 %collective-permute-start.48 = (f16[64,2048]{1,0:T(8,128)(2,1)S(1)}, f16[64,2048]{1,0:T(8,128)(2,1)S(1)}, u32[]{:S(2)}, u32[]{:S(2)}) collective-permute-start(f16[64,2048]{1,0:T(8,128)(2,1)S(1)} %get-tuple-element.174), channel_id=1, source_target_pairs={{0,6},{2,0},{4,2},{6,4},{1,7},{3,1},{5,3},{7,5},{8,14},{10,8},{12,... | collective-permute-start | bytes 786440 | tf_op jit(solution)/shard_map/ppermute | solution.py:55
  133.6 11.5 %collective-permute-start.49 = (f16[64,2048]{1,0:T(8,128)(2,1)S(1)}, f16[64,2048]{1,0:T(8,128)(2,1)S(1)}, u32[]{:S(2)}, u32[]{:S(2)}) collective-permute-start(f16[64,2048]{1,0:T(8,128)(2,1)S(1)} %get-tuple-element.173), channel_id=1, source_target_pairs={{0,2},{2,4},{4,6},{6,0},{1,3},{3,5},{5,7},{7,1},{8,10},{10,12},{12... | collective-permute-start | bytes 786440 | tf_op jit(solution)/shard_map/ppermute | solution.py:51
  146.2 9.3 %collective-permute-start.53 = (f16[64,2048]{1,0:T(8,128)(2,1)S(1)}, f16[64,2048]{1,0:T(8,128)(2,1)S(1)}, u32[]{:S(2)}, u32[]{:S(2)}) collective-permute-start(f16[64,2048]{1,0:T(8,128)(2,1)S(1)} %get-tuple-element.167), channel_id=1, source_target_pairs={{0,6},{2,0},{4,2},{6,4},{1,7},{3,1},{5,3},{7,5},{8,14},{10,8},{12,... | collective-permute-start | bytes 786440 | tf_op jit(solution)/shard_map/ppermute | solution.py:55
  149.3 9.6 %collective-permute-start.52 = (f16[64,2048]{1,0:T(8,128)(2,1)S(1)}, f16[64,2048]{1,0:T(8,128)(2,1)S(1)}, u32[]{:S(2)}, u32[]{:S(2)}) collective-permute-start(f16[64,2048]{1,0:T(8,128)(2,1)S(1)} %get-tuple-element.168), channel_id=1, source_target_pairs={{0,2},{2,4},{4,6},{6,0},{1,3},{3,5},{5,7},{7,1},{8,10},{10,12},{12... | collective-permute-start | bytes 786440 | tf_op jit(solution)/shard_map/ppermute | solution.py:51
  (48 other events, 242.2 us)
